TPU v7x, 32 devices: a whole 2x2x4 slice. The times are simulated.
32 devices in a mesh: section: 2 (over core), dp: 4 (over z), tensor: 4 (over y, x).
Axes of the slice: x: 2, y: 2, z: 4, core: 2. Of those that a mesh axis runs over, the one named last changes fastest.
Arguments:
- inputs: bfloat16 [2, 4096, 1024], P(None, ('dp', 'tensor')), may hold values from -6 to 6
- lengths: int32 [2, 4, 2], P(None, 'dp'), may hold values from 0 to 1024, as said below
- norm_gain: float32 [2, 2, 1024], P('section'), may hold values from 0.5 to 1.5
- w_query: bfloat16 [2, 1024, 1024], P('section', 'dp', 'tensor'), may hold values from -0.1875 to 0.1875
- w_key: bfloat16 [2, 1024, 1024], P('section', 'dp', 'tensor'), may hold values from -0.1875 to 0.1875
- w_value: bfloat16 [2, 1024, 2048], P('section', 'dp', 'tensor'), may hold values from -0.1875 to 0.1875
- w_gate: bfloat16 [2, 1024, 2048], P('section', 'dp', 'tensor'), may hold values from -0.1875 to 0.1875
- w_decay: bfloat16 [2, 1024, 16], P('section', 'dp', 'tensor'), may hold values from -0.1875 to 0.1875
- conv_weight: float32 [2, 4, 8, 512], P('section'), may hold values from -3 to 3
- head_rate: float32 [2, 8], P('section'), may hold values from -1 to 1.5
- head_bias: float32 [2, 8], P('section'), may hold values from -6 to -2
- out_gain: float32 [2, 256], P('section'), may hold values from 0.5 to 1.5
- w_out: bfloat16 [2, 2048, 1024], P('section', 'tensor', 'dp'), may hold values from -0.25 to 0.25
- w_updown: bfloat16 [2, 1024, 2, 2816], P('section', 'dp', None, 'tensor'), may hold values from -0.1875 to 0.1875
- w_down: bfloat16 [2, 2816, 1024], P('section', 'tensor', 'dp'), may hold values from -0.109375 to 0.109375
- cotangent: bfloat16 [2, 4096, 1024], P(None, ('dp', 'tensor')), may hold values from -6 to 6
Outputs:
- output: bfloat16 [2, 4096, 1024], P('section', ('dp', 'tensor'))
- input_grad: bfloat16 [2, 4096, 1024], P('section', ('dp', 'tensor'))
- grad_norm_gain: float32 [2, 2, 1024], P('section')
- grad_query: float32 [2, 1024, 1024], P('section', 'dp', 'tensor')
- grad_key: float32 [2, 1024, 1024], P('section', 'dp', 'tensor')
- grad_value: float32 [2, 1024, 2048], P('section', 'dp', 'tensor')
- grad_gate: float32 [2, 1024, 2048], P('section', 'dp', 'tensor')
- grad_decay: float32 [2, 1024, 16], P('section', 'dp', 'tensor')
- grad_conv: float32 [2, 4, 8, 512], P('section')
- grad_rate: float32 [2, 8], P('section')
- grad_bias: float32 [2, 8], P('section')
- grad_out_gain: float32 [2, 256], P('section')
- grad_out: float32 [2, 2048, 1024], P('section', 'tensor', 'dp')
- grad_updown: float32 [2, 1024, 2, 2816], P('section', 'dp', None, 'tensor')
- grad_down: float32 [2, 2816, 1024], P('section', 'tensor', 'dp')
Inputs may be any that keep to these rules, and one draw needn't show every extreme that they name: Each buffer's sequences lie back to back from its first token in slot order; lengths are multiples of 64 and a buffer's sum is at most 1024; the first slot holds 512 tokens or more; a zero length is an empty slot; for each dp index one micro-batch's buffer is one sequence of 1024 tokens.
All inputs are finite; a program needn't handle non-finite values.
Results may differ from a plain program's by a relative error of at most 0.025.
Values may be sent and summed in bfloat16 or wider, within the bound.
No kernel may reach another device: no remote copies, remote signals or barrier semaphores. Data moves between devices by JAX's collectives and lax.ppermute only.
A program may use at most 448 MiB of HBM per device.

v0:
```python
import jax
import jax.numpy as jnp
from jax import lax
from jax.sharding import PartitionSpec as P

KEYS = 128
BLOCK = 64


def from_behind(array, axis, by):
    peers = lax.axis_size(axis)
    return lax.ppermute(array, axis, [(i, (i + by) % peers) for i in range(peers)])


def rms_norm(hidden, gain):
    return hidden * lax.rsqrt(jnp.mean(hidden * hidden, axis=-1, keepdims=True) + 1e-06) * gain


def swiglu(updown):
    return jax.nn.silu(updown[:, 0]) * updown[:, 1]


def layout(lengths_row, buffer):
    ends = jnp.cumsum(lengths_row, dtype=jnp.int32)
    token = jnp.arange(buffer, dtype=jnp.int32)
    start = jnp.max(jnp.where(ends[None, :] <= token[:, None], ends[None, :], 0), axis=1)
    position = token - start
    live = (token < ends[-1]).astype(jnp.float32)
    reset = (position[::BLOCK] == 0).astype(jnp.float32)
    return (live, position, reset)


def mixer_core(
    proj_query,
    proj_key,
    proj_value,
    proj_gate,
    proj_decay,
    conv_part,
    rate_part,
    bias_part,
    gain_part,
    position,
    reset,
):
    maximum_precision = lax.Precision.HIGHEST
    rows = proj_query.shape[0]
    heads_here = conv_part.shape[1]
    key_size = proj_query.shape[1] // heads_here
    value_size = proj_value.shape[1] // heads_here
    stacked = jnp.concatenate(
        [
            proj_query.reshape(rows, heads_here, key_size),
            proj_key.reshape(rows, heads_here, key_size),
            proj_value.reshape(rows, heads_here, value_size),
        ],
        axis=2,
    )
    convolved = jnp.zeros(stacked.shape, jnp.float32)
    for lag in range(conv_part.shape[0]):
        moved = jnp.pad(stacked, ((lag, 0), (0, 0), (0, 0)))[:rows]
        keep = (position >= lag).astype(jnp.float32)[:, None, None]
        convolved = convolved + conv_part[lag][None] * moved * keep
    convolved = jax.nn.silu(convolved)
    query = convolved[..., :key_size]
    keys = convolved[..., key_size : 2 * key_size]
    values = convolved[..., 2 * key_size :]
    query = (
        query
        * lax.rsqrt(jnp.sum(query * query, axis=-1, keepdims=True) + 1e-06)
        * key_size ** (-0.5)
    )
    keys = keys * lax.rsqrt(jnp.sum(keys * keys, axis=-1, keepdims=True) + 1e-06)
    decay_in = proj_decay.reshape(rows, heads_here, 2)
    log_decay = -jnp.exp(rate_part) * jax.nn.softplus(decay_in[..., 0] + bias_part)
    strength = jax.nn.sigmoid(decay_in[..., 1])
    blocks = rows // BLOCK

    def to_blocks(array):
        return array.reshape(blocks, BLOCK, heads_here, -1).transpose(0, 2, 1, 3)

    query_blocks = to_blocks(query)
    key_blocks = to_blocks(keys)
    value_blocks = to_blocks(values)
    log_blocks = log_decay.reshape(blocks, BLOCK, heads_here).transpose(0, 2, 1)
    strength_blocks = strength.reshape(blocks, BLOCK, heads_here).transpose(0, 2, 1)
    cumlog = jnp.cumsum(log_blocks, axis=-1)
    lower = jnp.tril(jnp.ones((BLOCK, BLOCK), jnp.float32)) > 0.5
    strict = jnp.tril(jnp.ones((BLOCK, BLOCK), jnp.float32), -1) > 0.5
    spread = cumlog[..., :, None] - cumlog[..., None, :]
    ratio = jnp.where(lower, jnp.exp(jnp.where(lower, spread, 0.0)), 0.0)
    inner = jnp.einsum("nhik,nhjk->nhij", key_blocks, key_blocks, precision=maximum_precision)
    system = jnp.eye(BLOCK, dtype=jnp.float32) + jnp.where(
        strict, strength_blocks[..., :, None] * inner * ratio, 0.0
    )
    scaled_keys = key_blocks * (jnp.exp(cumlog) * strength_blocks)[..., None]
    scaled_values = value_blocks * strength_blocks[..., None]
    solved = lax.linalg.triangular_solve(
        system,
        jnp.concatenate([scaled_keys, scaled_values], axis=-1),
        left_side=True,
        lower=True,
        unit_diagonal=True,
    )
    weight_part = solved[..., :key_size]
    update_part = solved[..., key_size:]
    scores = (
        jnp.einsum("nhik,nhjk->nhij", query_blocks, key_blocks, precision=maximum_precision) * ratio
    )
    query_decayed = query_blocks * jnp.exp(cumlog)[..., None]
    key_tail = key_blocks * jnp.exp(cumlog[..., -1:] - cumlog)[..., None]
    last = jnp.exp(cumlog[..., -1])

    def advance(running_state, pieces):
        (
            weight_block_tile,
            update_block_tile,
            query_block_tile,
            score_block_tile,
            trailing_block,
            final_block,
            reset_blk,
        ) = pieces
        running_state = running_state * (1.0 - reset_blk)
        new_state_value = update_block_tile - jnp.einsum(
            "sny,syj->snj", weight_block_tile, running_state, precision=maximum_precision
        )
        block_outcome = jnp.einsum(
            "sny,syj->snj", query_block_tile, running_state, precision=maximum_precision
        ) + jnp.einsum(
            "okp,opx->okx", score_block_tile, new_state_value, precision=maximum_precision
        )
        running_state = final_block[:, None, None] * running_state + jnp.einsum(
            "nbt,nbu->ntu", trailing_block, new_state_value, precision=maximum_precision
        )
        return (running_state, block_outcome)

    initial = jnp.zeros((heads_here, key_size, value_size), jnp.float32)
    unused, results = lax.scan(
        jax.checkpoint(advance),
        initial,
        (weight_part, update_part, query_decayed, scores, key_tail, last, reset),
    )
    heads_out = results.transpose(0, 2, 1, 3).reshape(rows, heads_here, value_size)
    normed = (
        heads_out
        * lax.rsqrt(jnp.mean(heads_out * heads_out, axis=-1, keepdims=True) + 1e-06)
        * gain_part
    )
    gating = jax.nn.silu(proj_gate.reshape(rows, heads_here, value_size))
    return (normed * gating).reshape(rows, heads_here * value_size)


def spread_rows(values):
    return lax.all_gather(values, "tensor", axis=0, tiled=True)


def collect_rows(partial_value):
    return lax.psum_scatter(partial_value, "tensor", scatter_dimension=0, tiled=True)


def spread_grads(values):
    return lax.all_gather(values, "tensor", axis=0, tiled=True)


def collect_grads(partial_value):
    return lax.psum_scatter(
        partial_value.astype(jnp.bfloat16), "tensor", scatter_dimension=0, tiled=True
    ).astype(jnp.float32)


def contract_rows(left, right):
    return lax.dot_general(
        left, right, (((0,), (0,)), ((), ())), preferred_element_type=jnp.float32
    )


def contract_cols(left, right):
    return lax.dot_general(
        left, right, (((1,), (1,)), ((), ())), preferred_element_type=jnp.float32
    )


def layer_forward(hidden, weights, smalls, structure):
    query_all, key_all, value_all, gate_all, decay_all, out_all, updown_all, down_all = weights
    gains, conv_local, rate_local, bias_local, gain_out = smalls
    live_local, position, reset = structure
    normed, norm_back = jax.vjp(rms_norm, hidden, gains[0])
    normed_all = spread_rows(normed.astype(jnp.bfloat16))
    projected = tuple(
        (
            jnp.dot(normed_all, matrix, preferred_element_type=jnp.float32)
            for matrix in (query_all, key_all, value_all, gate_all, decay_all)
        )
    )

    def core(
        proj_query,
        proj_key,
        proj_value,
        proj_gate,
        proj_decay,
        conv_part,
        rate_part,
        bias_part,
        gain_part,
    ):
        return mixer_core(
            proj_query,
            proj_key,
            proj_value,
            proj_gate,
            proj_decay,
            conv_part,
            rate_part,
            bias_part,
            gain_part,
            position,
            reset,
        )

    mixed, core_back = jax.vjp(
        core,
        projected[0],
        projected[1],
        projected[2],
        projected[3],
        projected[4],
        conv_local,
        rate_local,
        bias_local,
        gain_out,
    )
    mixed_low = mixed.astype(jnp.bfloat16)
    branch = collect_rows(jnp.dot(mixed_low, out_all, preferred_element_type=jnp.float32))
    after = hidden + live_local[:, None] * branch
    normed_two, norm_two_back = jax.vjp(rms_norm, after, gains[1])
    normed_two_all = spread_rows(normed_two.astype(jnp.bfloat16))
    updown = jnp.einsum(
        "td,dgf->tgf", normed_two_all, updown_all, preferred_element_type=jnp.float32
    )
    active, active_back = jax.vjp(swiglu, updown)
    active_low = active.astype(jnp.bfloat16)
    ffn = collect_rows(jnp.dot(active_low, down_all, preferred_element_type=jnp.float32))
    block_outcome = after + live_local[:, None] * ffn
    return (
        block_outcome,
        (
            norm_back,
            normed_all,
            core_back,
            mixed_low,
            norm_two_back,
            normed_two_all,
            active_back,
            active_low,
        ),
    )


def layer_backward(grad, kept, weights, structure):
    query_all, key_all, value_all, gate_all, decay_all, out_all, updown_all, down_all = weights
    (
        norm_back,
        normed_all,
        core_back,
        mixed_low,
        norm_two_back,
        normed_two_all,
        active_back,
        active_low,
    ) = kept
    live_local = structure[0]
    ffn_grad = spread_grads((live_local[:, None] * grad).astype(jnp.bfloat16))
    grad_down = contract_rows(active_low, ffn_grad)
    (updown_grad,) = active_back(contract_cols(ffn_grad, down_all))
    updown_low = updown_grad.astype(jnp.bfloat16)
    grad_updown = jnp.einsum(
        "td,tgf->dgf", normed_two_all, updown_low, preferred_element_type=jnp.float32
    )
    back_two = collect_grads(
        jnp.einsum("tgf,dgf->td", updown_low, updown_all, preferred_element_type=jnp.float32)
    )
    after_norm_grad, gain_two_grad = norm_two_back(back_two)
    grad_after = grad + after_norm_grad
    branch_grad = spread_grads((live_local[:, None] * grad_after).astype(jnp.bfloat16))
    grad_out = contract_rows(mixed_low, branch_grad)
    core_grads = core_back(contract_cols(branch_grad, out_all))
    inward = jnp.zeros((normed_all.shape[0], normed_all.shape[1]), jnp.float32)
    inward_grads = []
    for matrix, piece in zip((query_all, key_all, value_all, gate_all, decay_all), core_grads[:5]):
        piece_low = piece.astype(jnp.bfloat16)
        inward_grads.append(contract_rows(normed_all, piece_low))
        inward = inward + contract_cols(piece_low, matrix)
    back_one = collect_grads(inward)
    hidden_norm_grad, gain_one_grad = norm_back(back_one)
    grad_before = grad_after + hidden_norm_grad
    large = (
        inward_grads[0],
        inward_grads[1],
        inward_grads[2],
        inward_grads[3],
        inward_grads[4],
        grad_out,
        grad_updown,
        grad_down,
    )
    small = (
        jnp.stack([gain_one_grad, gain_two_grad]),
        core_grads[5],
        core_grads[6],
        core_grads[7],
        core_grads[8],
    )
    return (grad_before, large, small)


def on_device(
    inputs,
    lengths,
    norm_gain,
    w_query,
    w_key,
    w_value,
    w_gate,
    w_decay,
    conv_weight,
    head_rate,
    head_bias,
    out_gain,
    w_out,
    w_updown,
    w_down,
    cotangent,
):
    section_index = lax.axis_index("section")
    sections = lax.axis_size("section")
    first_section = section_index == 0
    part = lax.axis_index("tensor")
    micro = inputs.shape[0]
    rows_here = inputs.shape[1]
    buffer = rows_here * lax.axis_size("tensor")
    heads_here = w_query.shape[2] // KEYS
    offset = part * heads_here
    conv_local = lax.dynamic_slice_in_dim(conv_weight[0], offset, heads_here, 1)
    rate_local = lax.dynamic_slice_in_dim(head_rate[0], offset, heads_here, 0)
    bias_local = lax.dynamic_slice_in_dim(head_bias[0], offset, heads_here, 0)
    smalls = (norm_gain[0], conv_local, rate_local, bias_local, out_gain[0])

    def fetch():
        return (
            lax.all_gather(w_query[0], "dp", axis=0, tiled=True),
            lax.all_gather(w_key[0], "dp", axis=0, tiled=True),
            lax.all_gather(w_value[0], "dp", axis=0, tiled=True),
            lax.all_gather(w_gate[0], "dp", axis=0, tiled=True),
            lax.all_gather(w_decay[0], "dp", axis=0, tiled=True),
            lax.all_gather(w_out[0], "dp", axis=1, tiled=True),
            lax.all_gather(w_updown[0], "dp", axis=0, tiled=True),
            lax.all_gather(w_down[0], "dp", axis=1, tiled=True),
        )

    received = jnp.zeros((rows_here, inputs.shape[2]), jnp.bfloat16)
    saved_steps = []
    outputs = []
    for step in range(micro + 1):
        weights = fetch()
        lengths_row = lax.dynamic_index_in_dim(
            lengths[:, 0], jnp.clip(step - section_index, 0, micro - 1), 0, keepdims=False
        )
        live, position, reset = layout(lengths_row, buffer)
        live_local = lax.dynamic_slice_in_dim(live, part * rows_here, rows_here)
        structure = (live_local, position, reset)
        own = inputs[min(step, micro - 1)]
        hidden = jnp.where(first_section, own, received).astype(jnp.float32)
        block_outcome, kept = layer_forward(hidden, weights, smalls, structure)
        result_low = block_outcome.astype(jnp.bfloat16)
        received = from_behind(result_low, "section", 1)
        saved_steps.append((kept, structure))
        if step >= 1:
            outputs.append(jnp.where(first_section, received, result_low))
    grad_received = jnp.zeros((rows_here, inputs.shape[2]), jnp.bfloat16)
    input_grads = [None] * micro
    large_total = None
    small_total = None
    for step in range(micro + 1):
        weights = fetch()
        index = micro - step - section_index
        valid = ((index >= 0) & (index < micro)).astype(jnp.float32)
        kept, structure = saved_steps[micro - step]
        own_grad = cotangent[max(micro - 1 - step, 0)]
        grad = jnp.where(first_section, grad_received, own_grad).astype(jnp.float32) * valid
        grad_before, large, small = layer_backward(grad, kept, weights, structure)
        large_total = large if large_total is None else jax.tree.map(jnp.add, large_total, large)
        small_total = small if small_total is None else jax.tree.map(jnp.add, small_total, small)
        grad_low = grad_before.astype(jnp.bfloat16)
        grad_received = from_behind(grad_low, "section", 1)
        if step >= 1:
            input_grads[micro - step] = jnp.where(first_section, grad_low, grad_received)
    owned = (
        lax.psum_scatter(
            large_total[0].astype(jnp.bfloat16), "dp", scatter_dimension=0, tiled=True
        ).astype(jnp.float32),
        lax.psum_scatter(
            large_total[1].astype(jnp.bfloat16), "dp", scatter_dimension=0, tiled=True
        ).astype(jnp.float32),
        lax.psum_scatter(
            large_total[2].astype(jnp.bfloat16), "dp", scatter_dimension=0, tiled=True
        ).astype(jnp.float32),
        lax.psum_scatter(
            large_total[3].astype(jnp.bfloat16), "dp", scatter_dimension=0, tiled=True
        ).astype(jnp.float32),
        lax.psum_scatter(
            large_total[4].astype(jnp.bfloat16), "dp", scatter_dimension=0, tiled=True
        ).astype(jnp.float32),
        lax.psum_scatter(
            large_total[5].astype(jnp.bfloat16), "dp", scatter_dimension=1, tiled=True
        ).astype(jnp.float32),
        lax.psum_scatter(
            large_total[6].astype(jnp.bfloat16), "dp", scatter_dimension=0, tiled=True
        ).astype(jnp.float32),
        lax.psum_scatter(
            large_total[7].astype(jnp.bfloat16), "dp", scatter_dimension=1, tiled=True
        ).astype(jnp.float32),
    )
    gain_grads, conv_grads, rate_grads, bias_grads, out_gain_grads = small_total
    conv_full = lax.dynamic_update_slice_in_dim(
        jnp.zeros(conv_weight.shape[1:], jnp.float32), conv_grads, offset, 1
    )
    rate_full = lax.dynamic_update_slice_in_dim(
        jnp.zeros(head_rate.shape[1:], jnp.float32), rate_grads, offset, 0
    )
    bias_full = lax.dynamic_update_slice_in_dim(
        jnp.zeros(head_bias.shape[1:], jnp.float32), bias_grads, offset, 0
    )
    summed = lax.psum(
        (gain_grads, conv_full, rate_full, bias_full, out_gain_grads), ("dp", "tensor")
    )
    share = micro // sections
    output_mine = lax.dynamic_slice_in_dim(jnp.stack(outputs), section_index * share, share, 0)
    grad_mine = lax.dynamic_slice_in_dim(jnp.stack(input_grads), section_index * share, share, 0)
    return (
        output_mine,
        grad_mine,
        summed[0][None],
        owned[0][None],
        owned[1][None],
        owned[2][None],
        owned[3][None],
        owned[4][None],
        summed[1][None],
        summed[2][None],
        summed[3][None],
        summed[4][None],
        owned[5][None],
        owned[6][None],
        owned[7][None],
    )


def solution(mesh):
    in_specs = (
        P(None, ("dp", "tensor"), None),
        P(None, "dp", None),
        P("section", None, None),
        P("section", "dp", "tensor"),
        P("section", "dp", "tensor"),
        P("section", "dp", "tensor"),
        P("section", "dp", "tensor"),
        P("section", "dp", "tensor"),
        P("section", None, None, None),
        P("section", None),
        P("section", None),
        P("section", None),
        P("section", "tensor", "dp"),
        P("section", "dp", None, "tensor"),
        P("section", "tensor", "dp"),
        P(None, ("dp", "tensor"), None),
    )
    out_specs = (
        P("section", ("dp", "tensor"), None),
        P("section", ("dp", "tensor"), None),
        P("section", None, None),
        P("section", "dp", "tensor"),
        P("section", "dp", "tensor"),
        P("section", "dp", "tensor"),
        P("section", "dp", "tensor"),
        P("section", "dp", "tensor"),
        P("section", None, None, None),
        P("section", None),
        P("section", None),
        P("section", None),
        P("section", "tensor", "dp"),
        P("section", "dp", None, "tensor"),
        P("section", "tensor", "dp"),
    )
    return jax.shard_map(
        on_device, mesh=mesh, in_specs=in_specs, out_specs=out_specs, check_vma=False
    )
```

profile of v0, /device:TPU:8, one launch (start us, length us, event | category | flops | bytes accessed | tf_op | source)
XLA Modules:
  0.0 3395.4 jit_solution(12186682986655306771)
XLA Ops:
  114.8 158.9 %custom-call.21 = f32[16,2,1,64,64]{3,4,2,1,0:T(8,128)} custom-call(f32[16,2,1,64,64]{4,3,2,1,0:T(8,128)} %get-tuple-element.2421), custom_call_target="InvertDiagBlocksLowerTriangular" | custom-call | tf_op jit(solution)/shard_map/jvp()/triangular_solve/custom-call.1 | solution.py:98
  289.1 108.4 %while.126 = (s32[]{:T(128)}, f32[2,128,256]{2,1,0:T(8,128)S(1)}, f32[16,2,64,256]{3,2,1,0:T(8,128)S(1)}, f32[16,2,128,256]{3,2,1,0:T(8,128)}, f32[16,2]{1,0:T(8...) while((s32[]{:T(128)}, f32[2,128,256]{2,1,0:T(8,128)S(1)}, ...), condition=%wide.region_7.10_spmd.clone, body=%wide.region_6.9_spmd.clone.sunk | while | flops 176816128 | bytes 3282118 | solution.py:139
  420.2 50.1 %reduce-scatter.23.cloned.1.call-done = f32[256,1024]{1,0:T(8,128)} async-done(((f32[1024,1024]{1,0:T(8,128)}), f32[256,1024]{1,0:T(8,128)}) %reduce-scatter.23.cloned.1.call-update) | async-done | bytes 1048592 | tf_op jit(solution)/shard_map/reduce_scatter | solution.py:159
  473.8 54.1 %all-gather.56.cloned.1.call-done = bf16[1,1024,2,704]{1,3,2,0:T(8,128)(2,1)} async-done(((bf16[1,256,2,704]{1,3,2,0:T(8,128)(2,1)}), bf16[1,1024,2,704]{1,3,2,0:T(8,128)(2,1)}) %all-gather.56.cloned.1.call-update) | async-done | bytes 2883600 | tf_op jit(solution)/shard_map/all_gather | solution.py:358
  527.9 39.1 %all-gather.28.cloned.1.call-done = bf16[1024,1024]{1,0:T(8,128)(2,1)} async-done(((bf16[256,1024]{1,0:T(8,128)(2,1)}), bf16[1024,1024]{1,0:T(8,128)(2,1)}) %all-gather.28.cloned.1.call-update) | async-done | bytes 2097168 | tf_op jit(solution)/shard_map/all_gather | solution.py:155
  609.2 51.8 %reduce-scatter.25.cloned.1.call-done = f32[256,1024]{1,0:T(8,128)} async-done(((f32[1024,1024]{1,0:T(8,128)}), f32[256,1024]{1,0:T(8,128)}) %reduce-scatter.25.cloned.1.call-update) | async-done | bytes 1048592 | tf_op jit(solution)/shard_map/reduce_scatter | solution.py:159
  669.1 32.9 all-gather.30.cloned.1.call-done
  742.2 158.9 %custom-call.22 = f32[16,2,1,64,64]{3,4,2,1,0:T(8,128)} custom-call(f32[16,2,1,64,64]{4,3,2,1,0:T(8,128)} %get-tuple-element.2419), custom_call_target="InvertDiagBlocksLowerTriangular" | custom-call | tf_op jit(solution)/shard_map/jvp()/triangular_solve/custom-call.1 | solution.py:98
  916.1 117.8 %while.127 = (s32[]{:T(128)}, f32[2,128,256]{2,1,0:T(8,128)S(1)}, f32[16,2,64,256]{3,2,1,0:T(8,128)}, f32[16,2,128,256]{3,2,1,0:T(8,128)}, f32[16,2]{1,0:T(8,128...) while((s32[]{:T(128)}, f32[2,128,256]{2,1,0:T(8,128)S(1)}, ...), condition=%wide.region_19.22_spmd.clone, body=%wide.region_18.21_spmd.clone.sunk | while | flops 176816128 | bytes 3282118 | solution.py:139
  1051.3 50.9 %reduce-scatter.27.cloned.1.call-done = f32[256,1024]{1,0:T(8,128)} async-done(((f32[1024,1024]{1,0:T(8,128)}), f32[256,1024]{1,0:T(8,128)}) %reduce-scatter.27.cloned.1.call-update) | async-done | bytes 1048592 | tf_op jit(solution)/shard_map/reduce_scatter | solution.py:159
  1105.0 35.4 %all-gather.32.cloned.1.call-done = bf16[1024,1024]{1,0:T(8,128)(2,1)} async-done(((bf16[256,1024]{1,0:T(8,128)(2,1)}), bf16[1024,1024]{1,0:T(8,128)(2,1)}) %all-gather.32.cloned.1.call-update) | async-done | bytes 2097168 | tf_op jit(solution)/shard_map/all_gather | solution.py:155
  1152.4 52.8 %reduce-scatter.29.cloned.1.call-done = f32[256,1024]{1,0:T(8,128)} async-done(((f32[1024,1024]{1,0:T(8,128)}), f32[256,1024]{1,0:T(8,128)}) %reduce-scatter.29.cloned.1.call-update) | async-done | bytes 1048592 | tf_op jit(solution)/shard_map/reduce_scatter | solution.py:159
  1210.9 35.2 %all-gather.34.cloned.1.call-done = bf16[1024,1024]{1,0:T(8,128)(2,1)} async-done(((bf16[256,1024]{1,0:T(8,128)(2,1)}), bf16[1024,1024]{1,0:T(8,128)(2,1)}) %all-gather.34.cloned.1.call-update) | async-done | bytes 2097168 | tf_op jit(solution)/shard_map/all_gather | solution.py:155
  1286.9 158.9 %custom-call.23 = f32[16,2,1,64,64]{3,4,2,1,0:T(8,128)} custom-call(f32[16,2,1,64,64]{4,3,2,1,0:T(8,128)} %get-tuple-element.2417), custom_call_target="InvertDiagBlocksLowerTriangular" | custom-call | tf_op jit(solution)/shard_map/jvp()/triangular_solve/custom-call.1 | solution.py:98
  1462.9 129.4 %while.128 = (s32[]{:T(128)}, f32[2,128,256]{2,1,0:T(8,128)S(1)}, f32[16,2,64,256]{3,2,1,0:T(8,128)}, f32[16,2,128,256]{3,2,1,0:T(8,128)}, f32[16,2]{1,0:T(8,128...) while((s32[]{:T(128)}, f32[2,128,256]{2,1,0:T(8,128)S(1)}, ...), condition=%wide.region_31.34_spmd.clone, body=%wide.region_30.33_spmd.clone.sunk | while | flops 176816128 | bytes 3282118 | solution.py:139
  1610.1 50.9 %reduce-scatter.31.cloned.1.call-done = f32[256,1024]{1,0:T(8,128)} async-done(((f32[1024,1024]{1,0:T(8,128)}), f32[256,1024]{1,0:T(8,128)}) %reduce-scatter.31.cloned.1.call-update) | async-done | bytes 1048592 | tf_op jit(solution)/shard_map/reduce_scatter | solution.py:159
  1665.3 34.8 %all-gather.36.cloned.1.call-done = bf16[1024,1024]{1,0:T(8,128)(2,1)} async-done(((bf16[256,1024]{1,0:T(8,128)(2,1)}), bf16[1024,1024]{1,0:T(8,128)(2,1)}) %all-gather.36.cloned.1.call-update) | async-done | bytes 2097168 | tf_op jit(solution)/shard_map/all_gather | solution.py:155
  1790.0 53.7 %reduce-scatter.33.cloned.1.call-done = f32[256,1024]{1,0:T(8,128)} async-done(((f32[1024,1024]{1,0:T(8,128)}), f32[256,1024]{1,0:T(8,128)}) %reduce-scatter.33.cloned.1.call-update) | async-done | bytes 1048592 | tf_op jit(solution)/shard_map/reduce_scatter | solution.py:159
  1851.8 30.2 all-gather.40.cloned.1.call-done
  1904.0 219.6 %while.129 = (s32[]{:T(128)}, f32[2,128,256]{2,1,0:T(8,128)S(1)}, f32[16,2,64,128]{3,2,1,0:T(8,128)}, f32[16,2,64,256]{3,2,1,0:T(8,128)}, f32[16,2,64,128]{3,2,1...) while((s32[]{:T(128)}, f32[2,128,256]{2,1,0:T(8,128)S(1)}, ...), condition=%wide.region_41.44_spmd.clone, body=%wide.region_39.43_spmd.clone.sunk | while | flops 403505152 | bytes 7373151 | solution.py:139
  2186.4 35.3 %reduce-scatter.37.cloned.1.call-done = bf16[256,1024]{1,0:T(8,128)(2,1)} async-done(((bf16[1024,1024]{1,0:T(8,128)(2,1)}), bf16[256,1024]{1,0:T(8,128)(2,1)}) %reduce-scatter.37.cloned.1.call-update) | async-done | bytes 524304 | tf_op jit(solution)/shard_map/reduce_scatter | solution.py:167
  2231.2 35.2 %all-gather.42.cloned.1.call-done = bf16[1024,1024]{1,0:T(8,128)(2,1)} async-done(((bf16[256,1024]{1,0:T(8,128)(2,1)}), bf16[1024,1024]{1,0:T(8,128)(2,1)}) %all-gather.42.cloned.1.call-update) | async-done | bytes 2097168 | tf_op jit(solution)/shard_map/all_gather | solution.py:163
  2280.1 35.3 %reduce-scatter.39.cloned.1.call-done = bf16[256,1024]{1,0:T(8,128)(2,1)} async-done(((bf16[1024,1024]{1,0:T(8,128)(2,1)}), bf16[256,1024]{1,0:T(8,128)(2,1)}) %reduce-scatter.39.cloned.1.call-update) | async-done | bytes 524304 | tf_op jit(solution)/shard_map/reduce_scatter | solution.py:167
  2324.0 31.7 all-gather.44.cloned.1.call-done
  2377.5 196.2 %while.130 = (s32[]{:T(128)}, f32[2,128,256]{2,1,0:T(8,128)S(1)}, f32[16,2,64,128]{3,2,1,0:T(8,128)}, f32[16,2,64,256]{3,2,1,0:T(8,128)}, f32[16,2,64,128]{3,2,1...) while((s32[]{:T(128)}, f32[2,128,256]{2,1,0:T(8,128)S(1)}, ...), condition=%wide.region_60.65_spmd.clone, body=%wide.region_58.64_spmd.clone.sunk | while | flops 403505152 | bytes 7373151 | solution.py:139
  2636.9 35.3 %reduce-scatter.41.cloned.1.call-done = bf16[256,1024]{1,0:T(8,128)(2,1)} async-done(((bf16[1024,1024]{1,0:T(8,128)(2,1)}), bf16[256,1024]{1,0:T(8,128)(2,1)}) %reduce-scatter.41.cloned.1.call-update) | async-done | bytes 524304 | tf_op jit(solution)/shard_map/reduce_scatter | solution.py:167
  2679.2 35.0 %all-gather.46.cloned.1.call-done = bf16[1024,1024]{1,0:T(8,128)(2,1)} async-done(((bf16[256,1024]{1,0:T(8,128)(2,1)}), bf16[1024,1024]{1,0:T(8,128)(2,1)}) %all-gather.46.cloned.1.call-update) | async-done | bytes 2097168 | tf_op jit(solution)/shard_map/all_gather | solution.py:163
  2728.0 35.3 %reduce-scatter.43.cloned.1.call-done = bf16[256,1024]{1,0:T(8,128)(2,1)} async-done(((bf16[1024,1024]{1,0:T(8,128)(2,1)}), bf16[256,1024]{1,0:T(8,128)(2,1)}) %reduce-scatter.43.cloned.1.call-update) | async-done | bytes 524304 | tf_op jit(solution)/shard_map/reduce_scatter | solution.py:167
  2827.7 209.1 %while.131 = (s32[]{:T(128)}, f32[2,128,256]{2,1,0:T(8,128)S(1)}, f32[16,2,64,128]{3,2,1,0:T(8,128)}, f32[16,2,64,256]{3,2,1,0:T(8,128)}, f32[16,2,64,128]{3,2,1...) while((s32[]{:T(128)}, f32[2,128,256]{2,1,0:T(8,128)S(1)}, ...), condition=%wide.region_79.84_spmd.clone, body=%wide.region_77.83_spmd.clone.sunk | while | flops 403505152 | bytes 7373151 | solution.py:139
  3186.2 37.4 %reduce-scatter.45.cloned.1.call-done = bf16[256,1024]{1,0:T(8,128)(2,1)} async-done(((bf16[1024,1024]{1,0:T(8,128)(2,1)}), bf16[256,1024]{1,0:T(8,128)(2,1)}) %reduce-scatter.45.cloned.1.call-update) | async-done | bytes 524304 | tf_op jit(solution)/shard_map/reduce_scatter | solution.py:167
  3280.8 70.3 %all-reduce.63 = (f32[1,2,1024]{2,1,0:T(2,128)}, f32[1,8]{1,0:T(1,128)}, f32[1,8]{1,0:T(1,128)}, f32[1,256]{1,0:T(1,128)}) all-reduce(f32[1,2,1024]{2,1,0:T(2,128)S(1)} %fusion.513, f32[1,8]{1,0:T(1,128)S(1)} %dynamic_update_slice.198, ...), channel_id=1, replica_groups=mesh['section'=2,'dp'=4,'tensor'=4] {'dp','tensor'}, use_global_device_ids=true, to_apply=%region_99.104 | all-reduce | flops 2320 | bytes 18560 | tf_op jit(solution)/shard_map/psum | solution.py:435
  3352.1 34.9 %all-reduce.66.cloned.1.call-done = f32[1,4,8,512]{3,2,1,0:T(8,128)} async-done(((f32[1,4,8,512]{3,2,1,0:T(8,128)}), f32[1,4,8,512]{3,2,1,0:T(8,128)}) %all-reduce.66.cloned.1.call-update) | async-done | bytes 65552 | tf_op jit(solution)/shard_map/psum | solution.py:435
  (2810 shorter events, 1872.5 us)
Async XLA Ops:
  12.3 394.2 %all-gather.52.cloned.1.call-start = ((), (), s32[]{:S(2)}) async-start(), calls=%async_computation.53 | async-start | bytes 1310720 | tf_op jit(solution)/shard_map/all_gather | solution.py:355
  13.0 400.0 %all-gather.54.cloned.1.call-start = ((), (), s32[]{:S(2)}) async-start(), calls=%async_computation.54 | async-start | bytes 1310720 | tf_op jit(solution)/shard_map/all_gather | solution.py:357
  13.6 456.7 %reduce-scatter.23.cloned.1.call-start = ((), (), s32[]{:S(2)}) async-start(), calls=%async_computation.21 | async-start | bytes 5242880 | tf_op jit(solution)/shard_map/reduce_scatter | solution.py:159
  417.8 110.1 %all-gather.56.cloned.1.call-start = ((), (), s32[]{:S(2)}) async-start(), calls=%async_computation.55 | async-start | bytes 3604480 | tf_op jit(solution)/shard_map/all_gather | solution.py:358
  418.4 148.6 %all-gather.28.cloned.1.call-start = ((), (), s32[]{:S(2)}) async-start(), calls=%async_computation.22 | async-start | bytes 2621440 | tf_op jit(solution)/shard_map/all_gather | solution.py:155
  473.0 130.5 %all-gather.58.cloned.1.call-start = ((), (), s32[]{:S(2)}) async-start(), calls=%async_computation.56 | async-start | bytes 1802240 | tf_op jit(solution)/shard_map/all_gather | solution.py:359
  473.8 187.3 %reduce-scatter.25.cloned.1.call-start = ((), (), s32[]{:S(2)}) async-start(), calls=%async_computation.23 | async-start | bytes 5242880 | tf_op jit(solution)/shard_map/reduce_scatter | solution.py:159
  609.2 92.8 %all-gather.30.cloned.1.call-start = ((), (), s32[]{:S(2)}) async-start(), calls=%async_computation.24 | async-start | bytes 2621440 | tf_op jit(solution)/shard_map/all_gather | solution.py:155
  666.5 435.7 %reduce-scatter.27.cloned.1.call-start = ((), (), s32[]{:S(2)}) async-start(), calls=%async_computation.25 | async-start | bytes 5242880 | tf_op jit(solution)/shard_map/reduce_scatter | solution.py:159
  1049.3 91.0 %all-gather.32.cloned.1.call-start = ((), (), s32[]{:S(2)}) async-start(), calls=%async_computation.26 | async-start | bytes 2621440 | tf_op jit(solution)/shard_map/all_gather | solution.py:155
  1104.9 100.3 %reduce-scatter.29.cloned.1.call-start = ((), (), s32[]{:S(2)}) async-start(), calls=%async_computation.27 | async-start | bytes 5242880 | tf_op jit(solution)/shard_map/reduce_scatter | solution.py:159
  1152.3 93.8 %all-gather.34.cloned.1.call-start = ((), (), s32[]{:S(2)}) async-start(), calls=%async_computation.28 | async-start | bytes 2621440 | tf_op jit(solution)/shard_map/all_gather | solution.py:155
  1210.7 450.3 %reduce-scatter.31.cloned.1.call-start = ((), (), s32[]{:S(2)}) async-start(), calls=%async_computation.29 | async-start | bytes 5242880 | tf_op jit(solution)/shard_map/reduce_scatter | solution.py:159
  1608.2 91.9 %all-gather.36.cloned.1.call-start = ((), (), s32[]{:S(2)}) async-start(), calls=%async_computation.30 | async-start | bytes 2621440 | tf_op jit(solution)/shard_map/all_gather | solution.py:155
  1665.3 122.7 %reduce-scatter.35.cloned.1.call-start = ((), (), s32[]{:S(2)}) async-start(), calls=%async_computation.33 | async-start | bytes 2621440 | tf_op jit(solution)/shard_map/reduce_scatter | solution.py:167
  1752.6 91.0 %reduce-scatter.33.cloned.1.call-start = ((), (), s32[]{:S(2)}) async-start(), calls=%async_computation.31 | async-start | bytes 5242880 | tf_op jit(solution)/shard_map/reduce_scatter | solution.py:159
  1758.3 123.8 %all-gather.40.cloned.1.call-start = ((), (), s32[]{:S(2)}) async-start(), calls=%async_computation.34 | async-start | bytes 2621440 | tf_op jit(solution)/shard_map/all_gather | solution.py:163
  1846.6 375.2 %reduce-scatter.37.cloned.1.call-start = ((), (), s32[]{:S(2)}) async-start(), calls=%async_computation.35 | async-start | bytes 2621440 | tf_op jit(solution)/shard_map/reduce_scatter | solution.py:167
  2186.4 80.0 %all-gather.42.cloned.1.call-start = ((), (), s32[]{:S(2)}) async-start(), calls=%async_computation.36 | async-start | bytes 2621440 | tf_op jit(solution)/shard_map/all_gather | solution.py:163
  2231.0 84.4 %reduce-scatter.39.cloned.1.call-start = ((), (), s32[]{:S(2)}) async-start(), calls=%async_computation.37 | async-start | bytes 2621440 | tf_op jit(solution)/shard_map/reduce_scatter | solution.py:167
  2320.2 352.1 %reduce-scatter.41.cloned.1.call-start = ((), (), s32[]{:S(2)}) async-start(), calls=%async_computation.39 | async-start | bytes 2621440 | tf_op jit(solution)/shard_map/reduce_scatter | solution.py:167
  2636.9 77.3 %all-gather.46.cloned.1.call-start = ((), (), s32[]{:S(2)}) async-start(), calls=%async_computation.40 | async-start | bytes 2621440 | tf_op jit(solution)/shard_map/all_gather | solution.py:163
  2678.8 84.5 %reduce-scatter.43.cloned.1.call-start = ((), (), s32[]{:S(2)}) async-start(), calls=%async_computation.41 | async-start | bytes 2621440 | tf_op jit(solution)/shard_map/reduce_scatter | solution.py:167
  2767.9 379.5 %reduce-scatter.59.cloned.1.call-start = ((), (), s32[]{:S(2)}) async-start(), calls=%async_computation.51 | async-start | bytes 1802240 | tf_op jit(solution)/shard_map/reduce_scatter | solution.py:421
  2785.5 363.9 %reduce-scatter.57.cloned.1.call-start = ((), (), s32[]{:S(2)}) async-start(), calls=%async_computation.50 | async-start | bytes 3604480 | tf_op jit(solution)/shard_map/reduce_scatter | solution.py:418
  2803.7 349.2 %reduce-scatter.61.cloned.1.call-start = ((), (), s32[]{:S(2)}) async-start(), calls=%async_computation.57 | async-start | bytes 327680
  3107.0 77.4 %reduce-scatter.55.cloned.1.call-start = ((), (), s32[]{:S(2)}) async-start(), calls=%async_computation.49 | async-start | bytes 1310720 | tf_op jit(solution)/shard_map/reduce_scatter | solution.py:415
  3122.7 100.9 %reduce-scatter.45.cloned.1.call-start = ((), (), s32[]{:S(2)}) async-start(), calls=%async_computation.43 | async-start | bytes 2621440 | tf_op jit(solution)/shard_map/reduce_scatter | solution.py:167
  3131.5 119.3 %reduce-scatter.53.cloned.1.call-start = ((), (), s32[]{:S(2)}) async-start(), calls=%async_computation.47 | async-start | bytes 1310720 | tf_op jit(solution)/shard_map/reduce_scatter | solution.py:409
  3137.6 141.3 %reduce-scatter.51.cloned.1.call-start = ((), (), s32[]{:S(2)}) async-start(), calls=%async_computation.46 | async-start | bytes 1310720 | tf_op jit(solution)/shard_map/reduce_scatter | solution.py:406
  3144.0 243.0 %all-reduce.66.cloned.1.call-start = ((), (), s32[]{:S(2)}) async-start(), calls=%async_computation.48 | async-start | bytes 131072 | tf_op jit(solution)/shard_map/psum | solution.py:435
  3226.5 124.5 %collective-permute-start.5 = (bf16[256,1024]{1,0:T(8,128)(2,1)S(1)}, bf16[256,1024]{1,0:T(8,128)(2,1)S(1)}, u32[]{:S(2)}, u32[]{:S(2)}) collective-permute-start(bf16[256,1024]{1,0:T(8,128)(2,1)S(1)} %fusion.268), channel_id=1, source_target_pairs={{0,16},{16,0},{1,17},{17,1},{2,18},{18,2},{3,19},{19,3},{4,20},{20... | collective-permute-start | bytes 1572872 | tf_op jit(solution)/shard_map/ppermute | solution.py:12
  (457 other events, 10673.4 us)
Sparse Core Ops, SparseCore 0:
  11.6 36.4 all-gather.25
  49.7 27.8 all-gather.49
  79.2 27.4 all-gather.51
  108.1 30.3 all-gather.53
  418.0 52.2 reduce-scatter.22
  471.8 56.1 all-gather.55
  530.5 36.4 all-gather.27
  568.7 34.7 all-gather.57
  609.3 51.7 reduce-scatter.24
  666.7 35.2 all-gather.29
  1049.5 52.6 reduce-scatter.26
  1105.0 35.2 all-gather.31
  1152.4 52.6 reduce-scatter.28
  1210.8 35.2 all-gather.33
  1608.3 52.6 reduce-scatter.30
  1664.8 35.2 all-gather.35
  1702.5 35.2 all-gather.37
  1752.7 35.2 reduce-scatter.34
  1791.0 52.6 reduce-scatter.32
  1846.7 35.2 all-gather.39
  2186.5 35.2 reduce-scatter.36
  2231.1 35.2 all-gather.41
  2280.2 35.1 reduce-scatter.38
  2320.3 35.3 all-gather.43
  2637.0 35.2 reduce-scatter.40
  2678.9 35.2 all-gather.45
  2728.0 35.1 reduce-scatter.42
  2768.0 35.3 all-gather.47
  2806.4 31.3 reduce-scatter.58
  2840.1 56.2 reduce-scatter.56
  3187.6 35.9 reduce-scatter.44
  3285.0 101.9 all-reduce.65
  (6 shorter events, 133.1 us)
where the time goes:
time: 3430 us; the launch traced here: 3400 us
  waiting for transfers between devices  1070 us (31%)
  matrix products  865 us (25%)
  other arithmetic  731 us (21%)
  local copies, waits for them, and re-layouts  517 us (15%)
  blocking collectives  114 us (3%)
  loops' own time  68.2 us (2%)
    another operation x4, other arithmetic, mixer_core(): lax.linalg.triangular_solve(system, jnp.concatenate([scaled_keys, scaled_...  477 us
    reduce_scatter x6, waiting for transfers between devices, collect_rows(): lax.psum_scatter(partial_value, 'tensor', scatter_dimension=0, tiled=True)  310 us
    reduce_scatter x6, waiting for transfers between devices, collect_grads(): lax.psum_scatter(partial_value.astype(jnp.bfloat16), 'tensor', scatter_di...  208 us
    squeeze x240, local copies, waits for them, and re-layouts, mixer_core(): lax.scan(jax.checkpoint(advance), initial, (weight_part, update_part, que...  197 us
    all_gather x6, waiting for transfers between devices, spread_rows(): return lax.all_gather(values, 'tensor', axis=0, tiled=True)  177 us
    all_gather x6, waiting for transfers between devices, spread_grads(): return lax.all_gather(values, 'tensor', axis=0, tiled=True)  162 us
    dot_general x144, matrix products, advance(): jnp.einsum('okp,opx->okx', score_block_tile, new_state_value, precision=m...  150 us
    dot_general x192, matrix products, advance(): jnp.einsum('sny,syj->snj', weight_block_tile, running_state, precision=ma...  142 us
  transfers between devices with their start and end apart: 44, of which 34 were waited for; matrix products, arithmetic and copies ran while one was open for 22% of the time, Pallas kernels for 0%

commit v1 on v0

v1 whole, which is shorter than its diff:
```python
import jax
import jax.numpy as jnp
from jax import lax
from jax.experimental import pallas as pl
from jax.experimental.pallas import tpu as pltpu
from jax.sharding import PartitionSpec as P

KEYS = 128
BLOCK = 64
F32 = jnp.float32
LOW = jnp.bfloat16
VMEM_LIMIT = 56 * 1024 * 1024


def _dot(left, right, dims):
    return lax.dot_general(
        left.astype(LOW), right.astype(LOW), (dims, ((), ())), preferred_element_type=F32
    )


def mm(left, right):
    return _dot(left, right, ((1,), (0,)))


def mm_nt(left, right):
    return _dot(left, right, ((1,), (1,)))


def mm_tn(left, right):
    return _dot(left, right, ((0,), (0,)))


def exact(left, right, dims=((1,), (0,))):
    return lax.dot_general(
        left, right, (dims, ((), ())), precision=lax.Precision.HIGHEST, preferred_element_type=F32
    )


def mm_split(left, right):
    left_high = left.astype(LOW)
    right_high = right.astype(LOW)
    left_low = (left - left_high.astype(F32)).astype(LOW)
    right_low = (right - right_high.astype(F32)).astype(LOW)
    return mm(left_high, right_high) + (mm(left_high, right_low) + mm(left_low, right_high))


def grid_of(size):
    row = lax.broadcasted_iota(jnp.int32, (size, size), 0)
    col = lax.broadcasted_iota(jnp.int32, (size, size), 1)
    return row, col


def rowsum(array):
    return jnp.sum(array, axis=1, keepdims=True)


def unit_lower_inverse(below, row, col):
    ones = jnp.where(row == col, 1.0, 0.0)
    inverse = ones - jnp.where((row // 2 == col // 2), below, 0.0)
    half = 2
    while half < BLOCK:
        span = 2 * half
        part = (row // span == col // span) & (row % span >= half) & (col % span < half)
        piece = jnp.where(part, below, 0.0)
        inverse = inverse - mm_split(inverse, mm_split(piece, inverse))
        half = span
    return inverse


def convolve(own, before, taps):
    padded = jnp.concatenate([before, own], axis=0)
    shifted = [own]
    total = taps[0:1] * own
    for lag in range(1, taps.shape[0]):
        moved = pltpu.roll(padded, lag, 0)[8:]
        shifted.append(moved)
        total = total + taps[lag : lag + 1] * moved
    return shifted, total


def decay_of(pair, rate_exp, bias, row, col):
    shifted = pair[:, 0:1] + bias
    soft = jnp.maximum(shifted, 0.0) + jnp.log1p(jnp.exp(-jnp.abs(shifted)))
    log_decay = -rate_exp * soft
    strength = jax.nn.sigmoid(pair[:, 1:2])
    lower = jnp.where(row >= col, 1.0, 0.0)
    after = jnp.where(row > col, 1.0, 0.0)
    spread = exact(lower, log_decay * after)
    cumlog = spread[:, 0:1] + log_decay[0:1]
    ratio = jnp.where(row >= col, jnp.exp(spread), 0.0)
    return shifted, log_decay, strength, cumlog, ratio


def unit(array, scale=1.0):
    inv = lax.rsqrt(rowsum(array * array) + 1e-06)
    return array * inv, inv * scale


def mixer_forward_kernel(meta, params, mine, other, taps, gain, mixed_a, mixed_b, o_a, o_b, states, inverses, state, carry):
    step = pl.program_id(0)
    groups = mine.shape[0] // BLOCK
    row, col = grid_of(BLOCK)

    @pl.when(step == 0)
    def _():
        state[...] = jnp.zeros_like(state)
        carry[...] = jnp.zeros_like(carry)

    sources = (mine, other)
    outs = (mixed_a, mixed_b)
    os = (o_a, o_b)
    prepared = {}
    for head in range(2):
        source = sources[head]
        for block in range(groups):
            rows = pl.ds(block * BLOCK, BLOCK)
            keep = 1.0 - meta[1 + step * groups + block].astype(F32)
            own = source[rows, 0 : 4 * KEYS]
            if block == 0:
                before = carry[head]
            else:
                before = source[pl.ds(block * BLOCK - 8, 8), 0 : 4 * KEYS]
            _, conv = convolve(own, before * keep, taps[head])
            active = conv * jax.nn.sigmoid(conv)
            query, _ = unit(active[:, :KEYS])
            query = query * KEYS ** (-0.5)
            keys, _ = unit(active[:, KEYS : 2 * KEYS])
            values = active[:, 2 * KEYS :]
            _, _, strength, cumlog, ratio = decay_of(
                source[rows, 6 * KEYS : 6 * KEYS + 2], params[head, 0], params[head, 1], row, col
            )
            gamma = jnp.exp(cumlog)
            last = cumlog[BLOCK - 1 :]
            both = mm_nt(jnp.concatenate([keys, query], axis=0), keys)
            below = jnp.where(row > col, strength * ratio * both[:BLOCK], 0.0)
            inverse = unit_lower_inverse(below, row, col)
            inverses[block, head] = inverse
            weight = mm(inverse, (strength * gamma) * keys).astype(LOW)
            update = mm(inverse, strength * values)
            scores = (both[BLOCK:] * ratio).astype(LOW)
            tail = (keys * jnp.exp(last - cumlog)).astype(LOW)
            prepared[block, head] = (
                weight,
                update,
                scores,
                tail,
                (query * gamma).astype(LOW),
                jnp.exp(last),
                keep,
            )
        carry[head] = source[pl.ds(groups * BLOCK - 8, 8), 0 : 4 * KEYS]
    current = [state[0], state[1]]
    for block in range(groups):
        for head in range(2):
            weight, update, scores, tail, query_low, last, keep = prepared[block, head]
            held = current[head] * keep
            held_low = held.astype(LOW)
            states[block, head] = held_low
            fresh = (update - mm(weight, held_low)).astype(LOW)
            current[head] = last * held + mm_tn(tail, fresh)
            rows = pl.ds(block * BLOCK, BLOCK)
            outcome = mm(query_low, held_low) + mm(scores, fresh)
            os[head][rows, :] = outcome
            inv = lax.rsqrt(jnp.mean(outcome * outcome, axis=1, keepdims=True) + 1e-06)
            gate = sources[head][rows, 4 * KEYS : 6 * KEYS]
            mixed = outcome * inv * gain[...] * (gate * jax.nn.sigmoid(gate))
            outs[head][rows, :] = mixed.astype(LOW)
    state[0] = current[0]
    state[1] = current[1]


def mixer_backward_kernel(
    meta, params, mine, other, edge_a, edge_b, o_a, o_b, dm_a, dm_b, states, inverses, taps, gain,
    d_mine, d_other, d_taps, d_gain, d_params, state_grad, carry,
):
    step = pl.program_id(0)
    seq = pl.num_programs(0) - 1 - step
    groups = mine.shape[0] // BLOCK
    row, col = grid_of(BLOCK)

    @pl.when(step == 0)
    def _():
        state_grad[...] = jnp.zeros_like(state_grad)
        carry[...] = jnp.zeros_like(carry)
        d_taps[...] = jnp.zeros_like(d_taps)
        d_gain[...] = jnp.zeros_like(d_gain)
        d_params[...] = jnp.zeros_like(d_params)

    sources = (mine, other)
    edges = (edge_a, edge_b)
    os = (o_a, o_b)
    dms = (dm_a, dm_b)
    dsts = (d_mine, d_other)
    lower = jnp.where(row >= col, 1.0, 0.0)
    after = jnp.where(row > col, 1.0, 0.0)
    kept = {}
    gain_total = jnp.zeros((1, 2 * KEYS), F32)
    for head in range(2):
        source = sources[head]
        for block in range(groups):
            rows = pl.ds(block * BLOCK, BLOCK)
            keep = 1.0 - meta[1 + seq * groups + block].astype(F32)
            own = source[rows, 0 : 4 * KEYS]
            if block == 0:
                before = edges[head][:, 0 : 4 * KEYS]
            else:
                before = source[pl.ds(block * BLOCK - 8, 8), 0 : 4 * KEYS]
            shifted, conv = convolve(own, before * keep, taps[head])
            sig = jax.nn.sigmoid(conv)
            active = conv * sig
            slope = sig * (1.0 + conv * (1.0 - sig))
            query_unit, query_inv = unit(active[:, :KEYS])
            query = query_unit * KEYS ** (-0.5)
            keys, keys_inv = unit(active[:, KEYS : 2 * KEYS])
            values = active[:, 2 * KEYS :]
            decay_pre, log_decay, strength, cumlog, ratio = decay_of(
                source[rows, 6 * KEYS : 6 * KEYS + 2], params[head, 0], params[head, 1], row, col
            )
            gamma = jnp.exp(cumlog)
            last = cumlog[BLOCK - 1 :]
            tail_scale = jnp.exp(last - cumlog)
            both = mm_nt(jnp.concatenate([keys, query], axis=0), keys)
            near = jnp.where(row > col, ratio * both[:BLOCK], 0.0)
            scores = both[BLOCK:] * ratio
            inverse = inverses[block, head].astype(LOW)
            held = states[block, head]
            weight = mm(inverse, (strength * gamma) * keys).astype(LOW)
            key_state = mm(keys, held)
            lacking = values - gamma * key_state
            fresh = mm(inverse, strength * lacking)
            outcome = os[head][rows, :]
            d_mixed = dms[head][rows, :]
            gate = source[rows, 4 * KEYS : 6 * KEYS]
            gate_sig = jax.nn.sigmoid(gate)
            gate_act = gate * gate_sig
            inv = lax.rsqrt(jnp.mean(outcome * outcome, axis=1, keepdims=True) + 1e-06)
            normed = outcome * inv
            weighted = d_mixed * gain[...]
            d_gate = weighted * normed * (gate_sig * (1.0 + gate * (1.0 - gate_sig)))
            dsts[head][rows, 4 * KEYS : 6 * KEYS] = d_gate.astype(LOW)
            gain_total = gain_total + jnp.sum(d_mixed * normed * gate_act, axis=0, keepdims=True)
            d_normed = weighted * gate_act
            d_out = inv * (d_normed - normed * jnp.mean(d_normed * normed, axis=1, keepdims=True))
            d_out_low = d_out.astype(LOW)
            part_fresh = mm_tn(scores, d_out_low)
            part_state = mm_tn(query * gamma, d_out_low)
            tail = keys * tail_scale
            kept[block, head] = dict(
                keep=keep, shifted=shifted, slope=slope, query_unit=query_unit, query_inv=query_inv,
                query=query, keys=keys, keys_inv=keys_inv, decay_pre=decay_pre, log_decay=log_decay,
                strength=strength, ratio=ratio, gamma=gamma, last=jnp.exp(last), tail=tail,
                tail_scale=tail_scale, near=near, scores=scores, inverse=inverse, held=held,
                weight=weight, key_state=key_state, lacking=lacking, fresh=fresh,
                d_out_low=d_out_low, part_fresh=part_fresh, part_state=part_state,
            )
    d_gain[...] += gain_total
    current = [state_grad[0], state_grad[1]]
    for block in reversed(range(groups)):
        for head in range(2):
            k = kept[block, head]
            k["ds"] = current[head]
            d_fresh = (k["part_fresh"] + mm(k["tail"], current[head])).astype(LOW)
            k["d_fresh"] = d_fresh
            below = k["last"] * current[head] + k["part_state"] - mm_tn(k["weight"], d_fresh)
            current[head] = below * k["keep"]
    state_grad[0] = current[0]
    state_grad[1] = current[1]
    for head in range(2):
        next_rows = carry[head]
        taps_here = taps[head]
        tap_sums = [jnp.zeros((1, 4 * KEYS), F32) for _ in range(4)]
        rate_sum = jnp.zeros((1, 1), F32)
        bias_sum = jnp.zeros((1, 1), F32)
        for block in reversed(range(groups)):
            rows = pl.ds(block * BLOCK, BLOCK)
            k = kept[block, head]
            keys, query, gamma, strength = k["keys"], k["query"], k["gamma"], k["strength"]
            fresh_low = k["fresh"].astype(LOW)
            ds_low = k["ds"].astype(LOW)
            d_fill = mm_tn(k["inverse"], k["d_fresh"])
            grams = mm_nt(jnp.concatenate([d_fill.astype(LOW), k["d_out_low"]], axis=0), fresh_low)
            d_below = jnp.where(row > col, -grams[:BLOCK], 0.0)
            d_scores = grams[BLOCK:]
            d_tail = mm_nt(fresh_low, ds_low)
            scaled = (strength * gamma) * d_fill
            through = mm_nt(jnp.concatenate([k["d_out_low"], scaled.astype(LOW)], axis=0), k["held"])
            d_qk = (d_scores * k["ratio"]).astype(LOW)
            d_kk = (strength * d_below * k["ratio"]).astype(LOW)
            pair = mm(jnp.concatenate([d_qk, d_kk], axis=0), keys)
            d_query = gamma * through[:BLOCK] + pair[:BLOCK]
            d_keys = (
                pair[BLOCK:]
                - through[BLOCK:]
                + k["tail_scale"] * d_tail
                + mm_tn(jnp.concatenate([d_qk, d_kk], axis=0), jnp.concatenate([query, keys], axis=0))
            )
            d_values = strength * d_fill
            d_strength = rowsum(d_fill * k["lacking"]) + rowsum(d_below * k["near"])
            spread_grad = d_scores * k["scores"] + strength * d_below * k["near"]
            tail_part = rowsum(d_tail * k["tail"])
            d_cum = gamma * rowsum(query * through[:BLOCK]) - rowsum(scaled * k["key_state"]) - tail_part
            at_last = jnp.sum(tail_part, axis=0, keepdims=True) + k["last"] * jnp.sum(
                rowsum(k["ds"] * k["held"].astype(F32)), axis=0, keepdims=True
            )
            place = lax.broadcasted_iota(jnp.int32, (BLOCK, 1), 0)
            d_cum = d_cum + jnp.where(place == BLOCK - 1, at_last, 0.0)
            spread_grad = spread_grad + jnp.where(col == 0, d_cum, 0.0)
            d_log = rowsum(exact(lower, spread_grad, ((0,), (0,))) * after)
            d_log = d_log + jnp.where(place == 0, jnp.sum(d_cum, axis=0, keepdims=True), 0.0)
            d_decay = d_log * (-params[head, 0]) * jax.nn.sigmoid(k["decay_pre"])
            rate_sum = rate_sum + jnp.sum(d_log * k["log_decay"], axis=0, keepdims=True)
            bias_sum = bias_sum + jnp.sum(d_decay, axis=0, keepdims=True)
            d_write = d_strength * strength * (1.0 - strength)
            dsts[head][rows, 6 * KEYS : 6 * KEYS + 2] = jnp.concatenate([d_decay, d_write], axis=1).astype(LOW)
            d_query = d_query * KEYS ** (-0.5)
            unit_q = k["query_unit"]
            d_active = jnp.concatenate(
                [
                    k["query_inv"] * (d_query - unit_q * rowsum(unit_q * d_query)),
                    k["keys_inv"] * (d_keys - keys * rowsum(keys * d_keys)),
                    d_values,
                ],
                axis=1,
            )
            d_conv = d_active * k["slope"]
            padded = jnp.concatenate([d_conv, next_rows], axis=0)
            d_own = taps_here[0:1] * d_conv
            tap_sums[0] = tap_sums[0] + jnp.sum(d_conv * k["shifted"][0], axis=0, keepdims=True)
            for lag in range(1, 4):
                moved = pltpu.roll(padded, BLOCK + 8 - lag, 0)[:BLOCK]
                d_own = d_own + taps_here[lag : lag + 1] * moved
                tap_sums[lag] = tap_sums[lag] + jnp.sum(
                    d_conv * k["shifted"][lag], axis=0, keepdims=True
                )
            dsts[head][rows, 0 : 4 * KEYS] = d_own.astype(LOW)
            next_rows = d_conv[0:8] * k["keep"]
        carry[head] = next_rows
        for lag in range(4):
            d_taps[head, lag : lag + 1, :] += tap_sums[lag]
        lane = lax.broadcasted_iota(jnp.int32, (1, KEYS), 1)
        d_params[head : head + 1, :] += jnp.where(lane == 0, rate_sum, 0.0) + jnp.where(
            lane == 1, bias_sum, 0.0
        )


def mixer_forward(meta, params, mine, other, taps, gain, parts):
    rows = mine.shape[0]
    wide = mine.shape[1]
    group = rows // parts
    per = group // BLOCK

    def place(step, meta):
        return (step ^ meta[0], 0)

    def stacked(step, meta):
        return (step, 0, 0, 0)

    vals = 2 * KEYS
    row_spec = pl.BlockSpec((group, vals), place)
    return pl.pallas_call(
        mixer_forward_kernel,
        grid_spec=pltpu.PrefetchScalarGridSpec(
            num_scalar_prefetch=1,
            grid=(parts,),
            in_specs=[
                pl.BlockSpec(memory_space=pltpu.SMEM),
                pl.BlockSpec((group, wide), place),
                pl.BlockSpec((group, wide), place),
                pl.BlockSpec((2, 4, 4 * KEYS), lambda step, meta: (0, 0, 0)),
                pl.BlockSpec((1, vals), lambda step, meta: (0, 0)),
            ],
            out_specs=[
                row_spec,
                row_spec,
                row_spec,
                row_spec,
                pl.BlockSpec((per, 2, KEYS, vals), stacked),
                pl.BlockSpec((per, 2, BLOCK, BLOCK), stacked),
            ],
            scratch_shapes=[pltpu.VMEM((2, KEYS, vals), F32), pltpu.VMEM((2, 8, 4 * KEYS), F32)],
        ),
        out_shape=[
            jax.ShapeDtypeStruct((rows, vals), LOW),
            jax.ShapeDtypeStruct((rows, vals), LOW),
            jax.ShapeDtypeStruct((rows, vals), F32),
            jax.ShapeDtypeStruct((rows, vals), F32),
            jax.ShapeDtypeStruct((rows // BLOCK, 2, KEYS, vals), LOW),
            jax.ShapeDtypeStruct((rows // BLOCK, 2, BLOCK, BLOCK), F32),
        ],
        compiler_params=pltpu.CompilerParams(vmem_limit_bytes=VMEM_LIMIT),
        name="mixer_forward",
    )(meta, params, mine, other, taps, gain)


def mixer_backward(meta, params, mine, other, o_a, o_b, dm_a, dm_b, states, inverses, taps, gain, parts):
    rows = mine.shape[0]
    wide = mine.shape[1]
    group = rows // parts
    per = group // BLOCK

    def place(step, meta):
        return ((parts - 1 - step) ^ meta[0], 0)

    def edge(step, meta):
        return ((jnp.maximum(parts - 2 - step, 0) ^ meta[0]) * (group // 8) + group // 8 - 1, 0)

    def stacked(step, meta):
        return (parts - 1 - step, 0, 0, 0)

    vals = 2 * KEYS
    row_spec = pl.BlockSpec((group, vals), place)
    wide_spec = pl.BlockSpec((group, wide), place)
    edge_spec = pl.BlockSpec((8, wide), edge)
    taps_spec = pl.BlockSpec((2, 4, 4 * KEYS), lambda step, meta: (0, 0, 0))
    gain_spec = pl.BlockSpec((1, vals), lambda step, meta: (0, 0))
    return pl.pallas_call(
        mixer_backward_kernel,
        grid_spec=pltpu.PrefetchScalarGridSpec(
            num_scalar_prefetch=1,
            grid=(parts,),
            in_specs=[
                pl.BlockSpec(memory_space=pltpu.SMEM),
                wide_spec,
                wide_spec,
                edge_spec,
                edge_spec,
                row_spec,
                row_spec,
                row_spec,
                row_spec,
                pl.BlockSpec((per, 2, KEYS, vals), stacked),
                pl.BlockSpec((per, 2, BLOCK, BLOCK), stacked),
                taps_spec,
                gain_spec,
            ],
            out_specs=[
                wide_spec,
                wide_spec,
                taps_spec,
                gain_spec,
                pl.BlockSpec((2, KEYS), lambda step, meta: (0, 0)),
            ],
            scratch_shapes=[pltpu.VMEM((2, KEYS, vals), F32), pltpu.VMEM((2, 8, 4 * KEYS), F32)],
        ),
        out_shape=[
            jax.ShapeDtypeStruct((rows, wide), LOW),
            jax.ShapeDtypeStruct((rows, wide), LOW),
            jax.ShapeDtypeStruct((2, 4, 4 * KEYS), F32),
            jax.ShapeDtypeStruct((1, vals), F32),
            jax.ShapeDtypeStruct((2, KEYS), F32),
        ],
        compiler_params=pltpu.CompilerParams(vmem_limit_bytes=VMEM_LIMIT),
        name="mixer_backward",
    )(meta, params, mine, other, mine, other, o_a, o_b, dm_a, dm_b, states, inverses, taps, gain)


def swap_section(array):
    return lax.ppermute(array, "section", [(0, 1), (1, 0)])


def send_by(array, offset):
    peers = lax.axis_size("tensor")
    return lax.ppermute(array, "tensor", [(i, i ^ offset) for i in range(peers)])


def spread_rows(values):
    peers = lax.axis_size("tensor")
    return [values] + [send_by(values, k) for k in range(1, peers)]


def collect_rows(parts):
    total = parts[0]
    for k in range(1, len(parts)):
        total = total + send_by(parts[k].astype(LOW), k).astype(F32)
    return total


def nn(left, right):
    return jnp.dot(left, right, preferred_element_type=F32)


def nt(left, right):
    return lax.dot_general(left, right, (((1,), (1,)), ((), ())), preferred_element_type=F32)


def tn(left, right):
    return lax.dot_general(left, right, (((0,), (0,)), ((), ())), preferred_element_type=F32)


def norm_forward(hidden, gain):
    inv = lax.rsqrt(jnp.mean(hidden * hidden, axis=-1, keepdims=True) + 1e-06)
    return (hidden * inv * gain).astype(LOW), inv


def norm_backward(hidden, inv, gain, grad):
    normed = hidden * inv
    weighted = grad * gain
    back = inv * (weighted - normed * jnp.mean(weighted * normed, axis=-1, keepdims=True))
    return back, jnp.sum(grad * normed, axis=0)


def layout(lengths_row, buffer):
    ends = jnp.cumsum(lengths_row, dtype=jnp.int32)
    token = jnp.arange(buffer, dtype=jnp.int32)
    start = jnp.max(jnp.where(ends[None, :] <= token[:, None], ends[None, :], 0), axis=1)
    live = (token < ends[-1]).astype(F32)
    reset = ((token - start)[::BLOCK] == 0).astype(jnp.int32)
    return live, reset


def split_rows(array, count):
    size = array.shape[0] // count
    return [array[k * size : (k + 1) * size] for k in range(count)]


def layer_forward(hidden, weights, gains, small, meta, live):
    mix_mine, mix_other, out_mine, out_other, up_mine, up_other, down_mine, down_other = weights
    params, taps, gain_out = small
    peers = lax.axis_size("tensor")
    normed, inv_one = norm_forward(hidden, gains[0])
    normed_all = jnp.concatenate(spread_rows(normed), axis=0)
    mine = nn(normed_all, mix_mine)
    other = nn(normed_all, mix_other)
    mixed_a, mixed_b, o_a, o_b, states, inverses = mixer_forward(
        meta, params, mine, other, taps, gain_out, peers
    )
    branch = collect_rows(
        [
            nt(a, out_mine) + nt(b, out_other)
            for a, b in zip(split_rows(mixed_a, peers), split_rows(mixed_b, peers))
        ]
    )
    after = hidden + live * branch
    normed_two, inv_two = norm_forward(after, gains[1])
    normed_two_all = spread_rows(normed_two)
    half = down_mine.shape[1]
    ups, actives, ffn = [], [], []
    for chunk in normed_two_all:
        pair = (nn(chunk, up_mine), nn(chunk, up_other))
        active = [(jax.nn.silu(u[:, :half]) * u[:, half:]).astype(LOW) for u in pair]
        ups.append(pair)
        actives.append(active)
        ffn.append(nt(active[0], down_mine) + nt(active[1], down_other))
    result = after + live * collect_rows(ffn)
    kept = (
        hidden, inv_one, normed_all, mine, other, o_a, o_b, states, inverses, mixed_a, mixed_b,
        after, inv_two, normed_two_all, ups, actives,
    )
    return result, kept


def layer_backward(grad, kept, weights, gains, small, meta, live, owners):
    mix_mine, mix_other, out_mine, out_other, up_mine, up_other, down_mine, down_other = weights
    params, taps, gain_out = small
    (
        hidden, inv_one, normed_all, mine, other, o_a, o_b, states, inverses, mixed_a, mixed_b,
        after, inv_two, normed_two_all, ups, actives,
    ) = kept
    peers = lax.axis_size("tensor")
    half = down_mine.shape[1]
    ffn_grads = spread_rows((live * grad).astype(LOW))
    d_ups, back = ([], []), []
    for chunk, pair in zip(ffn_grads, ups):
        partial = None
        for side, (u, down, up) in enumerate(
            ((pair[0], down_mine, up_mine), (pair[1], down_other, up_other))
        ):
            d_active = nn(chunk, down)
            gate, lift = u[:, :half], u[:, half:]
            sig = jax.nn.sigmoid(gate)
            d_gate = d_active * lift * (sig * (1.0 + gate * (1.0 - sig)))
            d_lift = d_active * (gate * sig)
            d_up = jnp.concatenate([d_gate, d_lift], axis=1).astype(LOW)
            d_ups[side].append(d_up)
            piece = nt(d_up, up)
            partial = piece if partial is None else partial + piece
        back.append(partial)
    back_two = collect_rows(back)
    two_all = jnp.concatenate(normed_two_all, axis=0)
    ffn_all = jnp.concatenate(ffn_grads, axis=0)
    ffn_parts = []
    for side in range(2):
        d_up_all = jnp.concatenate(d_ups[side], axis=0)
        active_all = jnp.concatenate([pair[side] for pair in actives], axis=0)
        ffn_parts.append((tn(two_all, d_up_all), tn(ffn_all, active_all)))
    ffn_owned = owners(*[jnp.concatenate(part, axis=1) for part in ffn_parts])
    back, gain_two_grad = norm_backward(after, inv_two, gains[1], back_two)
    grad_after = grad + back
    branch_all = jnp.concatenate(spread_rows((live * grad_after).astype(LOW)), axis=0)
    d_mine, d_other, d_taps, d_gain, d_params = mixer_backward(
        meta, params, mine, other, o_a, o_b, nn(branch_all, out_mine), nn(branch_all, out_other),
        states, inverses, taps, gain_out, peers,
    )
    back_one = collect_rows(
        [
            nt(a, mix_mine) + nt(b, mix_other)
            for a, b in zip(split_rows(d_mine, peers), split_rows(d_other, peers))
        ]
    )
    out_parts = [tn(branch_all, mixed_a), tn(branch_all, mixed_b)]
    mix_parts = [tn(normed_all, d_mine), tn(normed_all, d_other)]
    mix_owned = owners(
        *[jnp.concatenate([o, m], axis=1) for o, m in zip(out_parts, mix_parts)]
    )
    back, gain_one_grad = norm_backward(hidden, inv_one, gains[0], back_one)
    return (
        grad_after + back,
        (ffn_owned, mix_owned),
        (jnp.stack([gain_one_grad, gain_two_grad]), d_taps, d_params, d_gain),
    )


def on_device(
    inputs, lengths, norm_gain, w_query, w_key, w_value, w_gate, w_decay, conv_weight, head_rate,
    head_bias, out_gain, w_out, w_updown, w_down, cotangent,
):
    section = lax.axis_index("section")
    layers = lax.axis_size("section")
    first = section == 0
    part = lax.axis_index("tensor")
    rows_here = inputs.shape[1]
    buffer = rows_here * lax.axis_size("tensor")
    ff = w_down.shape[1]
    half = ff // 2
    vals = 2 * KEYS

    def half_mix(h):
        return jnp.concatenate(
            [
                w_query[0][:, h * KEYS : (h + 1) * KEYS],
                w_key[0][:, h * KEYS : (h + 1) * KEYS],
                w_value[0][:, h * vals : (h + 1) * vals],
                w_gate[0][:, h * vals : (h + 1) * vals],
                w_decay[0][:, h * 2 : (h + 1) * 2],
            ],
            axis=1,
        )

    def half_rest(h):
        hidden_part = slice(h * half, (h + 1) * half)
        return jnp.concatenate(
            [
                w_updown[0][:, 0, hidden_part],
                w_updown[0][:, 1, hidden_part],
                w_down[0][hidden_part].T,
                w_out[0][h * vals : (h + 1) * vals].T,
            ],
            axis=1,
        )

    def both_layers(halves):
        keep = jnp.where(first, halves[0], halves[1])
        got = swap_section(jnp.where(first, halves[1], halves[0]))
        return jnp.where(first, keep, got), jnp.where(first, got, keep)

    mix_shards = both_layers((half_mix(0), half_mix(1)))
    rest_shards = both_layers((half_rest(0), half_rest(1)))

    def fetch(layer):
        sides = []
        mix = lax.all_gather(mix_shards[layer], "dp", axis=0, tiled=True)
        rest = lax.all_gather(rest_shards[layer], "dp", axis=0, tiled=True)
        return mix, swap_section(mix), rest, swap_section(rest)

    def arrange(fetched):
        mix, mix_two, rest, rest_two = fetched
        return (
            mix, mix_two,
            rest[:, 3 * half :], rest_two[:, 3 * half :],
            rest[:, : 2 * half], rest_two[:, : 2 * half],
            rest[:, 2 * half : 3 * half], rest_two[:, 2 * half : 3 * half],
        )

    def of_all(array):
        return lax.all_gather(array, "section", axis=0, tiled=True)

    gains_all = of_all(norm_gain)
    sizes = (conv_weight.size, head_rate.size, head_bias.size, out_gain.size)
    packed = of_all(
        jnp.concatenate(
            [conv_weight.reshape(-1), head_rate.reshape(-1), head_bias.reshape(-1), out_gain.reshape(-1)]
        )[None]
    )
    edges = [0]
    for size in sizes:
        edges.append(edges[-1] + size)
    heads = conv_weight.shape[2]
    places = [part * 2 + section, part * 2 + 1 - section]
    smalls = []
    for layer in range(2):
        conv, rate, bias, gain_out = (packed[layer, a:b] for a, b in zip(edges[:-1], edges[1:]))
        conv = conv.reshape(conv_weight.shape[1:])
        taps = jnp.concatenate(
            [lax.dynamic_slice_in_dim(conv, p, 1, 1) for p in places], axis=1
        ).transpose(1, 0, 2)
        scale = jnp.stack([jnp.exp(rate), bias], axis=1)
        params = jnp.concatenate([lax.dynamic_slice_in_dim(scale, p, 1, 0) for p in places], axis=0)
        smalls.append((params, taps, gain_out[None]))

    lengths_row = lax.dynamic_index_in_dim(lengths[:, 0], section, 0, keepdims=False)
    live_all, reset = layout(lengths_row, buffer)
    live = lax.dynamic_slice_in_dim(live_all, part * rows_here, rows_here)[:, None]
    meta = jnp.concatenate([part[None].astype(jnp.int32), reset])

    def own_micro(array):
        return lax.dynamic_index_in_dim(array, section, 0, keepdims=False).astype(F32)

    weights = [arrange(fetch(layer)) for layer in range(2)]
    hidden = own_micro(inputs)
    kept = []
    for layer in range(2):
        result, saved = layer_forward(hidden, weights[layer], gains_all[layer], smalls[layer], meta, live)
        result_low = result.astype(LOW)
        hidden = result_low.astype(F32)
        kept.append(saved)

    def owners(mine, other):
        got = swap_section(other.astype(LOW))
        total = (mine + got.astype(F32)).astype(LOW)
        return lax.psum_scatter(total, "dp", scatter_dimension=0, tiled=True)

    grad = own_micro(cotangent)
    owned, small_grads = [None, None], [None, None]
    for layer in (1, 0):
        grad, owned[layer], small_grads[layer] = layer_backward(
            grad, kept[layer], weights[layer], gains_all[layer], smalls[layer], meta, live, owners
        )
        grad_low = grad.astype(LOW)
        grad = grad_low.astype(F32)

    halves = []
    for kind in range(2):
        keep = jnp.where(first, owned[0][kind], owned[1][kind])
        got = swap_section(jnp.where(first, owned[1][kind], owned[0][kind]))
        halves.append(
            (
                jnp.where(first, keep, got).astype(F32),
                jnp.where(first, got, keep).astype(F32),
            )
        )
    ffn_pair, mix_pair = halves

    def columns(pair, start, size):
        return jnp.concatenate([side[:, start : start + size] for side in pair], axis=1)

    grad_updown = jnp.stack([columns(ffn_pair, 0, half), columns(ffn_pair, half, half)], axis=1)
    grad_down = columns(ffn_pair, 2 * half, half).T
    grad_out = columns(mix_pair, 0, vals).T
    grad_query = columns(mix_pair, vals, KEYS)
    grad_key = columns(mix_pair, vals + KEYS, KEYS)
    grad_value = columns(mix_pair, vals + 2 * KEYS, vals)
    grad_gate = columns(mix_pair, 2 * vals + 2 * KEYS, vals)
    grad_decay = columns(mix_pair, 3 * vals + 2 * KEYS, 2)

    flat = []
    for layer in range(2):
        gain_grads, d_taps, d_params, d_gain = small_grads[layer]
        conv_full = jnp.zeros(conv_weight.shape[1:], F32)
        pair_full = jnp.zeros((heads, 2), F32)
        for side, p in enumerate(places):
            conv_full = lax.dynamic_update_slice_in_dim(conv_full, d_taps[side][:, None, :], p, 1)
            pair_full = lax.dynamic_update_slice_in_dim(pair_full, d_params[side : side + 1, :2], p, 0)
        flat.append(
            jnp.concatenate(
                [
                    conv_full.reshape(-1), pair_full[:, 0], pair_full[:, 1], d_gain.reshape(-1),
                    gain_grads.reshape(-1),
                ]
            )
        )
    summed = lax.psum(jnp.stack(flat), ("section", "dp", "tensor"))
    own = lax.dynamic_index_in_dim(summed, section, 0, keepdims=False)
    pieces = [own[a:b] for a, b in zip(edges[:-1], edges[1:])]
    return (
        result_low[None],
        grad_low[None],
        own[edges[-1] :].reshape(norm_gain.shape),
        grad_query[None],
        grad_key[None],
        grad_value[None],
        grad_gate[None],
        grad_decay[None],
        pieces[0].reshape(conv_weight.shape),
        pieces[1].reshape(head_rate.shape),
        pieces[2].reshape(head_bias.shape),
        pieces[3].reshape(out_gain.shape),
        grad_out[None],
        grad_updown[None],
        grad_down[None],
    )


def solution(mesh):
    in_specs = (
        P(None, ("dp", "tensor"), None),
        P(None, "dp", None),
        P("section", None, None),
        P("section", "dp", "tensor"),
        P("section", "dp", "tensor"),
        P("section", "dp", "tensor"),
        P("section", "dp", "tensor"),
        P("section", "dp", "tensor"),
        P("section", None, None, None),
        P("section", None),
        P("section", None),
        P("section", None),
        P("section", "tensor", "dp"),
        P("section", "dp", None, "tensor"),
        P("section", "tensor", "dp"),
        P(None, ("dp", "tensor"), None),
    )
    out_specs = (
        P("section", ("dp", "tensor"), None),
        P("section", ("dp", "tensor"), None),
        P("section", None, None),
        P("section", "dp", "tensor"),
        P("section", "dp", "tensor"),
        P("section", "dp", "tensor"),
        P("section", "dp", "tensor"),
        P("section", "dp", "tensor"),
        P("section", None, None, None),
        P("section", None),
        P("section", None),
        P("section", None),
        P("section", "tensor", "dp"),
        P("section", "dp", None, "tensor"),
        P("section", "tensor", "dp"),
    )
    return jax.shard_map(
        on_device, mesh=mesh, in_specs=in_specs, out_specs=out_specs, check_vma=False
    )
```

time: 3430 us -> 987 us (0.29)
  other arithmetic: 731 us -> 46.2 us
  waiting for transfers between devices: 1070 us -> 390 us
  matrix products: 865 us -> 228 us
  local copies, waits for them, and re-layouts: 517 us -> 41 us
  Pallas kernels: 0 us -> 195 us
  blocking collectives: 114 us -> 1.81 us
  loops' own time: 68.2 us -> 0 us
  starting transfers between devices: 4.69 us -> 57.8 us
    dot_general x717 -> x120, matrix products: 830 us -> 228 us  [the longest x64 107 us: nt(): lax.dot_general(left, right, (((1,), (1,)), ((), ())), preferred_element_...]
    reduce_scatter x19 -> x4, waiting for transfers between devices: 596 us -> 0.04 us  [owners(): return lax.psum_scatter(total, 'dp', scatter_dimension=0, tiled=True)]
    another operation x70 -> x5, other arithmetic: 493 us -> 1.09 us  [the longest x1 0.8 us: on_device(): summed = lax.psum(jnp.stack(flat), ('section', 'dp', 'tensor'))]
    all_gather x17 -> x4, waiting for transfers between devices: 430 us -> 82.5 us  [the longest x2 44 us: fetch(): rest = lax.all_gather(rest_shards[layer], 'dp', axis=0, tiled=True)]
    squeeze x240 -> x3, local copies, waits for them, and re-layouts: 197 us -> 1.25 us  [the longest x1 1.24 us: half_rest(): w_updown[0][:, 0, hidden_part]]
    pallas_call x0 -> x4, Pallas kernels: none -> 195 us  [the longest x2 125 us: mixer_forward(): pl.pallas_call(mixer_forward_kernel, grid_spec=pltpu.PrefetchScalarGridSp...]
    ppermute x6 -> x60, waiting for transfers between devices: 9.61 us -> 189 us  [the longest x48 187 us: send_by(): lax.ppermute(array, 'tensor', [(i, i ^ offset) for i in range(peers)])]
    dynamic_slice x195 -> x4, local copies, waits for them, and re-layouts: 101 us -> 0.83 us  [the longest x2 0.71 us: on_device(): lax.dynamic_slice_in_dim(scale, p, 1, 0)]
  transfers between devices with their start and end apart: 44 -> 70, of which waited for: 34 -> 28; matrix products, arithmetic and copies ran while one was open for 22% -> 30% of each run, Pallas kernels for 0% -> 20%
where the time goes in v1:
time: 987 us; the launch traced here: 980 us
  waiting for transfers between devices  390 us (40%)
  matrix products  228 us (23%)
  Pallas kernels  195 us (20%)
  starting transfers between devices  57.8 us (6%)
  other arithmetic  46.2 us (5%)
  local copies, waits for them, and re-layouts  41 us (4%)
  between operations  19.4 us (2%)
    ppermute x48, waiting for transfers between devices, send_by(): lax.ppermute(array, 'tensor', [(i, i ^ offset) for i in range(peers)])  187 us
    pallas_call x2, Pallas kernels, mixer_forward(): pl.pallas_call(mixer_forward_kernel, grid_spec=pltpu.PrefetchScalarGridSp...  125 us
    psum x1, waiting for transfers between devices, on_device(): summed = lax.psum(jnp.stack(flat), ('section', 'dp', 'tensor'))  118 us
    dot_general x64, matrix products, nt(): lax.dot_general(left, right, (((1,), (1,)), ((), ())), preferred_element_...  107 us
    dot_general x40, matrix products, nn(): return jnp.dot(left, right, preferred_element_type=F32)  77.9 us
    pallas_call x2, Pallas kernels, mixer_backward(): pl.pallas_call(mixer_backward_kernel, grid_spec=pltpu.PrefetchScalarGridS...  70.3 us
    ppermute x48, starting transfers between devices, send_by(): lax.ppermute(array, 'tensor', [(i, i ^ offset) for i in range(peers)])  56.6 us
    all_gather x2, waiting for transfers between devices, fetch(): rest = lax.all_gather(rest_shards[layer], 'dp', axis=0, tiled=True)  44 us
  transfers between devices with their start and end apart: 70, of which 28 were waited for; matrix products, arithmetic and copies ran while one was open for 30% of the time, Pallas kernels for 20%

profile of v1, /device:TPU:8, one launch (start us, length us, event | category | flops | bytes accessed | tf_op | source)
XLA Modules:
  0.0 980.0 jit_solution(14839211476373936332)
XLA Ops:
  27.1 42.5 %all-gather.8.cloned.1.call-done = bf16[1024,1312]{0,1:T(8,128)(2,1)} async-done(((bf16[256,1312]{0,1:T(8,128)(2,1)}), bf16[1024,1312]{0,1:T(8,128)(2,1)}) %all-gather.8.cloned.1.call-update) | async-done | bytes 2686992 | tf_op jit(solution)/shard_map/all_gather | solution.py:662
  71.6 38.6 %all-gather.6.cloned.1.call-done = bf16[1024,770]{0,1:T(8,128)(2,1)} async-done(((bf16[256,770]{0,1:T(8,128)(2,1)}), bf16[1024,770]{0,1:T(8,128)(2,1)}) %all-gather.6.cloned.1.call-update) | async-done | bytes 1576976 | tf_op jit(solution)/shard_map/all_gather | solution.py:661
  112.8 6.2 fusion.462.mine.edge_a
  119.0 6.1 fusion.461.other.edge_b
  125.1 62.4 %mixer_forward.2 = (bf16[1024,256]{1,0:T(8,128)(2,1)}, bf16[1024,256]{1,0:T(8,128)(2,1)}, f32[1024,256]{1,0:T(8,128)}, f32[1024,256]{1,0:T(8,128)}, bf16[16,2,12...) custom-call(s32[17]{0:T(128)} %pad_add_fusion.meta, f32[2,2]{1,0:T(2,128)} %pad_maximum_fusion.24.params, ...), custom_call_target="tpu_custom_call" | custom-call | tf_op jit(solution)/shard_map/mixer_forward/pallas_call | solution.py:360
  207.0 10.8 %collective-permute-done.8 = bf16[256,1024]{1,0:T(8,128)(2,1)S(1)} collective-permute-done((bf16[256,1024]{1,0:T(8,128)(2,1)}, bf16[256,1024]{1,0:T(8,128)(2,1)S(1)}, u32[]{:S(2)}, u32[]{:S(2)}) %collective-permute-start.8) | collective-permute-done | bytes 524320 | tf_op jit(solution)/shard_map/ppermute | solution.py:463
  227.3 18.5 %collective-permute-done.10 = bf16[256,1024]{1,0:T(8,128)(2,1)S(1)} collective-permute-done((bf16[256,1024]{1,0:T(8,128)(2,1)S(1)}, bf16[256,1024]{1,0:T(8,128)(2,1)S(1)}, u32[]{:S(2)}, u32[]{:S(2)}) %collective-permute-start.10) | collective-permute-done | bytes 524320 | tf_op jit(solution)/shard_map/ppermute | solution.py:463
  270.8 6.3 collective-permute-done.15
  277.1 9.5 collective-permute-done.13
  296.8 8.1 collective-permute-done.18
  304.9 9.8 collective-permute-done.17
  315.1 6.8 fusion.459.mine.edge_a
  321.9 6.3 fusion.458.other.edge_b
  328.2 62.4 %mixer_forward.3 = (bf16[1024,256]{1,0:T(8,128)(2,1)}, bf16[1024,256]{1,0:T(8,128)(2,1)}, f32[1024,256]{1,0:T(8,128)}, f32[1024,256]{1,0:T(8,128)}, bf16[16,2,12...) custom-call(s32[17]{0:T(128)} %pad_add_fusion.meta, f32[2,2]{1,0:T(2,128)} %pad_maximum_fusion.26.params, ...), custom_call_target="tpu_custom_call" | custom-call | tf_op jit(solution)/shard_map/mixer_forward/pallas_call | solution.py:360
  404.2 5.0 collective-permute-done.23
  410.0 10.6 %collective-permute-done.22 = bf16[256,1024]{1,0:T(8,128)(2,1)S(1)} collective-permute-done((bf16[256,1024]{1,0:T(8,128)(2,1)S(1)}, bf16[256,1024]{1,0:T(8,128)(2,1)S(1)}, u32[]{:S(2)}, u32[]{:S(2)}) %collective-permute-start.22) | collective-permute-done | bytes 524320 | tf_op jit(solution)/shard_map/ppermute | solution.py:463
  430.2 22.7 %collective-permute-done.28 = bf16[256,1024]{1,0:T(8,128)(2,1)S(1)} collective-permute-done((bf16[256,1024]{1,0:T(8,128)(2,1)S(1)}, bf16[256,1024]{1,0:T(8,128)(2,1)S(1)}, u32[]{:S(2)}, u32[]{:S(2)}) %collective-permute-start.28) | collective-permute-done | bytes 524320 | tf_op jit(solution)/shard_map/ppermute | solution.py:463
  462.8 4.8 collective-permute-done.24
  501.8 9.1 collective-permute-done.38
  510.9 8.0 collective-permute-done.37
  523.8 35.5 %mixer_backward.2 = (bf16[1024,770]{1,0:T(8,128)(2,1)}, bf16[1024,770]{1,0:T(8,128)(2,1)}, f32[2,4,512]{2,1,0:T(4,128)}, f32[1,256]{1,0:T(1,128)}, f32[2,128]{1,0:T(2,128)}) custom-call(s32[17]{0:T(128)} %pad_add_fusion.meta, f32[2,2]{1,0:T(2,128)} %pad_maximum_fusion.26.params, f32[1024,770]{1,0:T(8,128)} %fusion.459.mine.edge_a, ...), custom_call_target="tpu_custom_call" | custom-call | tf_op jit(solution)/shard_map/mixer_backward/pallas_call | solution.py:416
  591.5 5.9 fusion.457
  614.5 14.0 %collective-permute-done.42 = bf16[256,1024]{1,0:T(8,128)(2,1)} collective-permute-done((bf16[256,1024]{1,0:T(8,128)(2,1)}, bf16[256,1024]{1,0:T(8,128)(2,1)}, u32[]{:S(2)}, u32[]{:S(2)}) %collective-permute-start.42) | collective-permute-done | bytes 524320 | tf_op jit(solution)/shard_map/ppermute | solution.py:463
  658.2 4.1 fusion.1
  681.7 5.4 collective-permute-done.50
  687.2 9.2 collective-permute-done.49
  701.2 34.8 %mixer_backward.3 = (bf16[1024,770]{1,0:T(8,128)(2,1)}, bf16[1024,770]{1,0:T(8,128)(2,1)}, f32[2,4,512]{2,1,0:T(4,128)}, f32[1,256]{1,0:T(1,128)}, f32[2,128]{1,0:T(2,128)}) custom-call(s32[17]{0:T(128)} %pad_add_fusion.meta, f32[2,2]{1,0:T(2,128)} %pad_maximum_fusion.24.params, f32[1024,770]{1,0:T(8,128)} %fusion.462.mine.edge_a, ...), custom_call_target="tpu_custom_call" | custom-call | tf_op jit(solution)/shard_map/mixer_backward/pallas_call | solution.py:416
  744.1 3.8 fusion
  762.4 6.6 collective-permute-done.52
  777.0 5.1 fusion.3
  812.6 16.8 %collective-permute-done.27 = bf16[256,1024]{1,0:T(8,128)(2,1)} collective-permute-done((bf16[256,1024]{1,0:T(8,128)(2,1)S(1)}, bf16[256,1024]{1,0:T(8,128)(2,1)}, u32[]{:S(2)}, u32[]{:S(2)}) %collective-permute-start.27) | collective-permute-done | bytes 524320 | tf_op jit(solution)/shard_map/ppermute | solution.py:463
  837.6 118.2 %all-reduce.4.cloned.1.call-done = f32[2,18704]{1,0:T(2,128)} async-done(((f32[2,18704]{1,0:T(2,128)}), f32[2,18704]{1,0:T(2,128)}) %all-reduce.4.cloned.1.call-update) | async-done | bytes 149648 | tf_op jit(solution)/shard_map/psum | solution.py:771
  (722 shorter events, 347.0 us)
Async XLA Ops:
  8.0 61.6 %all-gather.8.cloned.1.call-start = ((), (), s32[]{:S(2)}) async-start(), calls=%async_computation.5 | async-start | bytes 3358720 | tf_op jit(solution)/shard_map/all_gather | solution.py:662
  15.3 55.1 %all-reduce.6.cloned.1.call-start = ((), (), s32[]{:S(2)}) async-start(), calls=%async_computation.13 | async-start | bytes 270336
  19.2 91.0 %all-gather.6.cloned.1.call-start = ((), (), s32[]{:S(2)}) async-start(), calls=%async_computation.4 | async-start | bytes 1986560 | tf_op jit(solution)/shard_map/all_gather | solution.py:661
  20.2 180.6 %all-gather.10.cloned.1.call-start = ((), (), s32[]{:S(2)}) async-start(), calls=%async_computation.6 | async-start | bytes 1986560 | tf_op jit(solution)/shard_map/all_gather | solution.py:661
  21.0 181.4 %all-gather.12.cloned.1.call-start = ((), (), s32[]{:S(2)}) async-start(), calls=%async_computation.7 | async-start | bytes 3358720 | tf_op jit(solution)/shard_map/all_gather | solution.py:662
  23.3 89.5 %collective-permute-start.2 = (bf16[256,1024]{1,0:T(8,128)(2,1)S(1)}, bf16[256,1024]{1,0:T(8,128)(2,1)S(1)}, u32[]{:S(2)}, u32[]{:S(2)}) collective-permute-start(bf16[256,1024]{1,0:T(8,128)(2,1)S(1)} %fusion.141), channel_id=1, source_target_pairs={{0,3},{1,2},{2,1},{3,0},{4,7},{5,6},{6,5},{7,4},{8,11},{9,10},{10,... | collective-permute-start | bytes 1572872 | tf_op jit(solution)/shard_map/ppermute | solution.py:463
  25.8 87.0 %collective-permute-start.1 = (bf16[256,1024]{1,0:T(8,128)(2,1)S(1)}, bf16[256,1024]{1,0:T(8,128)(2,1)}, u32[]{:S(2)}, u32[]{:S(2)}) collective-permute-start(bf16[256,1024]{1,0:T(8,128)(2,1)S(1)} %fusion.141), channel_id=1, source_target_pairs={{0,2},{1,3},{2,0},{3,1},{4,6},{5,7},{6,4},{7,5},{8,10},{9,11},{10,... | collective-permute-start | bytes 1572872 | tf_op jit(solution)/shard_map/ppermute | solution.py:463
  26.3 86.5 %collective-permute-start = (bf16[256,1024]{1,0:T(8,128)(2,1)S(1)}, bf16[256,1024]{1,0:T(8,128)(2,1)}, u32[]{:S(2)}, u32[]{:S(2)}) collective-permute-start(bf16[256,1024]{1,0:T(8,128)(2,1)S(1)} %fusion.141), channel_id=1, source_target_pairs={{0,1},{1,0},{2,3},{3,2},{4,5},{5,4},{6,7},{7,6},{8,9},{9,8},{10,11... | collective-permute-start | bytes 1572872 | tf_op jit(solution)/shard_map/ppermute | solution.py:463
  69.6 117.9 %collective-permute-start.6 = (bf16[1024,1312]{0,1:T(8,128)(2,1)}, bf16[1024,1312]{0,1:T(8,128)(2,1)}, u32[]{:S(2)}, u32[]{:S(2)}) collective-permute-start(bf16[1024,1312]{0,1:T(8,128)(2,1)} %all-gather.8.cloned.1.call-done), channel_id=1, source_target_pairs={{0,16},{16,0},{1,17},{17,1},{2,18},{18,2},{3,19},{19,3},{4,20},{20... | collective-permute-start | bytes 8060936 | tf_op jit(solution)/shard_map/ppermute | solution.py:458
  71.4 761.1 %reduce-scatter.11.cloned.1.call-start = ((), (), s32[]{:S(2)}) async-start(), calls=%async_computation.12 | async-start | bytes 2703360 | tf_op jit(solution)/shard_map/reduce_scatter | solution.py:720
  200.8 121.1 %collective-permute-start.19 = (bf16[1024,770]{0,1:T(8,128)(2,1)}, bf16[1024,770]{0,1:T(8,128)(2,1)S(1)}, u32[]{:S(2)}, u32[]{:S(2)}) collective-permute-start(bf16[1024,770]{0,1:T(8,128)(2,1)} %all-gather.10.cloned.1.call-done), channel_id=1, source_target_pairs={{0,16},{16,0},{1,17},{17,1},{2,18},{18,2},{3,19},{19,3},{4,20},{20... | collective-permute-start | bytes 4730888 | tf_op jit(solution)/shard_map/ppermute | solution.py:458
  202.4 188.3 %collective-permute-start.20 = (bf16[1024,1312]{0,1:T(8,128)(2,1)}, bf16[1024,1312]{0,1:T(8,128)(2,1)}, u32[]{:S(2)}, u32[]{:S(2)}) collective-permute-start(bf16[1024,1312]{0,1:T(8,128)(2,1)} %all-gather.12.cloned.1.call-done), channel_id=1, source_target_pairs={{0,16},{16,0},{1,17},{17,1},{2,18},{18,2},{3,19},{19,3},{4,20},{20... | collective-permute-start | bytes 8060936 | tf_op jit(solution)/shard_map/ppermute | solution.py:458
  221.2 33.9 %collective-permute-start.14 = (bf16[256,1024]{1,0:T(8,128)(2,1)S(1)}, bf16[256,1024]{1,0:T(8,128)(2,1)S(1)}, u32[]{:S(2)}, u32[]{:S(2)}) collective-permute-start(bf16[256,1024]{1,0:T(8,128)(2,1)S(1)} %multiply_convert_fusion.3), channel_id=1, source_target_pairs={{0,3},{1,2},{2,1},{3,0},{4,7},{5,6},{6,5},{7,4},{8,11},{9,10},{10,... | collective-permute-start | bytes 1572872 | tf_op jit(solution)/shard_map/ppermute | solution.py:463
  222.0 28.4 %collective-permute-start.12 = (bf16[256,1024]{1,0:T(8,128)(2,1)S(1)}, bf16[256,1024]{1,0:T(8,128)(2,1)S(1)}, u32[]{:S(2)}, u32[]{:S(2)}) collective-permute-start(bf16[256,1024]{1,0:T(8,128)(2,1)S(1)} %multiply_convert_fusion.3), channel_id=1, source_target_pairs={{0,2},{1,3},{2,0},{3,1},{4,6},{5,7},{6,4},{7,5},{8,10},{9,11},{10,... | collective-permute-start | bytes 1572872 | tf_op jit(solution)/shard_map/ppermute | solution.py:463
  400.6 56.1 %collective-permute-start.34 = (bf16[256,1024]{1,0:T(8,128)(2,1)S(1)}, bf16[256,1024]{1,0:T(8,128)(2,1)S(1)}, u32[]{:S(2)}, u32[]{:S(2)}) collective-permute-start(bf16[256,1024]{1,0:T(8,128)(2,1)S(1)} %fusion.132), channel_id=1, source_target_pairs={{0,3},{1,2},{2,1},{3,0},{4,7},{5,6},{6,5},{7,4},{8,11},{9,10},{10,... | collective-permute-start | bytes 1572872 | tf_op jit(solution)/shard_map/ppermute | solution.py:463
  401.7 77.1 %collective-permute-start.32 = (bf16[256,1024]{1,0:T(8,128)(2,1)S(1)}, bf16[256,1024]{1,0:T(8,128)(2,1)S(1)}, u32[]{:S(2)}, u32[]{:S(2)}) collective-permute-start(bf16[256,1024]{1,0:T(8,128)(2,1)S(1)} %fusion.132), channel_id=1, source_target_pairs={{0,2},{1,3},{2,0},{3,1},{4,6},{5,7},{6,4},{7,5},{8,10},{9,11},{10,... | collective-permute-start | bytes 1572872 | tf_op jit(solution)/shard_map/ppermute | solution.py:463
  409.2 60.9 %collective-permute-start.30 = (bf16[256,1024]{1,0:T(8,128)(2,1)S(1)}, bf16[256,1024]{1,0:T(8,128)(2,1)S(1)}, u32[]{:S(2)}, u32[]{:S(2)}) collective-permute-start(bf16[256,1024]{1,0:T(8,128)(2,1)S(1)} %fusion.132), channel_id=1, source_target_pairs={{0,1},{1,0},{2,3},{3,2},{4,5},{5,4},{6,7},{7,6},{8,9},{9,8},{10,11... | collective-permute-start | bytes 1572872 | tf_op jit(solution)/shard_map/ppermute | solution.py:463
  421.4 31.5 %collective-permute-start.28 = (bf16[256,1024]{1,0:T(8,128)(2,1)S(1)}, bf16[256,1024]{1,0:T(8,128)(2,1)S(1)}, u32[]{:S(2)}, u32[]{:S(2)}) collective-permute-start(bf16[256,1024]{1,0:T(8,128)(2,1)S(1)} %multiply_convert_fusion.2), channel_id=1, source_target_pairs={{0,3},{1,2},{2,1},{3,0},{4,7},{5,6},{6,5},{7,4},{8,11},{9,10},{10,... | collective-permute-start | bytes 1572872 | tf_op jit(solution)/shard_map/ppermute | solution.py:463
  422.5 53.8 %collective-permute-start.26 = (bf16[256,1024]{1,0:T(8,128)(2,1)S(1)}, bf16[256,1024]{1,0:T(8,128)(2,1)S(1)}, u32[]{:S(2)}, u32[]{:S(2)}) collective-permute-start(bf16[256,1024]{1,0:T(8,128)(2,1)S(1)} %multiply_convert_fusion.2), channel_id=1, source_target_pairs={{0,2},{1,3},{2,0},{3,1},{4,6},{5,7},{6,4},{7,5},{8,10},{9,11},{10,... | collective-permute-start | bytes 1572872 | tf_op jit(solution)/shard_map/ppermute | solution.py:463
  461.3 29.5 %collective-permute-start.35 = (bf16[256,1024]{1,0:T(8,128)(2,1)S(1)}, bf16[256,1024]{1,0:T(8,128)(2,1)S(1)}, u32[]{:S(2)}, u32[]{:S(2)}) collective-permute-start(bf16[256,1024]{1,0:T(8,128)(2,1)S(1)} %fusion.108), channel_id=1, source_target_pairs={{0,3},{1,2},{2,1},{3,0},{4,7},{5,6},{6,5},{7,4},{8,11},{9,10},{10,... | collective-permute-start | bytes 1572872 | tf_op jit(solution)/shard_map/ppermute | solution.py:463
  488.7 169.5 %collective-permute-start.58 = (bf16[1024,1056]{0,1:T(8,128)(2,1)}, bf16[1024,1056]{0,1:T(8,128)(2,1)}, u32[]{:S(2)}, u32[]{:S(2)}) collective-permute-start(bf16[1024,1056]{0,1:T(8,128)(2,1)} %pad_maximum_fusion.1), channel_id=1, source_target_pairs={{0,16},{16,0},{1,17},{17,1},{2,18},{18,2},{3,19},{19,3},{4,20},{20... | collective-permute-start | bytes 6488072 | tf_op jit(solution)/shard_map/ppermute | solution.py:458
  567.3 30.2 %collective-permute-start.41 = (bf16[256,1024]{1,0:T(8,128)(2,1)}, bf16[256,1024]{1,0:T(8,128)(2,1)}, u32[]{:S(2)}, u32[]{:S(2)}) collective-permute-start(bf16[256,1024]{1,0:T(8,128)(2,1)} %fusion.111), channel_id=1, source_target_pairs={{0,3},{1,2},{2,1},{3,0},{4,7},{5,6},{6,5},{7,4},{8,11},{9,10},{10,... | collective-permute-start | bytes 1572872 | tf_op jit(solution)/shard_map/ppermute | solution.py:463
  581.2 195.8 %collective-permute-start.55 = (bf16[1024,1026]{0,1:T(8,128)(2,1)}, bf16[1024,1026]{0,1:T(8,128)(2,1)}, u32[]{:S(2)}, u32[]{:S(2)}) collective-permute-start(bf16[1024,1026]{0,1:T(8,128)(2,1)} %pad_maximum_fusion.3), channel_id=1, source_target_pairs={{0,16},{16,0},{1,17},{17,1},{2,18},{18,2},{3,19},{19,3},{4,20},{20... | collective-permute-start | bytes 6303752 | tf_op jit(solution)/shard_map/ppermute | solution.py:458
  601.8 41.7 %collective-permute-start.46 = (bf16[256,1024]{1,0:T(8,128)(2,1)}, bf16[256,1024]{1,0:T(8,128)(2,1)}, u32[]{:S(2)}, u32[]{:S(2)}) collective-permute-start(bf16[256,1024]{1,0:T(8,128)(2,1)} %get-tuple-element.129), channel_id=1, source_target_pairs={{0,3},{1,2},{2,1},{3,0},{4,7},{5,6},{6,5},{7,4},{8,11},{9,10},{10,... | collective-permute-start | bytes 1572872 | tf_op jit(solution)/shard_map/ppermute | solution.py:463
  603.1 32.6 %collective-permute-start.44 = (bf16[256,1024]{1,0:T(8,128)(2,1)}, bf16[256,1024]{1,0:T(8,128)(2,1)}, u32[]{:S(2)}, u32[]{:S(2)}) collective-permute-start(bf16[256,1024]{1,0:T(8,128)(2,1)} %get-tuple-element.129), channel_id=1, source_target_pairs={{0,2},{1,3},{2,0},{3,1},{4,6},{5,7},{6,4},{7,5},{8,10},{9,11},{10,... | collective-permute-start | bytes 1572872 | tf_op jit(solution)/shard_map/ppermute | solution.py:463
  635.1 30.6 %collective-permute-start.43 = (bf16[256,1024]{1,0:T(8,128)(2,1)}, bf16[256,1024]{1,0:T(8,128)(2,1)}, u32[]{:S(2)}, u32[]{:S(2)}) collective-permute-start(bf16[256,1024]{1,0:T(8,128)(2,1)} %fusion.112), channel_id=1, source_target_pairs={{0,1},{1,0},{2,3},{3,2},{4,5},{5,4},{6,7},{7,6},{8,9},{9,8},{10,11... | collective-permute-start | bytes 1572872 | tf_op jit(solution)/shard_map/ppermute | solution.py:463
  662.4 170.1 %reduce-scatter.9.cloned.1.call-start = ((), (), s32[]{:S(2)}) async-start(), calls=%async_computation.11 | async-start | bytes 2703360 | tf_op jit(solution)/shard_map/reduce_scatter | solution.py:720
  665.7 78.4 %collective-permute-start.57 = (bf16[1024,1056]{0,1:T(8,128)(2,1)}, bf16[1024,1056]{0,1:T(8,128)(2,1)}, u32[]{:S(2)}, u32[]{:S(2)}) collective-permute-start(bf16[1024,1056]{0,1:T(8,128)(2,1)} %pad_maximum_fusion), channel_id=1, source_target_pairs={{0,16},{16,0},{1,17},{17,1},{2,18},{18,2},{3,19},{19,3},{4,20},{20... | collective-permute-start | bytes 6488072 | tf_op jit(solution)/shard_map/ppermute | solution.py:458
  748.0 207.9 %all-reduce.4.cloned.1.call-start = ((), (), s32[]{:S(2)}) async-start(), calls=%async_computation.8 | async-start | bytes 301056 | tf_op jit(solution)/shard_map/psum | solution.py:771
  776.9 186.2 %reduce-scatter.7.cloned.1.call-start = ((), (), s32[]{:S(2)}) async-start(), calls=%async_computation.10 | async-start | bytes 2641920 | tf_op jit(solution)/shard_map/reduce_scatter | solution.py:720
  782.1 181.0 %reduce-scatter.5.cloned.1.call-start = ((), (), s32[]{:S(2)}) async-start(), calls=%async_computation.9 | async-start | bytes 2641920 | tf_op jit(solution)/shard_map/reduce_scatter | solution.py:720
  834.3 127.3 %collective-permute-start.59 = (bf16[256,1056]{0,1:T(8,128)(2,1)}, bf16[256,1056]{0,1:T(8,128)(2,1)}, u32[]{:S(2)}, u32[]{:S(2)}) collective-permute-start(bf16[256,1056]{0,1:T(8,128)(2,1)} %broadcast_select_fusion.4), channel_id=1, source_target_pairs={{0,16},{16,0},{1,17},{17,1},{2,18},{18,2},{3,19},{19,3},{4,20},{20... | collective-permute-start | bytes 1622024 | tf_op jit(solution)/shard_map/ppermute | solution.py:458
  (199 other events, 2593.2 us)
Sparse Core Ops, SparseCore 0:
  15.4 54.1 all-gather.7
  71.7 38.3 all-gather.5
  111.7 36.1 all-gather.9
  149.9 52.3 all-gather.11
  662.4 42.2 reduce-scatter.10
  748.1 43.3 reduce-scatter.8
  793.7 44.3 reduce-scatter.6
  840.5 43.9 reduce-scatter.4
Sparse Core Ops, SparseCore 1:
  19.3 19.0 all-reduce.5
  777.0 178.8 all-reduce.3

commit v2 on v1

--- a/solution.py
+++ b/solution.py
@@ -54,17 +54,18 @@
     return jnp.sum(array, axis=1, keepdims=True)
 
 
-def unit_lower_inverse(below, row, col):
+def unit_lower_inverses(belows, row, col):
     ones = jnp.where(row == col, 1.0, 0.0)
-    inverse = ones - jnp.where((row // 2 == col // 2), below, 0.0)
+    near = row // 2 == col // 2
+    inverses = [ones - jnp.where(near, below, 0.0) for below in belows]
     half = 2
     while half < BLOCK:
         span = 2 * half
         part = (row // span == col // span) & (row % span >= half) & (col % span < half)
-        piece = jnp.where(part, below, 0.0)
-        inverse = inverse - mm_split(inverse, mm_split(piece, inverse))
+        pieces = [mm_split(jnp.where(part, b, 0.0), i) for b, i in zip(belows, inverses)]
+        inverses = [i - mm_split(i, p) for p, i in zip(pieces, inverses)]
         half = span
-    return inverse
+    return inverses
 
 
 def convolve(own, before, taps):
@@ -96,7 +97,10 @@
     return array * inv, inv * scale
 
 
-def mixer_forward_kernel(meta, params, mine, other, taps, gain, mixed_a, mixed_b, o_a, o_b, states, inverses, state, carry):
+def mixer_forward_kernel(
+    meta, params, normed, mix_mine, mix_other, taps, gain,
+    mine, other, mixed_a, mixed_b, o_a, o_b, states, inverses, branch, state, carry,
+):
     step = pl.program_id(0)
     groups = mine.shape[0] // BLOCK
     row, col = grid_of(BLOCK)
@@ -106,6 +110,8 @@
         state[...] = jnp.zeros_like(state)
         carry[...] = jnp.zeros_like(carry)
 
+    mine[...] = mm(normed[...], mix_mine[:, : 7 * KEYS])
+    other[...] = mm(normed[...], mix_other[:, : 7 * KEYS])
     sources = (mine, other)
     outs = (mixed_a, mixed_b)
     os = (o_a, o_b)
@@ -133,15 +139,12 @@
             last = cumlog[BLOCK - 1 :]
             both = mm_nt(jnp.concatenate([keys, query], axis=0), keys)
             below = jnp.where(row > col, strength * ratio * both[:BLOCK], 0.0)
-            inverse = unit_lower_inverse(below, row, col)
-            inverses[block, head] = inverse
-            weight = mm(inverse, (strength * gamma) * keys).astype(LOW)
-            update = mm(inverse, strength * values)
             scores = (both[BLOCK:] * ratio).astype(LOW)
             tail = (keys * jnp.exp(last - cumlog)).astype(LOW)
             prepared[block, head] = (
-                weight,
-                update,
+                below,
+                ((strength * gamma) * keys).astype(LOW),
+                (strength * values).astype(LOW),
                 scores,
                 tail,
                 (query * gamma).astype(LOW),
@@ -149,6 +152,14 @@
                 keep,
             )
         carry[head] = source[pl.ds(groups * BLOCK - 8, 8), 0 : 4 * KEYS]
+    order = list(prepared)
+    solved = unit_lower_inverses([prepared[place][0] for place in order], row, col)
+    for place, inverse in zip(order, solved):
+        inverse_low = inverse.astype(LOW)
+        inverses[place[0], place[1]] = inverse_low
+        _, scaled_keys, scaled_values, *rest = prepared[place]
+        weight = mm(inverse_low, scaled_keys).astype(LOW)
+        prepared[place] = (weight, mm(inverse_low, scaled_values), *rest)
     current = [state[0], state[1]]
     for block in range(groups):
         for head in range(2):
@@ -167,11 +178,16 @@
             outs[head][rows, :] = mixed.astype(LOW)
     state[0] = current[0]
     state[1] = current[1]
+    branch[...] = (
+        mm_nt(mixed_a[...], mix_mine[:, 7 * KEYS :])
+        + mm_nt(mixed_b[...], mix_other[:, 7 * KEYS :])
+    ).astype(LOW)
 
 
 def mixer_backward_kernel(
-    meta, params, mine, other, edge_a, edge_b, o_a, o_b, dm_a, dm_b, states, inverses, taps, gain,
-    d_mine, d_other, d_taps, d_gain, d_params, state_grad, carry,
+    meta, params, mine, other, edge_a, edge_b, o_a, o_b, normed_in, d_branch, states, inverses,
+    mix_mine, mix_other, taps, gain,
+    d_mine, d_other, d_taps, d_gain, d_params, inward, d_norm_gain, state_grad, carry, dm_a, dm_b,
 ):
     step = pl.program_id(0)
     seq = pl.num_programs(0) - 1 - step
@@ -185,6 +201,10 @@
         d_taps[...] = jnp.zeros_like(d_taps)
         d_gain[...] = jnp.zeros_like(d_gain)
         d_params[...] = jnp.zeros_like(d_params)
+        d_norm_gain[...] = jnp.zeros_like(d_norm_gain)
+
+    dm_a[...] = mm(d_branch[...], mix_mine[:, 7 * KEYS :])
+    dm_b[...] = mm(d_branch[...], mix_other[:, 7 * KEYS :])
 
     sources = (mine, other)
     edges = (edge_a, edge_b)
@@ -222,7 +242,7 @@
             both = mm_nt(jnp.concatenate([keys, query], axis=0), keys)
             near = jnp.where(row > col, ratio * both[:BLOCK], 0.0)
             scores = both[BLOCK:] * ratio
-            inverse = inverses[block, head].astype(LOW)
+            inverse = inverses[block, head]
             held = states[block, head]
             weight = mm(inverse, (strength * gamma) * keys).astype(LOW)
             key_state = mm(keys, held)
@@ -311,7 +331,10 @@
             rate_sum = rate_sum + jnp.sum(d_log * k["log_decay"], axis=0, keepdims=True)
             bias_sum = bias_sum + jnp.sum(d_decay, axis=0, keepdims=True)
             d_write = d_strength * strength * (1.0 - strength)
-            dsts[head][rows, 6 * KEYS : 6 * KEYS + 2] = jnp.concatenate([d_decay, d_write], axis=1).astype(LOW)
+            lanes = lax.broadcasted_iota(jnp.int32, (BLOCK, KEYS), 1)
+            dsts[head][rows, 6 * KEYS : 7 * KEYS] = (
+                jnp.where(lanes == 0, d_decay, 0.0) + jnp.where(lanes == 1, d_write, 0.0)
+            ).astype(LOW)
             d_query = d_query * KEYS ** (-0.5)
             unit_q = k["query_unit"]
             d_active = jnp.concatenate(
@@ -341,11 +364,80 @@
         d_params[head : head + 1, :] += jnp.where(lane == 0, rate_sum, 0.0) + jnp.where(
             lane == 1, bias_sum, 0.0
         )
-
-
-def mixer_forward(meta, params, mine, other, taps, gain, parts):
-    rows = mine.shape[0]
-    wide = mine.shape[1]
+    back = mm_nt(d_mine[...], mix_mine[:, : 7 * KEYS]) + mm_nt(d_other[...], mix_other[:, : 7 * KEYS])
+    inward[...] = back.astype(LOW)
+    d_norm_gain[...] += jnp.sum(back * normed_in[...].astype(F32), axis=0, keepdims=True)
+
+
+def ffn_forward_kernel(rows, mine, other, u_a, u_b, act_a, act_b, out):
+    half = mine.shape[1] // 3
+    total = None
+    for weight, u_out, act in ((mine, u_a, act_a), (other, u_b, act_b)):
+        u = mm(rows[...], weight[:, : 2 * half])
+        u_out[...] = u
+        gate = u[:, :half]
+        active = (gate * jax.nn.sigmoid(gate) * u[:, half:]).astype(LOW)
+        act[...] = active
+        piece = mm_nt(active, weight[:, 2 * half :])
+        total = piece if total is None else total + piece
+    out[...] = total.astype(LOW)
+
+
+def ffn_backward_kernel(grad, u_a, u_b, mine, other, d_a, d_b, out):
+    half = mine.shape[1] // 3
+    total = None
+    for weight, u_in, d_out in ((mine, u_a, d_a), (other, u_b, d_b)):
+        d_active = mm(grad[...], weight[:, 2 * half :])
+        gate, lift = u_in[:, :half], u_in[:, half:]
+        sig = jax.nn.sigmoid(gate)
+        d_gate = (d_active * lift * (sig * (1.0 + gate * (1.0 - sig)))).astype(LOW)
+        d_lift = (d_active * (gate * sig)).astype(LOW)
+        d_out[:, :half] = d_gate
+        d_out[:, half:] = d_lift
+        piece = mm_nt(d_gate, weight[:, :half]) + mm_nt(d_lift, weight[:, half : 2 * half])
+        total = piece if total is None else total + piece
+    out[...] = total.astype(LOW)
+
+
+def ffn_forward(rows, weights):
+    count, width = rows.shape
+    half = weights[0].shape[1] // 3
+    return pl.pallas_call(
+        ffn_forward_kernel,
+        out_shape=[
+            jax.ShapeDtypeStruct((count, 2 * half), F32),
+            jax.ShapeDtypeStruct((count, 2 * half), F32),
+            jax.ShapeDtypeStruct((count, half), LOW),
+            jax.ShapeDtypeStruct((count, half), LOW),
+            jax.ShapeDtypeStruct((count, width), LOW),
+        ],
+        compiler_params=pltpu.CompilerParams(vmem_limit_bytes=VMEM_LIMIT),
+        name="ffn_forward",
+    )(rows, *weights)
+
+
+def ffn_backward(grad, pair, weights):
+    count, width = grad.shape
+    half = weights[0].shape[1] // 3
+    return pl.pallas_call(
+        ffn_backward_kernel,
+        out_shape=[
+            jax.ShapeDtypeStruct((count, 2 * half), LOW),
+            jax.ShapeDtypeStruct((count, 2 * half), LOW),
+            jax.ShapeDtypeStruct((count, width), LOW),
+        ],
+        compiler_params=pltpu.CompilerParams(vmem_limit_bytes=VMEM_LIMIT),
+        name="ffn_backward",
+    )(grad, *pair, *weights)
+
+
+def whole(array):
+    return pl.BlockSpec(array.shape, lambda step, meta: (0,) * array.ndim)
+
+
+def mixer_forward(meta, params, normed, weights, taps, gain, parts):
+    rows, width = normed.shape
+    wide = 7 * KEYS
     group = rows // parts
     per = group // BLOCK
 
@@ -357,6 +449,8 @@
 
     vals = 2 * KEYS
     row_spec = pl.BlockSpec((group, vals), place)
+    wide_spec = pl.BlockSpec((group, wide), place)
+    full_spec = pl.BlockSpec((group, width), place)
     return pl.pallas_call(
         mixer_forward_kernel,
         grid_spec=pltpu.PrefetchScalarGridSpec(
@@ -364,36 +458,43 @@
             grid=(parts,),
             in_specs=[
                 pl.BlockSpec(memory_space=pltpu.SMEM),
-                pl.BlockSpec((group, wide), place),
-                pl.BlockSpec((group, wide), place),
-                pl.BlockSpec((2, 4, 4 * KEYS), lambda step, meta: (0, 0, 0)),
-                pl.BlockSpec((1, vals), lambda step, meta: (0, 0)),
+                full_spec,
+                *[whole(weight) for weight in weights],
+                whole(taps),
+                whole(gain),
             ],
             out_specs=[
+                wide_spec,
+                wide_spec,
                 row_spec,
                 row_spec,
                 row_spec,
                 row_spec,
                 pl.BlockSpec((per, 2, KEYS, vals), stacked),
                 pl.BlockSpec((per, 2, BLOCK, BLOCK), stacked),
+                full_spec,
             ],
             scratch_shapes=[pltpu.VMEM((2, KEYS, vals), F32), pltpu.VMEM((2, 8, 4 * KEYS), F32)],
         ),
         out_shape=[
+            jax.ShapeDtypeStruct((rows, wide), F32),
+            jax.ShapeDtypeStruct((rows, wide), F32),
             jax.ShapeDtypeStruct((rows, vals), LOW),
             jax.ShapeDtypeStruct((rows, vals), LOW),
             jax.ShapeDtypeStruct((rows, vals), F32),
             jax.ShapeDtypeStruct((rows, vals), F32),
             jax.ShapeDtypeStruct((rows // BLOCK, 2, KEYS, vals), LOW),
-            jax.ShapeDtypeStruct((rows // BLOCK, 2, BLOCK, BLOCK), F32),
+            jax.ShapeDtypeStruct((rows // BLOCK, 2, BLOCK, BLOCK), LOW),
+            jax.ShapeDtypeStruct((rows, width), LOW),
         ],
         compiler_params=pltpu.CompilerParams(vmem_limit_bytes=VMEM_LIMIT),
         name="mixer_forward",
-    )(meta, params, mine, other, taps, gain)
-
-
-def mixer_backward(meta, params, mine, other, o_a, o_b, dm_a, dm_b, states, inverses, taps, gain, parts):
-    rows = mine.shape[0]
+    )(meta, params, normed, *weights, taps, gain)
+
+
+def mixer_backward(meta, params, saved, normed, d_branch, weights, taps, gain, parts):
+    mine, other, o_a, o_b, states, inverses = saved
+    rows, width = normed.shape
     wide = mine.shape[1]
     group = rows // parts
     per = group // BLOCK
@@ -410,9 +511,8 @@
     vals = 2 * KEYS
     row_spec = pl.BlockSpec((group, vals), place)
     wide_spec = pl.BlockSpec((group, wide), place)
+    full_spec = pl.BlockSpec((group, width), place)
     edge_spec = pl.BlockSpec((8, wide), edge)
-    taps_spec = pl.BlockSpec((2, 4, 4 * KEYS), lambda step, meta: (0, 0, 0))
-    gain_spec = pl.BlockSpec((1, vals), lambda step, meta: (0, 0))
     return pl.pallas_call(
         mixer_backward_kernel,
         grid_spec=pltpu.PrefetchScalarGridSpec(
@@ -426,32 +526,45 @@
                 edge_spec,
                 row_spec,
                 row_spec,
-                row_spec,
-                row_spec,
+                full_spec,
+                full_spec,
                 pl.BlockSpec((per, 2, KEYS, vals), stacked),
                 pl.BlockSpec((per, 2, BLOCK, BLOCK), stacked),
-                taps_spec,
-                gain_spec,
+                *[whole(weight) for weight in weights],
+                whole(taps),
+                whole(gain),
             ],
             out_specs=[
                 wide_spec,
                 wide_spec,
-                taps_spec,
-                gain_spec,
+                whole(taps),
+                whole(gain),
                 pl.BlockSpec((2, KEYS), lambda step, meta: (0, 0)),
+                full_spec,
+                pl.BlockSpec((1, width), lambda step, meta: (0, 0)),
             ],
-            scratch_shapes=[pltpu.VMEM((2, KEYS, vals), F32), pltpu.VMEM((2, 8, 4 * KEYS), F32)],
+            scratch_shapes=[
+                pltpu.VMEM((2, KEYS, vals), F32),
+                pltpu.VMEM((2, 8, 4 * KEYS), F32),
+                pltpu.VMEM((group, vals), F32),
+                pltpu.VMEM((group, vals), F32),
+            ],
         ),
         out_shape=[
             jax.ShapeDtypeStruct((rows, wide), LOW),
             jax.ShapeDtypeStruct((rows, wide), LOW),
-            jax.ShapeDtypeStruct((2, 4, 4 * KEYS), F32),
-            jax.ShapeDtypeStruct((1, vals), F32),
+            jax.ShapeDtypeStruct(taps.shape, F32),
+            jax.ShapeDtypeStruct(gain.shape, F32),
             jax.ShapeDtypeStruct((2, KEYS), F32),
+            jax.ShapeDtypeStruct((rows, width), LOW),
+            jax.ShapeDtypeStruct((1, width), F32),
         ],
         compiler_params=pltpu.CompilerParams(vmem_limit_bytes=VMEM_LIMIT),
         name="mixer_backward",
-    )(meta, params, mine, other, mine, other, o_a, o_b, dm_a, dm_b, states, inverses, taps, gain)
+    )(
+        meta, params, mine, other, mine, other, o_a, o_b, normed, d_branch, states, inverses,
+        *weights, taps, gain,
+    )
 
 
 def swap_section(array):
@@ -469,7 +582,7 @@
 
 
 def collect_rows(parts):
-    total = parts[0]
+    total = parts[0].astype(F32)
     for k in range(1, len(parts)):
         total = total + send_by(parts[k].astype(LOW), k).astype(F32)
     return total
@@ -513,67 +626,78 @@
     return [array[k * size : (k + 1) * size] for k in range(count)]
 
 
-def layer_forward(hidden, weights, gains, small, meta, live):
-    mix_mine, mix_other, out_mine, out_other, up_mine, up_other, down_mine, down_other = weights
+def layer_forward(hidden, weights, gains, small, meta, live, between, last):
+    mix_weights = weights
     params, taps, gain_out = small
     peers = lax.axis_size("tensor")
     normed, inv_one = norm_forward(hidden, gains[0])
     normed_all = jnp.concatenate(spread_rows(normed), axis=0)
-    mine = nn(normed_all, mix_mine)
-    other = nn(normed_all, mix_other)
-    mixed_a, mixed_b, o_a, o_b, states, inverses = mixer_forward(
-        meta, params, mine, other, taps, gain_out, peers
-    )
-    branch = collect_rows(
-        [
-            nt(a, out_mine) + nt(b, out_other)
-            for a, b in zip(split_rows(mixed_a, peers), split_rows(mixed_b, peers))
-        ]
-    )
+    if last is not None:
+        normed_all, last = lax.optimization_barrier((normed_all, last))
+        last = spread_rows(last)
+    mine, other, mixed_a, mixed_b, o_a, o_b, states, inverses, branch = mixer_forward(
+        meta, params, normed_all, mix_weights, taps, gain_out, peers
+    )
+    ffn_weights = between[0](branch)
+    if last is not None:
+        branch, last = lax.optimization_barrier((branch, last))
+    branch = collect_rows(split_rows(branch, peers))
     after = hidden + live * branch
     normed_two, inv_two = norm_forward(after, gains[1])
     normed_two_all = spread_rows(normed_two)
-    half = down_mine.shape[1]
     ups, actives, ffn = [], [], []
-    for chunk in normed_two_all:
-        pair = (nn(chunk, up_mine), nn(chunk, up_other))
-        active = [(jax.nn.silu(u[:, :half]) * u[:, half:]).astype(LOW) for u in pair]
-        ups.append(pair)
-        actives.append(active)
-        ffn.append(nt(active[0], down_mine) + nt(active[1], down_other))
-    result = after + live * collect_rows(ffn)
+    for place, chunk in enumerate(normed_two_all):
+        if place:
+            chunk, ffn[-1] = lax.optimization_barrier((chunk, ffn[-1]))
+        u_a, u_b, act_a, act_b, partial = ffn_forward(chunk, ffn_weights)
+        ups.append((u_a, u_b))
+        actives.append((act_a, act_b))
+        ffn.append(partial)
+    between[1](ffn[-1])
     kept = (
         hidden, inv_one, normed_all, mine, other, o_a, o_b, states, inverses, mixed_a, mixed_b,
         after, inv_two, normed_two_all, ups, actives,
     )
-    return result, kept
-
-
-def layer_backward(grad, kept, weights, gains, small, meta, live, owners):
-    mix_mine, mix_other, out_mine, out_other, up_mine, up_other, down_mine, down_other = weights
+    return ffn, kept, last, (mix_weights, ffn_weights)
+
+
+def finish_forward(after, live, ffn):
+    return (after + live * collect_rows(ffn)).astype(LOW)
+
+
+def share(mine, other):
+    got = swap_section(other.astype(LOW))
+    return (mine + got.astype(F32)).astype(LOW)
+
+
+def scatter(total):
+    return lax.psum_scatter(total, "dp", scatter_dimension=0, tiled=True)
+
+
+def exchange_sum(array, axis):
+    peers = lax.axis_size(axis)
+    offset = 1
+    while offset < peers:
+        array = array + lax.ppermute(array, axis, [(i, i ^ offset) for i in range(peers)])
+        offset *= 2
+    return array
+
+
+def layer_backward(grad, kept, weights, gains, small, meta, live, ffn_grads, waiting, beside, final):
+    mix_weights, ffn_weights = weights
     params, taps, gain_out = small
     (
         hidden, inv_one, normed_all, mine, other, o_a, o_b, states, inverses, mixed_a, mixed_b,
         after, inv_two, normed_two_all, ups, actives,
     ) = kept
     peers = lax.axis_size("tensor")
-    half = down_mine.shape[1]
-    ffn_grads = spread_rows((live * grad).astype(LOW))
+    if ffn_grads is None:
+        ffn_grads = spread_rows((live * grad).astype(LOW))
     d_ups, back = ([], []), []
     for chunk, pair in zip(ffn_grads, ups):
-        partial = None
-        for side, (u, down, up) in enumerate(
-            ((pair[0], down_mine, up_mine), (pair[1], down_other, up_other))
-        ):
-            d_active = nn(chunk, down)
-            gate, lift = u[:, :half], u[:, half:]
-            sig = jax.nn.sigmoid(gate)
-            d_gate = d_active * lift * (sig * (1.0 + gate * (1.0 - sig)))
-            d_lift = d_active * (gate * sig)
-            d_up = jnp.concatenate([d_gate, d_lift], axis=1).astype(LOW)
-            d_ups[side].append(d_up)
-            piece = nt(d_up, up)
-            partial = piece if partial is None else partial + piece
+        d_a, d_b, partial = ffn_backward(chunk, pair, ffn_weights)
+        d_ups[0].append(d_a)
+        d_ups[1].append(d_b)
         back.append(partial)
     back_two = collect_rows(back)
     two_all = jnp.concatenate(normed_two_all, axis=0)
@@ -583,30 +707,35 @@
         d_up_all = jnp.concatenate(d_ups[side], axis=0)
         active_all = jnp.concatenate([pair[side] for pair in actives], axis=0)
         ffn_parts.append((tn(two_all, d_up_all), tn(ffn_all, active_all)))
-    ffn_owned = owners(*[jnp.concatenate(part, axis=1) for part in ffn_parts])
+    ffn_total = share(*[jnp.concatenate(part, axis=1) for part in ffn_parts])
     back, gain_two_grad = norm_backward(after, inv_two, gains[1], back_two)
     grad_after = grad + back
     branch_all = jnp.concatenate(spread_rows((live * grad_after).astype(LOW)), axis=0)
-    d_mine, d_other, d_taps, d_gain, d_params = mixer_backward(
-        meta, params, mine, other, o_a, o_b, nn(branch_all, out_mine), nn(branch_all, out_other),
-        states, inverses, taps, gain_out, peers,
-    )
-    back_one = collect_rows(
-        [
-            nt(a, mix_mine) + nt(b, mix_other)
-            for a, b in zip(split_rows(d_mine, peers), split_rows(d_other, peers))
-        ]
-    )
-    out_parts = [tn(branch_all, mixed_a), tn(branch_all, mixed_b)]
-    mix_parts = [tn(normed_all, d_mine), tn(normed_all, d_other)]
-    mix_owned = owners(
-        *[jnp.concatenate([o, m], axis=1) for o, m in zip(out_parts, mix_parts)]
-    )
-    back, gain_one_grad = norm_backward(hidden, inv_one, gains[0], back_one)
+    out_total = share(tn(branch_all, mixed_a), tn(branch_all, mixed_b))
+    early = jnp.concatenate([ffn_total, out_total], axis=1)
+    early, branch_all, waiting = lax.optimization_barrier((early, branch_all, waiting))
+    early_owned = scatter(early)
+    d_mine, d_other, d_taps, d_gain, d_params, inward, gain_one_grad = mixer_backward(
+        meta, params, (mine, other, o_a, o_b, states, inverses), normed_all, branch_all,
+        mix_weights, taps, gain_out, peers,
+    )
+    waiting = beside(waiting)
+    inward, waiting = lax.optimization_barrier((inward, waiting))
+    mix_total = share(tn(normed_all, d_mine[:, : 6 * KEYS]), tn(normed_all, d_other[:, : 6 * KEYS]))
+    if final:
+        inward, mix_total = lax.optimization_barrier((inward, mix_total))
+    back_one = collect_rows(split_rows(inward, peers))
+    early_owned, mix_total = lax.optimization_barrier((early_owned, mix_total))
+    mix_owned = scatter(mix_total)
+    pairs = jnp.concatenate([d[:, 6 * KEYS : 6 * KEYS + 2] for d in (d_mine, d_other)], axis=1)
+    decay_grad = tn(pairs, normed_all)
+    gain_one_grad = gain_one_grad[0] / gains[0]
+    back, _ = norm_backward(hidden, inv_one, gains[0], back_one)
     return (
         grad_after + back,
-        (ffn_owned, mix_owned),
-        (jnp.stack([gain_one_grad, gain_two_grad]), d_taps, d_params, d_gain),
+        [early_owned, mix_owned],
+        (jnp.stack([gain_one_grad, gain_two_grad]), *lax.optimization_barrier((d_taps, d_params, d_gain, decay_grad, mix_total))[:4]),
+        waiting,
     )
 
 
@@ -622,7 +751,11 @@
     buffer = rows_here * lax.axis_size("tensor")
     ff = w_down.shape[1]
     half = ff // 2
+    wide = -(-half // KEYS) * KEYS
     vals = 2 * KEYS
+
+    def zeros(count):
+        return jnp.zeros((w_query.shape[1], count), LOW)
 
     def half_mix(h):
         return jnp.concatenate(
@@ -632,18 +765,22 @@
                 w_value[0][:, h * vals : (h + 1) * vals],
                 w_gate[0][:, h * vals : (h + 1) * vals],
                 w_decay[0][:, h * 2 : (h + 1) * 2],
+                zeros(KEYS - 2),
+                w_out[0][h * vals : (h + 1) * vals].T,
             ],
             axis=1,
         )
 
-    def half_rest(h):
+    def half_ffn(h):
         hidden_part = slice(h * half, (h + 1) * half)
         return jnp.concatenate(
             [
                 w_updown[0][:, 0, hidden_part],
+                zeros(wide - half),
                 w_updown[0][:, 1, hidden_part],
+                zeros(wide - half),
                 w_down[0][hidden_part].T,
-                w_out[0][h * vals : (h + 1) * vals].T,
+                zeros(wide - half),
             ],
             axis=1,
         )
@@ -654,25 +791,19 @@
         return jnp.where(first, keep, got), jnp.where(first, got, keep)
 
     mix_shards = both_layers((half_mix(0), half_mix(1)))
-    rest_shards = both_layers((half_rest(0), half_rest(1)))
-
-    def fetch(layer):
-        sides = []
-        mix = lax.all_gather(mix_shards[layer], "dp", axis=0, tiled=True)
-        rest = lax.all_gather(rest_shards[layer], "dp", axis=0, tiled=True)
-        return mix, swap_section(mix), rest, swap_section(rest)
-
-    def arrange(fetched):
-        mix, mix_two, rest, rest_two = fetched
-        return (
-            mix, mix_two,
-            rest[:, 3 * half :], rest_two[:, 3 * half :],
-            rest[:, : 2 * half], rest_two[:, : 2 * half],
-            rest[:, 2 * half : 3 * half], rest_two[:, 2 * half : 3 * half],
+    ffn_shards = both_layers((half_ffn(0), half_ffn(1)))
+
+    def gather(shard, *before):
+        if before:
+            shard, *before = lax.optimization_barrier((shard, *before))
+        full = lax.all_gather(shard, "dp", axis=0, tiled=True)
+        return (full, *before)
+
+    def of_all(array):
+        got = swap_section(array)
+        return jnp.concatenate(
+            [jnp.where(first, array, got), jnp.where(first, got, array)], axis=0
         )
-
-    def of_all(array):
-        return lax.all_gather(array, "section", axis=0, tiled=True)
 
     gains_all = of_all(norm_gain)
     sizes = (conv_weight.size, head_rate.size, head_bias.size, out_gain.size)
@@ -705,26 +836,52 @@
     def own_micro(array):
         return lax.dynamic_index_in_dim(array, section, 0, keepdims=False).astype(F32)
 
-    weights = [arrange(fetch(layer)) for layer in range(2)]
     hidden = own_micro(inputs)
-    kept = []
-    for layer in range(2):
-        result, saved = layer_forward(hidden, weights[layer], gains_all[layer], smalls[layer], meta, live)
-        result_low = result.astype(LOW)
-        hidden = result_low.astype(F32)
-        kept.append(saved)
-
-    def owners(mine, other):
-        got = swap_section(other.astype(LOW))
-        total = (mine + got.astype(F32)).astype(LOW)
-        return lax.psum_scatter(total, "dp", scatter_dimension=0, tiled=True)
+    (mix_full,) = gather(mix_shards[0])
+    ffn_full, mix_full = gather(ffn_shards[0], mix_full)
+    mix_pair = (mix_full, swap_section(mix_full))
+    held = {}
+
+    def first_mixed(branch):
+        held["mix"], full, _ = gather(mix_shards[1], ffn_full, branch)
+        return full, swap_section(full)
+
+    def first_done(partial):
+        held["ffn"], held["mix"], _ = gather(ffn_shards[1], held["mix"], partial)
+
+    def second_mixed(branch):
+        return held["ffn"], swap_section(held["ffn"])
+
+    def second_done(partial):
+        pass
+
+    ffn, saved, _, weights_one = layer_forward(
+        hidden, mix_pair, gains_all[0], smalls[0], meta, live, (first_mixed, first_done), None
+    )
+    kept = [saved]
+    hidden = finish_forward(saved[11], live, ffn).astype(F32)
+    mix_pair = (held["mix"], swap_section(held["mix"]))
+    ffn_last, saved, spread, weights_two = layer_forward(
+        hidden, mix_pair, gains_all[1], smalls[1], meta, live, (second_mixed, second_done),
+        (live * own_micro(cotangent)).astype(LOW),
+    )
+    kept.append(saved)
+    weights = [weights_one, weights_two]
 
     grad = own_micro(cotangent)
     owned, small_grads = [None, None], [None, None]
     for layer in (1, 0):
-        grad, owned[layer], small_grads[layer] = layer_backward(
-            grad, kept[layer], weights[layer], gains_all[layer], smalls[layer], meta, live, owners
+        waiting = ffn_last if layer == 1 else owned[1]
+        grad, owned[layer], small_grads[layer], waiting = layer_backward(
+            grad, kept[layer], weights[layer], gains_all[layer], smalls[layer], meta, live,
+            spread if layer == 1 else None, waiting,
+            (lambda parts: finish_forward(kept[1][11], live, parts)) if layer == 1 else (lambda x: x),
+            layer == 0,
         )
+        if layer == 0:
+            owned[1] = waiting
+        else:
+            result_low = waiting
         grad_low = grad.astype(LOW)
         grad = grad_low.astype(F32)
 
@@ -738,23 +895,31 @@
                 jnp.where(first, got, keep).astype(F32),
             )
         )
-    ffn_pair, mix_pair = halves
+    early_pair, mix_pair = halves
 
     def columns(pair, start, size):
         return jnp.concatenate([side[:, start : start + size] for side in pair], axis=1)
 
-    grad_updown = jnp.stack([columns(ffn_pair, 0, half), columns(ffn_pair, half, half)], axis=1)
-    grad_down = columns(ffn_pair, 2 * half, half).T
-    grad_out = columns(mix_pair, 0, vals).T
-    grad_query = columns(mix_pair, vals, KEYS)
-    grad_key = columns(mix_pair, vals + KEYS, KEYS)
-    grad_value = columns(mix_pair, vals + 2 * KEYS, vals)
-    grad_gate = columns(mix_pair, 2 * vals + 2 * KEYS, vals)
-    grad_decay = columns(mix_pair, 3 * vals + 2 * KEYS, 2)
+    grad_updown = jnp.stack([columns(early_pair, 0, half), columns(early_pair, wide, half)], axis=1)
+    grad_down = columns(early_pair, 2 * wide, half).T
+    grad_out = columns(early_pair, 3 * wide, vals).T
+    grad_query = columns(mix_pair, 0, KEYS)
+    grad_key = columns(mix_pair, KEYS, KEYS)
+    grad_value = columns(mix_pair, 2 * KEYS, vals)
+    grad_gate = columns(mix_pair, vals + 2 * KEYS, vals)
+
+    pairs = jnp.stack([small_grads[layer][4] for layer in range(2)])
+    pairs = exchange_sum(pairs[:, :2] + swap_section(pairs[:, 2:]), "dp")
+    pairs = lax.dynamic_slice_in_dim(
+        pairs, lax.axis_index("dp") * w_query.shape[1], w_query.shape[1], 2
+    )
+    keep = jnp.where(first, pairs[0], pairs[1])
+    got = swap_section(jnp.where(first, pairs[1], pairs[0]))
+    grad_decay = jnp.concatenate([jnp.where(first, keep, got), jnp.where(first, got, keep)], axis=0).T
 
     flat = []
     for layer in range(2):
-        gain_grads, d_taps, d_params, d_gain = small_grads[layer]
+        gain_grads, d_taps, d_params, d_gain, _ = small_grads[layer]
         conv_full = jnp.zeros(conv_weight.shape[1:], F32)
         pair_full = jnp.zeros((heads, 2), F32)
         for side, p in enumerate(places):
@@ -768,8 +933,9 @@
                 ]
             )
         )
-    summed = lax.psum(jnp.stack(flat), ("section", "dp", "tensor"))
-    own = lax.dynamic_index_in_dim(summed, section, 0, keepdims=False)
+    got = swap_section(jnp.where(first, flat[1], flat[0]))
+    own = jnp.where(first, flat[0], flat[1]) + got
+    own = exchange_sum(exchange_sum(own, "tensor"), "dp")
     pieces = [own[a:b] for a, b in zip(edges[:-1], edges[1:])]
     return (
         result_low[None],

time: 987 us -> 744 us (0.75)
  matrix products: 228 us -> 36.6 us
  waiting for transfers between devices: 390 us -> 279 us
  Pallas kernels: 195 us -> 226 us
  starting transfers between devices: 57.8 us -> 73.2 us
    dot_general x104 -> x0, matrix products: 184 us -> none  [the longest x64 107 us: nt(): lax.dot_general(left, right, (((1,), (1,)), ((), ())), preferred_element_...]
    psum x1 -> x0, waiting for transfers between devices: 118 us -> none  [on_device(): summed = lax.psum(jnp.stack(flat), ('section', 'dp', 'tensor'))]
    pallas_call x0 -> x16, Pallas kernels: none -> 88.1 us  [the longest x8 47.9 us: ffn_backward(): pl.pallas_call(ffn_backward_kernel, out_shape=[jax.ShapeDtypeStruct((coun...]
    pallas_call x2, Pallas kernels: 125 us -> 54.4 us  [mixer_forward(): pl.pallas_call(mixer_forward_kernel, grid_spec=pltpu.PrefetchScalarGridSp...]
    all_gather x4, waiting for transfers between devices: 82.5 us -> 54.1 us  [gather(): full = lax.all_gather(shard, 'dp', axis=0, tiled=True)]
    ppermute x48, waiting for transfers between devices: 187 us -> 205 us  [send_by(): lax.ppermute(array, 'tensor', [(i, i ^ offset) for i in range(peers)])]
    ppermute x0 -> x6, waiting for transfers between devices: none -> 16.6 us  [exchange_sum(): lax.ppermute(array, axis, [(i, i ^ offset) for i in range(peers)])]
    pallas_call x2, Pallas kernels: 70.3 us -> 83.8 us  [mixer_backward(): pl.pallas_call(mixer_backward_kernel, grid_spec=pltpu.PrefetchScalarGridS...]
  transfers between devices with their start and end apart: 70 -> 81, of which waited for: 28 -> 33; matrix products, arithmetic and copies ran while one was open for 30% -> 14% of each run, Pallas kernels for 20% -> 30%
where the time goes in v2:
time: 744 us; the launch traced here: 732 us
  waiting for transfers between devices  279 us (38%)
  Pallas kernels  226 us (30%)
  starting transfers between devices  73.2 us (10%)
  other arithmetic  50.8 us (7%)
  local copies, waits for them, and re-layouts  48.8 us (7%)
  matrix products  36.6 us (5%)
  between operations  16.9 us (2%)
    ppermute x48, waiting for transfers between devices, send_by(): lax.ppermute(array, 'tensor', [(i, i ^ offset) for i in range(peers)])  205 us
    pallas_call x2, Pallas kernels, mixer_backward(): pl.pallas_call(mixer_backward_kernel, grid_spec=pltpu.PrefetchScalarGridS...  83.8 us
    ppermute x48, starting transfers between devices, send_by(): lax.ppermute(array, 'tensor', [(i, i ^ offset) for i in range(peers)])  57.4 us
    pallas_call x2, Pallas kernels, mixer_forward(): pl.pallas_call(mixer_forward_kernel, grid_spec=pltpu.PrefetchScalarGridSp...  54.4 us
    all_gather x4, waiting for transfers between devices, gather(): full = lax.all_gather(shard, 'dp', axis=0, tiled=True)  54.1 us
    pallas_call x8, Pallas kernels, ffn_backward(): pl.pallas_call(ffn_backward_kernel, out_shape=[jax.ShapeDtypeStruct((coun...  47.9 us
    pallas_call x8, Pallas kernels, ffn_forward(): pl.pallas_call(ffn_forward_kernel, out_shape=[jax.ShapeDtypeStruct((count...  40.2 us
    dot_general x18, matrix products, tn(): lax.dot_general(left, right, (((0,), (0,)), ((), ())), preferred_element_...  36.6 us
  transfers between devices with their start and end apart: 81, of which 33 were waited for; matrix products, arithmetic and copies ran while one was open for 14% of the time, Pallas kernels for 30%

profile of v2, /device:TPU:8, one launch (start us, length us, event | category | flops | bytes accessed | tf_op | source)
XLA Modules:
  0.0 731.8 jit_solution(12569459917481636314)
XLA Ops:
  26.7 38.1 %all-gather.5.cloned.1.call-done.mix_mine = bf16[1024,1152]{1,0:T(8,128)(2,1)} async-done(((bf16[256,1152]{1,0:T(8,128)(2,1)}), bf16[1024,1152]{1,0:T(8,128)(2,1)}) %all-gather.5.cloned.1.call-update) | async-done | bytes 2359312 | tf_op jit(solution)/shard_map/all_gather | solution.py:799
  72.6 27.2 %mixer_forward.2 = (f32[1024,896]{1,0:T(8,128)}, f32[1024,896]{1,0:T(8,128)}, bf16[1024,256]{1,0:T(8,128)(2,1)}, bf16[1024,256]{1,0:T(8,128)(2,1)}, f32[1024,256...) custom-call(s32[17]{0:T(128)} %pad_add_fusion.meta, ...), custom_call_target="tpu_custom_call" | custom-call | tf_op jit(solution)/shard_map/mixer_forward/pallas_call | solution.py:454
  99.8 16.0 %all-gather.7.cloned.1.call-done.mine = bf16[1024,1152]{1,0:T(8,128)(2,1)} async-done(((bf16[256,1152]{1,0:T(8,128)(2,1)}), bf16[1024,1152]{1,0:T(8,128)(2,1)}) %all-gather.7.cloned.1.call-update) | async-done | bytes 2359312 | tf_op jit(solution)/shard_map/all_gather | solution.py:799
  124.2 10.4 %collective-permute-done.10 = bf16[256,1024]{1,0:T(8,128)(2,1)S(1)} collective-permute-done((bf16[256,1024]{1,0:T(8,128)(2,1)}, bf16[256,1024]{1,0:T(8,128)(2,1)S(1)}, u32[]{:S(2)}, u32[]{:S(2)}) %collective-permute-start.10) | collective-permute-done | bytes 524320 | tf_op jit(solution)/shard_map/ppermute | solution.py:576
  134.6 10.8 %collective-permute-done.8 = bf16[256,1024]{1,0:T(8,128)(2,1)S(1)} collective-permute-done((bf16[256,1024]{1,0:T(8,128)(2,1)}, bf16[256,1024]{1,0:T(8,128)(2,1)S(1)}, u32[]{:S(2)}, u32[]{:S(2)}) %collective-permute-start.8) | collective-permute-done | bytes 524320 | tf_op jit(solution)/shard_map/ppermute | solution.py:576
  190.1 9.8 %collective-permute-done.17 = bf16[256,1024]{1,0:T(8,128)(2,1)S(1)} collective-permute-done((bf16[256,1024]{1,0:T(8,128)(2,1)}, bf16[256,1024]{1,0:T(8,128)(2,1)S(1)}, u32[]{:S(2)}, u32[]{:S(2)}) %collective-permute-start.17) | collective-permute-done | bytes 524320 | tf_op jit(solution)/shard_map/ppermute | solution.py:576
  199.9 5.5 collective-permute-done.16
  211.3 11.3 %collective-permute-done.18 = bf16[256,1024]{1,0:T(8,128)(2,1)S(1)} collective-permute-done((bf16[256,1024]{1,0:T(8,128)(2,1)S(1)}, bf16[256,1024]{1,0:T(8,128)(2,1)S(1)}, u32[]{:S(2)}, u32[]{:S(2)}) %collective-permute-start.18) | collective-permute-done | bytes 524320 | tf_op jit(solution)/shard_map/ppermute | solution.py:576
  222.6 9.2 %collective-permute-done.19 = bf16[256,1024]{1,0:T(8,128)(2,1)S(1)} collective-permute-done((bf16[256,1024]{1,0:T(8,128)(2,1)S(1)}, bf16[256,1024]{1,0:T(8,128)(2,1)S(1)}, u32[]{:S(2)}, u32[]{:S(2)}) %collective-permute-start.19) | collective-permute-done | bytes 524320 | tf_op jit(solution)/shard_map/ppermute | solution.py:576
  239.1 27.3 %mixer_forward.3 = (f32[1024,896]{1,0:T(8,128)}, f32[1024,896]{1,0:T(8,128)}, bf16[1024,256]{1,0:T(8,128)(2,1)}, bf16[1024,256]{1,0:T(8,128)(2,1)}, f32[1024,256...) custom-call(s32[17]{0:T(128)} %pad_add_fusion.meta, ...), custom_call_target="tpu_custom_call" | custom-call | tf_op jit(solution)/shard_map/mixer_forward/pallas_call | solution.py:454
  271.9 11.2 %collective-permute-done.25 = bf16[256,1024]{1,0:T(8,128)(2,1)S(1)} collective-permute-done((bf16[256,1024]{1,0:T(8,128)(2,1)S(1)}, bf16[256,1024]{1,0:T(8,128)(2,1)S(1)}, u32[]{:S(2)}, u32[]{:S(2)}) %collective-permute-start.25) | collective-permute-done | bytes 524320 | tf_op jit(solution)/shard_map/ppermute | solution.py:576
  283.1 11.5 %collective-permute-done.26 = bf16[256,1024]{1,0:T(8,128)(2,1)S(1)} collective-permute-done((bf16[256,1024]{1,0:T(8,128)(2,1)S(1)}, bf16[256,1024]{1,0:T(8,128)(2,1)S(1)}, u32[]{:S(2)}, u32[]{:S(2)}) %collective-permute-start.26) | collective-permute-done | bytes 524320 | tf_op jit(solution)/shard_map/ppermute | solution.py:576
  327.4 6.1 ffn_backward.9
  334.6 5.9 ffn_backward.10
  346.7 5.9 ffn_backward.11
  354.0 6.2 ffn_backward.8
  370.3 11.3 %collective-permute-done.36 = bf16[256,1024]{1,0:T(8,128)(2,1)S(1)} collective-permute-done((bf16[256,1024]{1,0:T(8,128)(2,1)S(1)}, bf16[256,1024]{1,0:T(8,128)(2,1)S(1)}, u32[]{:S(2)}, u32[]{:S(2)}) %collective-permute-start.36) | collective-permute-done | bytes 524320 | tf_op jit(solution)/shard_map/ppermute | solution.py:576
  381.6 10.9 %collective-permute-done.37 = bf16[256,1024]{1,0:T(8,128)(2,1)S(1)} collective-permute-done((bf16[256,1024]{1,0:T(8,128)(2,1)S(1)}, bf16[256,1024]{1,0:T(8,128)(2,1)S(1)}, u32[]{:S(2)}, u32[]{:S(2)}) %collective-permute-start.37) | collective-permute-done | bytes 524320 | tf_op jit(solution)/shard_map/ppermute | solution.py:576
  405.9 42.2 %mixer_backward.2 = (bf16[1024,896]{1,0:T(8,128)(2,1)}, bf16[1024,896]{1,0:T(8,128)(2,1)}, f32[2,4,512]{2,1,0:T(4,128)}, f32[1,256]{1,0:T(1,128)}, f32[2,128]{1,...) custom-call(s32[17]{0:T(128)} %pad_add_fusion.meta, f32[2,2]{1,0:T(2,128)} %pad_maximum_fusion.19.params, ...), custom_call_target="tpu_custom_call" | custom-call | tf_op jit(solution)/shard_map/mixer_backward/pallas_call | solution.py:516
  453.7 11.4 %collective-permute-done.43 = bf16[256,1024]{1,0:T(8,128)(2,1)S(1)} collective-permute-done((bf16[256,1024]{1,0:T(8,128)(2,1)S(1)}, bf16[256,1024]{1,0:T(8,128)(2,1)S(1)}, u32[]{:S(2)}, u32[]{:S(2)}) %collective-permute-start.43) | collective-permute-done | bytes 524320 | tf_op jit(solution)/shard_map/ppermute | solution.py:576
  465.0 9.7 %collective-permute-done.44 = bf16[256,1024]{1,0:T(8,128)(2,1)S(1)} collective-permute-done((bf16[256,1024]{1,0:T(8,128)(2,1)S(1)}, bf16[256,1024]{1,0:T(8,128)(2,1)S(1)}, u32[]{:S(2)}, u32[]{:S(2)}) %collective-permute-start.44) | collective-permute-done | bytes 524320 | tf_op jit(solution)/shard_map/ppermute | solution.py:576
  483.3 5.9 ffn_backward.12
  492.4 5.9 ffn_backward.13
  499.1 5.9 ffn_backward.14
  505.9 6.0 ffn_backward.15
  525.8 7.0 collective-permute-done.47
  532.8 12.4 %collective-permute-done.49 = bf16[256,1024]{1,0:T(8,128)(2,1)} collective-permute-done((bf16[256,1024]{1,0:T(8,128)(2,1)}, bf16[256,1024]{1,0:T(8,128)(2,1)}, u32[]{:S(2)}, u32[]{:S(2)}) %collective-permute-start.49) | collective-permute-done | bytes 524320 | tf_op jit(solution)/shard_map/ppermute | solution.py:576
  554.2 11.4 %collective-permute-done.53 = bf16[256,1024]{1,0:T(8,128)(2,1)S(1)} collective-permute-done((bf16[256,1024]{1,0:T(8,128)(2,1)S(1)}, bf16[256,1024]{1,0:T(8,128)(2,1)S(1)}, u32[]{:S(2)}, u32[]{:S(2)}) %collective-permute-start.53) | collective-permute-done | bytes 524320 | tf_op jit(solution)/shard_map/ppermute | solution.py:576
  565.5 10.4 %collective-permute-done.54 = bf16[256,1024]{1,0:T(8,128)(2,1)S(1)} collective-permute-done((bf16[256,1024]{1,0:T(8,128)(2,1)S(1)}, bf16[256,1024]{1,0:T(8,128)(2,1)S(1)}, u32[]{:S(2)}, u32[]{:S(2)}) %collective-permute-start.54) | collective-permute-done | bytes 524320 | tf_op jit(solution)/shard_map/ppermute | solution.py:576
  588.0 41.6 %mixer_backward.3 = (bf16[1024,896]{1,0:T(8,128)(2,1)}, bf16[1024,896]{1,0:T(8,128)(2,1)}, f32[2,4,512]{2,1,0:T(4,128)}, f32[1,256]{1,0:T(1,128)}, f32[2,128]{1,...) custom-call(s32[17]{0:T(128)} %pad_add_fusion.meta, f32[2,2]{1,0:T(2,128)} %pad_maximum_fusion.21.params, ...), custom_call_target="tpu_custom_call" | custom-call | tf_op jit(solution)/shard_map/mixer_backward/pallas_call | solution.py:516
  652.1 10.8 %collective-permute-done.59 = bf16[256,1024]{1,0:T(8,128)(2,1)S(1)} collective-permute-done((bf16[256,1024]{1,0:T(8,128)(2,1)S(1)}, bf16[256,1024]{1,0:T(8,128)(2,1)S(1)}, u32[]{:S(2)}, u32[]{:S(2)}) %collective-permute-start.59) | collective-permute-done | bytes 524320 | tf_op jit(solution)/shard_map/ppermute | solution.py:576
  662.9 11.5 %collective-permute-done.60 = bf16[256,1024]{1,0:T(8,128)(2,1)S(1)} collective-permute-done((bf16[256,1024]{1,0:T(8,128)(2,1)S(1)}, bf16[256,1024]{1,0:T(8,128)(2,1)S(1)}, u32[]{:S(2)}, u32[]{:S(2)}) %collective-permute-start.60) | collective-permute-done | bytes 524320 | tf_op jit(solution)/shard_map/ppermute | solution.py:576
  (653 shorter events, 288.2 us)
Async XLA Ops:
  7.2 57.6 %all-gather.5.cloned.1.call-start = ((), (), s32[]{:S(2)}) async-start(), calls=%async_computation.4 | async-start | bytes 2949120 | tf_op jit(solution)/shard_map/all_gather | solution.py:799
  14.7 101.1 %all-gather.7.cloned.1.call-start = ((), (), s32[]{:S(2)}) async-start(), calls=%async_computation.5 | async-start | bytes 2949120 | tf_op jit(solution)/shard_map/all_gather | solution.py:799
  15.1 49.9 %collective-permute-start = (f32[1,16656]{1,0:T(1,128)S(1)}, f32[1,16656]{1,0:T(1,128)S(1)}, u32[]{:S(2)}, u32[]{:S(2)}) collective-permute-start(f32[1,16656]{1,0:T(1,128)S(1)} %broadcast_in_dim.60), channel_id=1, source_target_pairs={{0,16},{16,0},{1,17},{17,1},{2,18},{18,2},{3,19},{19,3},{4,20},{20... | collective-permute-start | bytes 199880 | tf_op jit(solution)/shard_map/ppermute | solution.py:571
  20.8 47.4 %collective-permute-start.2 = (bf16[256,1024]{1,0:T(8,128)(2,1)S(1)}, bf16[256,1024]{1,0:T(8,128)(2,1)}, u32[]{:S(2)}, u32[]{:S(2)}) collective-permute-start(bf16[256,1024]{1,0:T(8,128)(2,1)S(1)} %fusion.46), channel_id=1, source_target_pairs={{0,1},{1,0},{2,3},{3,2},{4,5},{5,4},{6,7},{7,6},{8,9},{9,8},{10,11... | collective-permute-start | bytes 1572872 | tf_op jit(solution)/shard_map/ppermute | solution.py:576
  22.4 45.8 %collective-permute-start.3 = (bf16[256,1024]{1,0:T(8,128)(2,1)S(1)}, bf16[256,1024]{1,0:T(8,128)(2,1)}, u32[]{:S(2)}, u32[]{:S(2)}) collective-permute-start(bf16[256,1024]{1,0:T(8,128)(2,1)S(1)} %fusion.46), channel_id=1, source_target_pairs={{0,2},{1,3},{2,0},{3,1},{4,6},{5,7},{6,4},{7,5},{8,10},{9,11},{10,... | collective-permute-start | bytes 1572872 | tf_op jit(solution)/shard_map/ppermute | solution.py:576
  23.9 44.3 %collective-permute-start.4 = (bf16[256,1024]{1,0:T(8,128)(2,1)S(1)}, bf16[256,1024]{1,0:T(8,128)(2,1)}, u32[]{:S(2)}, u32[]{:S(2)}) collective-permute-start(bf16[256,1024]{1,0:T(8,128)(2,1)S(1)} %fusion.46), channel_id=1, source_target_pairs={{0,3},{1,2},{2,1},{3,0},{4,7},{5,6},{6,5},{7,4},{8,11},{9,10},{10,... | collective-permute-start | bytes 1572872 | tf_op jit(solution)/shard_map/ppermute | solution.py:576
  64.9 121.6 %all-gather.9.cloned.1.call-start = ((), (), s32[]{:S(2)}) async-start(), calls=%async_computation.6 | async-start | bytes 2949120 | tf_op jit(solution)/shard_map/all_gather | solution.py:799
  115.8 121.1 %all-gather.11.cloned.1.call-start = ((), (), s32[]{:S(2)}) async-start(), calls=%async_computation.7 | async-start | bytes 2949120 | tf_op jit(solution)/shard_map/all_gather | solution.py:799
  116.0 36.1 %collective-permute-start.12 = (bf16[1024,1152]{1,0:T(8,128)(2,1)}, bf16[1024,1152]{1,0:T(8,128)(2,1)S(1)}, u32[]{:S(2)}, u32[]{:S(2)}) collective-permute-start(bf16[1024,1152]{1,0:T(8,128)(2,1)} %all-gather.7.cloned.1.call-done.mine), channel_id=1, source_target_pairs={{0,16},{16,0},{1,17},{17,1},{2,18},{18,2},{3,19},{19,3},{4,20},{20... | collective-permute-start | bytes 7077896 | tf_op jit(solution)/shard_map/ppermute | solution.py:571
  150.9 29.7 %collective-permute-start.15 = (bf16[256,1024]{1,0:T(8,128)(2,1)S(1)}, bf16[256,1024]{1,0:T(8,128)(2,1)S(1)}, u32[]{:S(2)}, u32[]{:S(2)}) collective-permute-start(bf16[256,1024]{1,0:T(8,128)(2,1)S(1)} %multiply_convert_fusion.3.rows), channel_id=1, source_target_pairs={{0,3},{1,2},{2,1},{3,0},{4,7},{5,6},{6,5},{7,4},{8,11},{9,10},{10,... | collective-permute-start | bytes 1572872 | tf_op jit(solution)/shard_map/ppermute | solution.py:576
  186.5 360.8 %reduce-scatter.5.cloned.1.call-start = ((), (), s32[]{:S(2)}) async-start(), calls=%async_computation.8 | async-start | bytes 3604480 | tf_op jit(solution)/shard_map/reduce_scatter | solution.py:674
  190.1 49.0 %collective-permute-start.21 = (bf16[1024,1152]{1,0:T(8,128)(2,1)}, bf16[1024,1152]{1,0:T(8,128)(2,1)}, u32[]{:S(2)}, u32[]{:S(2)}) collective-permute-start(bf16[1024,1152]{1,0:T(8,128)(2,1)} %all-gather.9.cloned.1.call-done.mix_mine), channel_id=1, source_target_pairs={{0,16},{16,0},{1,17},{17,1},{2,18},{18,2},{3,19},{19,3},{4,20},{20... | collective-permute-start | bytes 7077896 | tf_op jit(solution)/shard_map/ppermute | solution.py:571
  233.3 33.0 %collective-permute-start.22 = (bf16[256,1024]{1,0:T(8,128)(2,1)}, bf16[256,1024]{1,0:T(8,128)(2,1)}, u32[]{:S(2)}, u32[]{:S(2)}) collective-permute-start(bf16[256,1024]{1,0:T(8,128)(2,1)} %get-tuple-element.189.grad), channel_id=1, source_target_pairs={{0,1},{1,0},{2,3},{3,2},{4,5},{5,4},{6,7},{7,6},{8,9},{9,8},{10,11... | collective-permute-start | bytes 1572872 | tf_op jit(solution)/shard_map/ppermute | solution.py:576
  234.3 32.1 %collective-permute-start.23 = (bf16[256,1024]{1,0:T(8,128)(2,1)}, bf16[256,1024]{1,0:T(8,128)(2,1)S(1)}, u32[]{:S(2)}, u32[]{:S(2)}) collective-permute-start(bf16[256,1024]{1,0:T(8,128)(2,1)} %get-tuple-element.189.grad), channel_id=1, source_target_pairs={{0,2},{1,3},{2,0},{3,1},{4,6},{5,7},{6,4},{7,5},{8,10},{9,11},{10,... | collective-permute-start | bytes 1572872 | tf_op jit(solution)/shard_map/ppermute | solution.py:576
  235.2 31.2 %collective-permute-start.24 = (bf16[256,1024]{1,0:T(8,128)(2,1)}, bf16[256,1024]{1,0:T(8,128)(2,1)S(1)}, u32[]{:S(2)}, u32[]{:S(2)}) collective-permute-start(bf16[256,1024]{1,0:T(8,128)(2,1)} %get-tuple-element.189.grad), channel_id=1, source_target_pairs={{0,3},{1,2},{2,1},{3,0},{4,7},{5,6},{6,5},{7,4},{8,11},{9,10},{10,... | collective-permute-start | bytes 1572872 | tf_op jit(solution)/shard_map/ppermute | solution.py:576
  236.9 66.7 %collective-permute-start.31 = (bf16[1024,1152]{1,0:T(8,128)(2,1)}, bf16[1024,1152]{1,0:T(8,128)(2,1)S(1)}, u32[]{:S(2)}, u32[]{:S(2)}) collective-permute-start(bf16[1024,1152]{1,0:T(8,128)(2,1)} %all-gather.11.cloned.1.call-done.mine), channel_id=1, source_target_pairs={{0,16},{16,0},{1,17},{17,1},{2,18},{18,2},{3,19},{19,3},{4,20},{20... | collective-permute-start | bytes 7077896 | tf_op jit(solution)/shard_map/ppermute | solution.py:571
  269.4 25.3 %collective-permute-start.26 = (bf16[256,1024]{1,0:T(8,128)(2,1)S(1)}, bf16[256,1024]{1,0:T(8,128)(2,1)S(1)}, u32[]{:S(2)}, u32[]{:S(2)}) collective-permute-start(bf16[256,1024]{1,0:T(8,128)(2,1)S(1)} %get-tuple-element.341), channel_id=1, source_target_pairs={{0,2},{1,3},{2,0},{3,1},{4,6},{5,7},{6,4},{7,5},{8,10},{9,11},{10,... | collective-permute-start | bytes 1572872 | tf_op jit(solution)/shard_map/ppermute | solution.py:576
  298.5 28.9 %collective-permute-start.30 = (bf16[256,1024]{1,0:T(8,128)(2,1)S(1)}, bf16[256,1024]{1,0:T(8,128)(2,1)S(1)}, u32[]{:S(2)}, u32[]{:S(2)}) collective-permute-start(bf16[256,1024]{1,0:T(8,128)(2,1)S(1)} %multiply_convert_fusion.2.rows), channel_id=1, source_target_pairs={{0,3},{1,2},{2,1},{3,0},{4,7},{5,6},{6,5},{7,4},{8,11},{9,10},{10,... | collective-permute-start | bytes 1572872 | tf_op jit(solution)/shard_map/ppermute | solution.py:576
  333.5 31.2 %collective-permute-start.33 = (bf16[256,1024]{1,0:T(8,128)(2,1)}, bf16[256,1024]{1,0:T(8,128)(2,1)S(1)}, u32[]{:S(2)}, u32[]{:S(2)}) collective-permute-start(bf16[256,1024]{1,0:T(8,128)(2,1)} %get-tuple-element.225), channel_id=1, source_target_pairs={{0,1},{1,0},{2,3},{3,2},{4,5},{5,4},{6,7},{7,6},{8,9},{9,8},{10,11... | collective-permute-start | bytes 1572872 | tf_op jit(solution)/shard_map/ppermute | solution.py:576
  364.6 34.0 %collective-permute-start.32 = (bf16[1024,1152]{0,1:T(8,128)(2,1)S(1)}, bf16[1024,1152]{0,1:T(8,128)(2,1)S(1)}, u32[]{:S(2)}, u32[]{:S(2)}) collective-permute-start(bf16[1024,1152]{0,1:T(8,128)(2,1)S(1)} %pad_maximum_fusion.2), channel_id=1, source_target_pairs={{0,16},{16,0},{1,17},{17,1},{2,18},{18,2},{3,19},{19,3},{4,20},{20... | collective-permute-start | bytes 7077896 | tf_op jit(solution)/shard_map/ppermute | solution.py:571
  401.4 186.5 %reduce-scatter.7.cloned.1.call-start = ((), (), s32[]{:S(2)}) async-start(), calls=%async_computation.9 | async-start | bytes 1966080 | tf_op jit(solution)/shard_map/reduce_scatter | solution.py:674
  402.5 45.7 %collective-permute-start.40 = (bf16[256,1024]{1,0:T(8,128)(2,1)S(1)}, bf16[256,1024]{1,0:T(8,128)(2,1)S(1)}, u32[]{:S(2)}, u32[]{:S(2)}) collective-permute-start(bf16[256,1024]{1,0:T(8,128)(2,1)S(1)} %copy-done.110), channel_id=1, source_target_pairs={{0,1},{1,0},{2,3},{3,2},{4,5},{5,4},{6,7},{7,6},{8,9},{9,8},{10,11... | collective-permute-start | bytes 1572872 | tf_op jit(solution)/shard_map/ppermute | solution.py:576
  403.4 44.8 %collective-permute-start.41 = (bf16[256,1024]{1,0:T(8,128)(2,1)S(1)}, bf16[256,1024]{1,0:T(8,128)(2,1)S(1)}, u32[]{:S(2)}, u32[]{:S(2)}) collective-permute-start(bf16[256,1024]{1,0:T(8,128)(2,1)S(1)} %copy-done.111), channel_id=1, source_target_pairs={{0,2},{1,3},{2,0},{3,1},{4,6},{5,7},{6,4},{7,5},{8,10},{9,11},{10,... | collective-permute-start | bytes 1572872 | tf_op jit(solution)/shard_map/ppermute | solution.py:576
  404.5 43.7 %collective-permute-start.42 = (bf16[256,1024]{1,0:T(8,128)(2,1)}, bf16[256,1024]{1,0:T(8,128)(2,1)S(1)}, u32[]{:S(2)}, u32[]{:S(2)}) collective-permute-start(bf16[256,1024]{1,0:T(8,128)(2,1)} %get-tuple-element.241), channel_id=1, source_target_pairs={{0,3},{1,2},{2,1},{3,0},{4,7},{5,6},{6,5},{7,4},{8,11},{9,10},{10,... | collective-permute-start | bytes 1572872 | tf_op jit(solution)/shard_map/ppermute | solution.py:576
  478.9 26.1 %collective-permute-start.50 = (bf16[256,1024]{1,0:T(8,128)(2,1)S(1)}, bf16[256,1024]{1,0:T(8,128)(2,1)S(1)}, u32[]{:S(2)}, u32[]{:S(2)}) collective-permute-start(bf16[256,1024]{1,0:T(8,128)(2,1)S(1)} %get-tuple-element.321.grad), channel_id=1, source_target_pairs={{0,3},{1,2},{2,1},{3,0},{4,7},{5,6},{6,5},{7,4},{8,11},{9,10},{10,... | collective-permute-start | bytes 1572872 | tf_op jit(solution)/shard_map/ppermute | solution.py:576
  483.3 37.9 %collective-permute-start.57 = (bf16[1024,768]{1,0:T(8,128)(2,1)}, bf16[1024,768]{1,0:T(8,128)(2,1)}, u32[]{:S(2)}, u32[]{:S(2)}) collective-permute-start(bf16[1024,768]{1,0:T(8,128)(2,1)} %convolution_convert_fusion.1), channel_id=1, source_target_pairs={{0,16},{16,0},{1,17},{17,1},{2,18},{18,2},{3,19},{19,3},{4,20},{20... | collective-permute-start | bytes 4718600 | tf_op jit(solution)/shard_map/ppermute | solution.py:571
  516.6 66.7 %collective-permute-start.52 = (bf16[1024,1152]{0,1:T(8,128)(2,1)S(1)}, bf16[1024,1152]{0,1:T(8,128)(2,1)}, u32[]{:S(2)}, u32[]{:S(2)}) collective-permute-start(bf16[1024,1152]{0,1:T(8,128)(2,1)S(1)} %pad_maximum_fusion.3), channel_id=1, source_target_pairs={{0,16},{16,0},{1,17},{17,1},{2,18},{18,2},{3,19},{19,3},{4,20},{20... | collective-permute-start | bytes 7077896 | tf_op jit(solution)/shard_map/ppermute | solution.py:571
  519.7 25.5 %collective-permute-start.49 = (bf16[256,1024]{1,0:T(8,128)(2,1)}, bf16[256,1024]{1,0:T(8,128)(2,1)}, u32[]{:S(2)}, u32[]{:S(2)}) collective-permute-start(bf16[256,1024]{1,0:T(8,128)(2,1)} %get-tuple-element.252), channel_id=1, source_target_pairs={{0,2},{1,3},{2,0},{3,1},{4,6},{5,7},{6,4},{7,5},{8,10},{9,11},{10,... | collective-permute-start | bytes 1572872 | tf_op jit(solution)/shard_map/ppermute | solution.py:576
  547.4 129.0 %reduce-scatter.9.cloned.1.call-start = ((), (), s32[]{:S(2)}) async-start(), calls=%async_computation.10 | async-start | bytes 3604480 | tf_op jit(solution)/shard_map/reduce_scatter | solution.py:674
  588.0 130.9 %reduce-scatter.11.cloned.1.call-start = ((), (), s32[]{:S(2)}) async-start(), calls=%async_computation.11 | async-start | bytes 1966080 | tf_op jit(solution)/shard_map/reduce_scatter | solution.py:674
  649.1 25.3 %collective-permute-start.60 = (bf16[256,1024]{1,0:T(8,128)(2,1)S(1)}, bf16[256,1024]{1,0:T(8,128)(2,1)S(1)}, u32[]{:S(2)}, u32[]{:S(2)}) collective-permute-start(bf16[256,1024]{1,0:T(8,128)(2,1)S(1)} %get-tuple-element.335), channel_id=1, source_target_pairs={{0,2},{1,3},{2,0},{3,1},{4,6},{5,7},{6,4},{7,5},{8,10},{9,11},{10,... | collective-permute-start | bytes 1572872 | tf_op jit(solution)/shard_map/ppermute | solution.py:576
  677.4 38.9 %collective-permute-start.72 = (bf16[256,1408]{0,1:T(8,128)(2,1)}, bf16[256,1408]{0,1:T(8,128)(2,1)}, u32[]{:S(2)}, u32[]{:S(2)}) collective-permute-start(bf16[256,1408]{0,1:T(8,128)(2,1)} %broadcast_select_fusion), channel_id=1, source_target_pairs={{0,16},{16,0},{1,17},{17,1},{2,18},{18,2},{3,19},{19,3},{4,20},{20... | collective-permute-start | bytes 2162696 | tf_op jit(solution)/shard_map/ppermute | solution.py:571
  (193 other events, 1986.3 us)
Sparse Core Ops, SparseCore 0:
  14.8 50.0 all-gather.4
  66.4 49.2 all-gather.6
  117.9 49.2 all-gather.8
  186.6 47.8 all-gather.10
  401.6 54.9 reduce-scatter.4
  547.5 34.0 reduce-scatter.6
  588.1 55.2 reduce-scatter.8
  678.1 36.6 reduce-scatter.10

commit v3 on v2

--- a/solution.py
+++ b/solution.py
@@ -9,7 +9,9 @@
 BLOCK = 64
 F32 = jnp.float32
 LOW = jnp.bfloat16
-VMEM_LIMIT = 56 * 1024 * 1024
+WIDTH = 8
+MIXER_VMEM = 56 * 1024 * 1024
+FFN_VMEM = 14 * 1024 * 1024
 
 
 def _dot(left, right, dims):
@@ -52,6 +54,13 @@
 
 def rowsum(array):
     return jnp.sum(array, axis=1, keepdims=True)
+
+
+def side_by_side(steps, width):
+    for first in range(0, len(steps), width):
+        running = steps[first : first + width]
+        while running:
+            running = [step for step in running if next(step, running) is not running]
 
 
 def unit_lower_inverses(belows, row, col):
@@ -116,42 +125,50 @@
     outs = (mixed_a, mixed_b)
     os = (o_a, o_b)
     prepared = {}
+
+    def prepare(head, block):
+        source = sources[head]
+        rows = pl.ds(block * BLOCK, BLOCK)
+        keep = 1.0 - meta[1 + step * groups + block].astype(F32)
+        own = source[rows, 0 : 4 * KEYS]
+        if block == 0:
+            before = carry[head]
+        else:
+            before = source[pl.ds(block * BLOCK - 8, 8), 0 : 4 * KEYS]
+        _, conv = convolve(own, before * keep, taps[head])
+        active = conv * jax.nn.sigmoid(conv)
+        yield
+        query, _ = unit(active[:, :KEYS])
+        query = query * KEYS ** (-0.5)
+        keys, _ = unit(active[:, KEYS : 2 * KEYS])
+        values = active[:, 2 * KEYS :]
+        yield
+        _, _, strength, cumlog, ratio = decay_of(
+            source[rows, 6 * KEYS : 6 * KEYS + 2], params[head, 0], params[head, 1], row, col
+        )
+        yield
+        gamma = jnp.exp(cumlog)
+        last = cumlog[BLOCK - 1 :]
+        both = mm_nt(jnp.concatenate([keys, query], axis=0), keys)
+        yield
+        below = jnp.where(row > col, strength * ratio * both[:BLOCK], 0.0)
+        scores = (both[BLOCK:] * ratio).astype(LOW)
+        tail = (keys * jnp.exp(last - cumlog)).astype(LOW)
+        prepared[block, head] = (
+            below,
+            ((strength * gamma) * keys).astype(LOW),
+            (strength * values).astype(LOW),
+            scores,
+            tail,
+            (query * gamma).astype(LOW),
+            jnp.exp(last),
+            keep,
+        )
+
+    places = [(block, head) for block in range(groups) for head in range(2)]
+    side_by_side([prepare(head, block) for block, head in places], WIDTH)
     for head in range(2):
-        source = sources[head]
-        for block in range(groups):
-            rows = pl.ds(block * BLOCK, BLOCK)
-            keep = 1.0 - meta[1 + step * groups + block].astype(F32)
-            own = source[rows, 0 : 4 * KEYS]
-            if block == 0:
-                before = carry[head]
-            else:
-                before = source[pl.ds(block * BLOCK - 8, 8), 0 : 4 * KEYS]
-            _, conv = convolve(own, before * keep, taps[head])
-            active = conv * jax.nn.sigmoid(conv)
-            query, _ = unit(active[:, :KEYS])
-            query = query * KEYS ** (-0.5)
-            keys, _ = unit(active[:, KEYS : 2 * KEYS])
-            values = active[:, 2 * KEYS :]
-            _, _, strength, cumlog, ratio = decay_of(
-                source[rows, 6 * KEYS : 6 * KEYS + 2], params[head, 0], params[head, 1], row, col
-            )
-            gamma = jnp.exp(cumlog)
-            last = cumlog[BLOCK - 1 :]
-            both = mm_nt(jnp.concatenate([keys, query], axis=0), keys)
-            below = jnp.where(row > col, strength * ratio * both[:BLOCK], 0.0)
-            scores = (both[BLOCK:] * ratio).astype(LOW)
-            tail = (keys * jnp.exp(last - cumlog)).astype(LOW)
-            prepared[block, head] = (
-                below,
-                ((strength * gamma) * keys).astype(LOW),
-                (strength * values).astype(LOW),
-                scores,
-                tail,
-                (query * gamma).astype(LOW),
-                jnp.exp(last),
-                keep,
-            )
-        carry[head] = source[pl.ds(groups * BLOCK - 8, 8), 0 : 4 * KEYS]
+        carry[head] = sources[head][pl.ds(groups * BLOCK - 8, 8), 0 : 4 * KEYS]
     order = list(prepared)
     solved = unit_lower_inverses([prepared[place][0] for place in order], row, col)
     for place, inverse in zip(order, solved):
@@ -214,66 +231,78 @@
     lower = jnp.where(row >= col, 1.0, 0.0)
     after = jnp.where(row > col, 1.0, 0.0)
     kept = {}
-    gain_total = jnp.zeros((1, 2 * KEYS), F32)
-    for head in range(2):
+    gain_parts = []
+    places = [(block, head) for block in range(groups) for head in range(2)]
+
+    def recompute(head, block):
         source = sources[head]
-        for block in range(groups):
-            rows = pl.ds(block * BLOCK, BLOCK)
-            keep = 1.0 - meta[1 + seq * groups + block].astype(F32)
-            own = source[rows, 0 : 4 * KEYS]
-            if block == 0:
-                before = edges[head][:, 0 : 4 * KEYS]
-            else:
-                before = source[pl.ds(block * BLOCK - 8, 8), 0 : 4 * KEYS]
-            shifted, conv = convolve(own, before * keep, taps[head])
-            sig = jax.nn.sigmoid(conv)
-            active = conv * sig
-            slope = sig * (1.0 + conv * (1.0 - sig))
-            query_unit, query_inv = unit(active[:, :KEYS])
-            query = query_unit * KEYS ** (-0.5)
-            keys, keys_inv = unit(active[:, KEYS : 2 * KEYS])
-            values = active[:, 2 * KEYS :]
-            decay_pre, log_decay, strength, cumlog, ratio = decay_of(
-                source[rows, 6 * KEYS : 6 * KEYS + 2], params[head, 0], params[head, 1], row, col
-            )
-            gamma = jnp.exp(cumlog)
-            last = cumlog[BLOCK - 1 :]
-            tail_scale = jnp.exp(last - cumlog)
-            both = mm_nt(jnp.concatenate([keys, query], axis=0), keys)
-            near = jnp.where(row > col, ratio * both[:BLOCK], 0.0)
-            scores = both[BLOCK:] * ratio
-            inverse = inverses[block, head]
-            held = states[block, head]
-            weight = mm(inverse, (strength * gamma) * keys).astype(LOW)
-            key_state = mm(keys, held)
-            lacking = values - gamma * key_state
-            fresh = mm(inverse, strength * lacking)
-            outcome = os[head][rows, :]
-            d_mixed = dms[head][rows, :]
-            gate = source[rows, 4 * KEYS : 6 * KEYS]
-            gate_sig = jax.nn.sigmoid(gate)
-            gate_act = gate * gate_sig
-            inv = lax.rsqrt(jnp.mean(outcome * outcome, axis=1, keepdims=True) + 1e-06)
-            normed = outcome * inv
-            weighted = d_mixed * gain[...]
-            d_gate = weighted * normed * (gate_sig * (1.0 + gate * (1.0 - gate_sig)))
-            dsts[head][rows, 4 * KEYS : 6 * KEYS] = d_gate.astype(LOW)
-            gain_total = gain_total + jnp.sum(d_mixed * normed * gate_act, axis=0, keepdims=True)
-            d_normed = weighted * gate_act
-            d_out = inv * (d_normed - normed * jnp.mean(d_normed * normed, axis=1, keepdims=True))
-            d_out_low = d_out.astype(LOW)
-            part_fresh = mm_tn(scores, d_out_low)
-            part_state = mm_tn(query * gamma, d_out_low)
-            tail = keys * tail_scale
-            kept[block, head] = dict(
-                keep=keep, shifted=shifted, slope=slope, query_unit=query_unit, query_inv=query_inv,
-                query=query, keys=keys, keys_inv=keys_inv, decay_pre=decay_pre, log_decay=log_decay,
-                strength=strength, ratio=ratio, gamma=gamma, last=jnp.exp(last), tail=tail,
-                tail_scale=tail_scale, near=near, scores=scores, inverse=inverse, held=held,
-                weight=weight, key_state=key_state, lacking=lacking, fresh=fresh,
-                d_out_low=d_out_low, part_fresh=part_fresh, part_state=part_state,
-            )
-    d_gain[...] += gain_total
+        rows = pl.ds(block * BLOCK, BLOCK)
+        keep = 1.0 - meta[1 + seq * groups + block].astype(F32)
+        own = source[rows, 0 : 4 * KEYS]
+        if block == 0:
+            before = edges[head][:, 0 : 4 * KEYS]
+        else:
+            before = source[pl.ds(block * BLOCK - 8, 8), 0 : 4 * KEYS]
+        shifted, conv = convolve(own, before * keep, taps[head])
+        sig = jax.nn.sigmoid(conv)
+        active = conv * sig
+        slope = sig * (1.0 + conv * (1.0 - sig))
+        yield
+        query_unit, query_inv = unit(active[:, :KEYS])
+        query = query_unit * KEYS ** (-0.5)
+        keys, keys_inv = unit(active[:, KEYS : 2 * KEYS])
+        values = active[:, 2 * KEYS :]
+        yield
+        decay_pre, log_decay, strength, cumlog, ratio = decay_of(
+            source[rows, 6 * KEYS : 6 * KEYS + 2], params[head, 0], params[head, 1], row, col
+        )
+        yield
+        gamma = jnp.exp(cumlog)
+        last = cumlog[BLOCK - 1 :]
+        tail_scale = jnp.exp(last - cumlog)
+        both = mm_nt(jnp.concatenate([keys, query], axis=0), keys)
+        yield
+        near = jnp.where(row > col, ratio * both[:BLOCK], 0.0)
+        scores = both[BLOCK:] * ratio
+        inverse = inverses[block, head]
+        held = states[block, head]
+        weight = mm(inverse, (strength * gamma) * keys).astype(LOW)
+        key_state = mm(keys, held)
+        yield
+        lacking = values - gamma * key_state
+        fresh = mm(inverse, strength * lacking)
+        yield
+        outcome = os[head][rows, :]
+        d_mixed = dms[head][rows, :]
+        gate = source[rows, 4 * KEYS : 6 * KEYS]
+        gate_sig = jax.nn.sigmoid(gate)
+        gate_act = gate * gate_sig
+        inv = lax.rsqrt(jnp.mean(outcome * outcome, axis=1, keepdims=True) + 1e-06)
+        normed = outcome * inv
+        yield
+        weighted = d_mixed * gain[...]
+        d_gate = weighted * normed * (gate_sig * (1.0 + gate * (1.0 - gate_sig)))
+        dsts[head][rows, 4 * KEYS : 6 * KEYS] = d_gate.astype(LOW)
+        gain_parts.append(jnp.sum(d_mixed * normed * gate_act, axis=0, keepdims=True))
+        yield
+        d_normed = weighted * gate_act
+        d_out = inv * (d_normed - normed * jnp.mean(d_normed * normed, axis=1, keepdims=True))
+        d_out_low = d_out.astype(LOW)
+        yield
+        part_fresh = mm_tn(scores, d_out_low)
+        part_state = mm_tn(query * gamma, d_out_low)
+        tail = keys * tail_scale
+        kept[block, head] = dict(
+            keep=keep, shifted=shifted, slope=slope, query_unit=query_unit, query_inv=query_inv,
+            query=query, keys=keys, keys_inv=keys_inv, decay_pre=decay_pre, log_decay=log_decay,
+            strength=strength, ratio=ratio, gamma=gamma, last=jnp.exp(last), tail=tail,
+            tail_scale=tail_scale, near=near, scores=scores, inverse=inverse, held=held,
+            weight=weight, key_state=key_state, lacking=lacking, fresh=fresh,
+            d_out_low=d_out_low, part_fresh=part_fresh, part_state=part_state,
+        )
+
+    side_by_side([recompute(head, block) for block, head in places], WIDTH)
+    d_gain[...] += sum(gain_parts)
     current = [state_grad[0], state_grad[1]]
     for block in reversed(range(groups)):
         for head in range(2):
@@ -285,67 +314,84 @@
             current[head] = below * k["keep"]
     state_grad[0] = current[0]
     state_grad[1] = current[1]
+
+    def differentiate(head, block):
+        rows = pl.ds(block * BLOCK, BLOCK)
+        k = kept[block, head]
+        keys, query, gamma, strength = k["keys"], k["query"], k["gamma"], k["strength"]
+        fresh_low = k["fresh"].astype(LOW)
+        ds_low = k["ds"].astype(LOW)
+        d_fill = mm_tn(k["inverse"], k["d_fresh"])
+        yield
+        grams = mm_nt(jnp.concatenate([d_fill.astype(LOW), k["d_out_low"]], axis=0), fresh_low)
+        yield
+        d_below = jnp.where(row > col, -grams[:BLOCK], 0.0)
+        d_scores = grams[BLOCK:]
+        d_tail = mm_nt(fresh_low, ds_low)
+        scaled = (strength * gamma) * d_fill
+        yield
+        through = mm_nt(jnp.concatenate([k["d_out_low"], scaled.astype(LOW)], axis=0), k["held"])
+        d_qk = (d_scores * k["ratio"]).astype(LOW)
+        d_kk = (strength * d_below * k["ratio"]).astype(LOW)
+        pair = mm(jnp.concatenate([d_qk, d_kk], axis=0), keys)
+        yield
+        d_query = gamma * through[:BLOCK] + pair[:BLOCK]
+        d_keys = (
+            pair[BLOCK:]
+            - through[BLOCK:]
+            + k["tail_scale"] * d_tail
+            + mm_tn(jnp.concatenate([d_qk, d_kk], axis=0), jnp.concatenate([query, keys], axis=0))
+        )
+        yield
+        d_values = strength * d_fill
+        d_strength = rowsum(d_fill * k["lacking"]) + rowsum(d_below * k["near"])
+        spread_grad = d_scores * k["scores"] + strength * d_below * k["near"]
+        tail_part = rowsum(d_tail * k["tail"])
+        d_cum = gamma * rowsum(query * through[:BLOCK]) - rowsum(scaled * k["key_state"]) - tail_part
+        at_last = jnp.sum(tail_part, axis=0, keepdims=True) + k["last"] * jnp.sum(
+            rowsum(k["ds"] * k["held"].astype(F32)), axis=0, keepdims=True
+        )
+        place = lax.broadcasted_iota(jnp.int32, (BLOCK, 1), 0)
+        d_cum = d_cum + jnp.where(place == BLOCK - 1, at_last, 0.0)
+        spread_grad = spread_grad + jnp.where(col == 0, d_cum, 0.0)
+        yield
+        d_log = rowsum(exact(lower, spread_grad, ((0,), (0,))) * after)
+        d_log = d_log + jnp.where(place == 0, jnp.sum(d_cum, axis=0, keepdims=True), 0.0)
+        yield
+        d_decay = d_log * (-params[head, 0]) * jax.nn.sigmoid(k["decay_pre"])
+        k["rate"] = jnp.sum(d_log * k["log_decay"], axis=0, keepdims=True)
+        k["bias"] = jnp.sum(d_decay, axis=0, keepdims=True)
+        d_write = d_strength * strength * (1.0 - strength)
+        lanes = lax.broadcasted_iota(jnp.int32, (BLOCK, KEYS), 1)
+        dsts[head][rows, 6 * KEYS : 7 * KEYS] = (
+            jnp.where(lanes == 0, d_decay, 0.0) + jnp.where(lanes == 1, d_write, 0.0)
+        ).astype(LOW)
+        yield
+        d_query = d_query * KEYS ** (-0.5)
+        unit_q = k["query_unit"]
+        d_active = jnp.concatenate(
+            [
+                k["query_inv"] * (d_query - unit_q * rowsum(unit_q * d_query)),
+                k["keys_inv"] * (d_keys - keys * rowsum(keys * d_keys)),
+                d_values,
+            ],
+            axis=1,
+        )
+        yield
+        d_conv = d_active * k["slope"]
+        k["d_conv"] = d_conv
+
+    side_by_side([differentiate(head, block) for block, head in reversed(places)], WIDTH)
     for head in range(2):
         next_rows = carry[head]
         taps_here = taps[head]
         tap_sums = [jnp.zeros((1, 4 * KEYS), F32) for _ in range(4)]
-        rate_sum = jnp.zeros((1, 1), F32)
-        bias_sum = jnp.zeros((1, 1), F32)
+        rate_sum = sum(kept[block, head]["rate"] for block in range(groups))
+        bias_sum = sum(kept[block, head]["bias"] for block in range(groups))
         for block in reversed(range(groups)):
             rows = pl.ds(block * BLOCK, BLOCK)
             k = kept[block, head]
-            keys, query, gamma, strength = k["keys"], k["query"], k["gamma"], k["strength"]
-            fresh_low = k["fresh"].astype(LOW)
-            ds_low = k["ds"].astype(LOW)
-            d_fill = mm_tn(k["inverse"], k["d_fresh"])
-            grams = mm_nt(jnp.concatenate([d_fill.astype(LOW), k["d_out_low"]], axis=0), fresh_low)
-            d_below = jnp.where(row > col, -grams[:BLOCK], 0.0)
-            d_scores = grams[BLOCK:]
-            d_tail = mm_nt(fresh_low, ds_low)
-            scaled = (strength * gamma) * d_fill
-            through = mm_nt(jnp.concatenate([k["d_out_low"], scaled.astype(LOW)], axis=0), k["held"])
-            d_qk = (d_scores * k["ratio"]).astype(LOW)
-            d_kk = (strength * d_below * k["ratio"]).astype(LOW)
-            pair = mm(jnp.concatenate([d_qk, d_kk], axis=0), keys)
-            d_query = gamma * through[:BLOCK] + pair[:BLOCK]
-            d_keys = (
-                pair[BLOCK:]
-                - through[BLOCK:]
-                + k["tail_scale"] * d_tail
-                + mm_tn(jnp.concatenate([d_qk, d_kk], axis=0), jnp.concatenate([query, keys], axis=0))
-            )
-            d_values = strength * d_fill
-            d_strength = rowsum(d_fill * k["lacking"]) + rowsum(d_below * k["near"])
-            spread_grad = d_scores * k["scores"] + strength * d_below * k["near"]
-            tail_part = rowsum(d_tail * k["tail"])
-            d_cum = gamma * rowsum(query * through[:BLOCK]) - rowsum(scaled * k["key_state"]) - tail_part
-            at_last = jnp.sum(tail_part, axis=0, keepdims=True) + k["last"] * jnp.sum(
-                rowsum(k["ds"] * k["held"].astype(F32)), axis=0, keepdims=True
-            )
-            place = lax.broadcasted_iota(jnp.int32, (BLOCK, 1), 0)
-            d_cum = d_cum + jnp.where(place == BLOCK - 1, at_last, 0.0)
-            spread_grad = spread_grad + jnp.where(col == 0, d_cum, 0.0)
-            d_log = rowsum(exact(lower, spread_grad, ((0,), (0,))) * after)
-            d_log = d_log + jnp.where(place == 0, jnp.sum(d_cum, axis=0, keepdims=True), 0.0)
-            d_decay = d_log * (-params[head, 0]) * jax.nn.sigmoid(k["decay_pre"])
-            rate_sum = rate_sum + jnp.sum(d_log * k["log_decay"], axis=0, keepdims=True)
-            bias_sum = bias_sum + jnp.sum(d_decay, axis=0, keepdims=True)
-            d_write = d_strength * strength * (1.0 - strength)
-            lanes = lax.broadcasted_iota(jnp.int32, (BLOCK, KEYS), 1)
-            dsts[head][rows, 6 * KEYS : 7 * KEYS] = (
-                jnp.where(lanes == 0, d_decay, 0.0) + jnp.where(lanes == 1, d_write, 0.0)
-            ).astype(LOW)
-            d_query = d_query * KEYS ** (-0.5)
-            unit_q = k["query_unit"]
-            d_active = jnp.concatenate(
-                [
-                    k["query_inv"] * (d_query - unit_q * rowsum(unit_q * d_query)),
-                    k["keys_inv"] * (d_keys - keys * rowsum(keys * d_keys)),
-                    d_values,
-                ],
-                axis=1,
-            )
-            d_conv = d_active * k["slope"]
+            d_conv = k["d_conv"]
             padded = jnp.concatenate([d_conv, next_rows], axis=0)
             d_own = taps_here[0:1] * d_conv
             tap_sums[0] = tap_sums[0] + jnp.sum(d_conv * k["shifted"][0], axis=0, keepdims=True)
@@ -411,7 +457,7 @@
             jax.ShapeDtypeStruct((count, half), LOW),
             jax.ShapeDtypeStruct((count, width), LOW),
         ],
-        compiler_params=pltpu.CompilerParams(vmem_limit_bytes=VMEM_LIMIT),
+        compiler_params=pltpu.CompilerParams(vmem_limit_bytes=FFN_VMEM),
         name="ffn_forward",
     )(rows, *weights)
 
@@ -426,7 +472,7 @@
             jax.ShapeDtypeStruct((count, 2 * half), LOW),
             jax.ShapeDtypeStruct((count, width), LOW),
         ],
-        compiler_params=pltpu.CompilerParams(vmem_limit_bytes=VMEM_LIMIT),
+        compiler_params=pltpu.CompilerParams(vmem_limit_bytes=FFN_VMEM),
         name="ffn_backward",
     )(grad, *pair, *weights)
 
@@ -487,7 +533,7 @@
             jax.ShapeDtypeStruct((rows // BLOCK, 2, BLOCK, BLOCK), LOW),
             jax.ShapeDtypeStruct((rows, width), LOW),
         ],
-        compiler_params=pltpu.CompilerParams(vmem_limit_bytes=VMEM_LIMIT),
+        compiler_params=pltpu.CompilerParams(vmem_limit_bytes=MIXER_VMEM),
         name="mixer_forward",
     )(meta, params, normed, *weights, taps, gain)
 
@@ -559,7 +605,7 @@
             jax.ShapeDtypeStruct((rows, width), LOW),
             jax.ShapeDtypeStruct((1, width), F32),
         ],
-        compiler_params=pltpu.CompilerParams(vmem_limit_bytes=VMEM_LIMIT),
+        compiler_params=pltpu.CompilerParams(vmem_limit_bytes=MIXER_VMEM),
         name="mixer_backward",
     )(
         meta, params, mine, other, mine, other, o_a, o_b, normed, d_branch, states, inverses,
@@ -638,12 +684,12 @@
     mine, other, mixed_a, mixed_b, o_a, o_b, states, inverses, branch = mixer_forward(
         meta, params, normed_all, mix_weights, taps, gain_out, peers
     )
-    ffn_weights = between[0](branch)
     if last is not None:
         branch, last = lax.optimization_barrier((branch, last))
     branch = collect_rows(split_rows(branch, peers))
     after = hidden + live * branch
     normed_two, inv_two = norm_forward(after, gains[1])
+    ffn_weights = between(normed_two)
     normed_two_all = spread_rows(normed_two)
     ups, actives, ffn = [], [], []
     for place, chunk in enumerate(normed_two_all):
@@ -653,7 +699,6 @@
         ups.append((u_a, u_b))
         actives.append((act_a, act_b))
         ffn.append(partial)
-    between[1](ffn[-1])
     kept = (
         hidden, inv_one, normed_all, mine, other, o_a, o_b, states, inverses, mixed_a, mixed_b,
         after, inv_two, normed_two_all, ups, actives,
@@ -672,6 +717,23 @@
 
 def scatter(total):
     return lax.psum_scatter(total, "dp", scatter_dimension=0, tiled=True)
+
+
+def scatter_direct(total):
+    peers = lax.axis_size("dp")
+    me = lax.axis_index("dp")
+    size = total.shape[0] // peers
+
+    def part(owner):
+        return lax.dynamic_slice_in_dim(total, owner * size, size, 0)
+
+    result = part(me).astype(F32)
+    for k in range(1, peers):
+        sent = part((me + k) % peers)
+        result = result + lax.ppermute(
+            sent, "dp", [(i, (i + k) % peers) for i in range(peers)]
+        ).astype(F32)
+    return result.astype(LOW)
 
 
 def exchange_sum(array, axis):
@@ -722,19 +784,29 @@
     waiting = beside(waiting)
     inward, waiting = lax.optimization_barrier((inward, waiting))
     mix_total = share(tn(normed_all, d_mine[:, : 6 * KEYS]), tn(normed_all, d_other[:, : 6 * KEYS]))
-    if final:
-        inward, mix_total = lax.optimization_barrier((inward, mix_total))
-    back_one = collect_rows(split_rows(inward, peers))
-    early_owned, mix_total = lax.optimization_barrier((early_owned, mix_total))
-    mix_owned = scatter(mix_total)
     pairs = jnp.concatenate([d[:, 6 * KEYS : 6 * KEYS + 2] for d in (d_mine, d_other)], axis=1)
     decay_grad = tn(pairs, normed_all)
     gain_one_grad = gain_one_grad[0] / gains[0]
+    small_grads = (jnp.stack([gain_one_grad, gain_two_grad]), d_taps, d_params, d_gain, decay_grad)
+    early_owned, mix_total = lax.optimization_barrier((early_owned, mix_total))
+    if final is not None:
+        early_owned, mix_total, inward, small_grads = lax.optimization_barrier(
+            (early_owned, mix_total, inward, small_grads)
+        )
+    if final is None:
+        mix_owned = scatter(mix_total)
+    else:
+        (own, pairs), mix_total = lax.optimization_barrier((final(small_grads), mix_total))
+        mix_owned = scatter_direct(mix_total)
+        small_grads, inward = lax.optimization_barrier(
+            ((exchange_sum(own, "tensor"), pairs), inward)
+        )
+    back_one = collect_rows(split_rows(inward, peers))
     back, _ = norm_backward(hidden, inv_one, gains[0], back_one)
     return (
         grad_after + back,
         [early_owned, mix_owned],
-        (jnp.stack([gain_one_grad, gain_two_grad]), *lax.optimization_barrier((d_taps, d_params, d_gain, decay_grad, mix_total))[:4]),
+        small_grads,
         waiting,
     )
 
@@ -842,31 +914,52 @@
     mix_pair = (mix_full, swap_section(mix_full))
     held = {}
 
-    def first_mixed(branch):
-        held["mix"], full, _ = gather(mix_shards[1], ffn_full, branch)
+    def first_mixed(normed):
+        held["mix"], full, _ = gather(mix_shards[1], ffn_full, normed)
         return full, swap_section(full)
 
-    def first_done(partial):
-        held["ffn"], held["mix"], _ = gather(ffn_shards[1], held["mix"], partial)
-
-    def second_mixed(branch):
+    def second_mixed(normed):
         return held["ffn"], swap_section(held["ffn"])
 
-    def second_done(partial):
-        pass
-
     ffn, saved, _, weights_one = layer_forward(
-        hidden, mix_pair, gains_all[0], smalls[0], meta, live, (first_mixed, first_done), None
+        hidden, mix_pair, gains_all[0], smalls[0], meta, live, first_mixed, None
     )
     kept = [saved]
-    hidden = finish_forward(saved[11], live, ffn).astype(F32)
+    hidden = finish_forward(saved[11], live, ffn)
+    held["ffn"], held["mix"], _ = gather(ffn_shards[1], held["mix"], hidden)
+    hidden = hidden.astype(F32)
     mix_pair = (held["mix"], swap_section(held["mix"]))
     ffn_last, saved, spread, weights_two = layer_forward(
-        hidden, mix_pair, gains_all[1], smalls[1], meta, live, (second_mixed, second_done),
+        hidden, mix_pair, gains_all[1], smalls[1], meta, live, second_mixed,
         (live * own_micro(cotangent)).astype(LOW),
     )
     kept.append(saved)
     weights = [weights_one, weights_two]
+
+    def sum_small(last):
+        flat = []
+        for gain_grads, d_taps, d_params, d_gain, _ in (last, small_grads[1]):
+            conv_full = jnp.zeros(conv_weight.shape[1:], F32)
+            pair_full = jnp.zeros((heads, 2), F32)
+            for side, p in enumerate(places):
+                conv_full = lax.dynamic_update_slice_in_dim(conv_full, d_taps[side][:, None, :], p, 1)
+                pair_full = lax.dynamic_update_slice_in_dim(
+                    pair_full, d_params[side : side + 1, :2], p, 0
+                )
+            flat.append(
+                jnp.concatenate(
+                    [
+                        conv_full.reshape(-1), pair_full[:, 0], pair_full[:, 1], d_gain.reshape(-1),
+                        gain_grads.reshape(-1),
+                    ]
+                )
+            )
+        pairs = jnp.stack([last[4], small_grads[1][4]])
+        sent = jnp.concatenate([jnp.where(first, flat[1], flat[0]), pairs[:, 2:].reshape(-1)])
+        kept_here = jnp.concatenate([jnp.where(first, flat[0], flat[1]), pairs[:, :2].reshape(-1)])
+        total = exchange_sum(kept_here + swap_section(sent), "dp")
+        size = flat[0].size
+        return total[:size], total[size:]
 
     grad = own_micro(cotangent)
     owned, small_grads = [None, None], [None, None]
@@ -876,7 +969,7 @@
             grad, kept[layer], weights[layer], gains_all[layer], smalls[layer], meta, live,
             spread if layer == 1 else None, waiting,
             (lambda parts: finish_forward(kept[1][11], live, parts)) if layer == 1 else (lambda x: x),
-            layer == 0,
+            sum_small if layer == 0 else None,
         )
         if layer == 0:
             owned[1] = waiting
@@ -885,57 +978,35 @@
         grad_low = grad.astype(LOW)
         grad = grad_low.astype(F32)
 
-    halves = []
-    for kind in range(2):
+    def own_halves(kind):
         keep = jnp.where(first, owned[0][kind], owned[1][kind])
         got = swap_section(jnp.where(first, owned[1][kind], owned[0][kind]))
-        halves.append(
-            (
-                jnp.where(first, keep, got).astype(F32),
-                jnp.where(first, got, keep).astype(F32),
-            )
-        )
-    early_pair, mix_pair = halves
+        return (
+            jnp.where(first, keep, got).astype(F32),
+            jnp.where(first, got, keep).astype(F32),
+        )
 
     def columns(pair, start, size):
         return jnp.concatenate([side[:, start : start + size] for side in pair], axis=1)
 
+    early_pair = own_halves(0)
     grad_updown = jnp.stack([columns(early_pair, 0, half), columns(early_pair, wide, half)], axis=1)
     grad_down = columns(early_pair, 2 * wide, half).T
     grad_out = columns(early_pair, 3 * wide, vals).T
+    own, pairs = small_grads[0]
+    pairs = lax.dynamic_slice_in_dim(
+        pairs.reshape(2, 2, -1), lax.axis_index("dp") * w_query.shape[1], w_query.shape[1], 2
+    )
+    mix_pair = own_halves(1)
     grad_query = columns(mix_pair, 0, KEYS)
     grad_key = columns(mix_pair, KEYS, KEYS)
     grad_value = columns(mix_pair, 2 * KEYS, vals)
     grad_gate = columns(mix_pair, vals + 2 * KEYS, vals)
 
-    pairs = jnp.stack([small_grads[layer][4] for layer in range(2)])
-    pairs = exchange_sum(pairs[:, :2] + swap_section(pairs[:, 2:]), "dp")
-    pairs = lax.dynamic_slice_in_dim(
-        pairs, lax.axis_index("dp") * w_query.shape[1], w_query.shape[1], 2
-    )
     keep = jnp.where(first, pairs[0], pairs[1])
     got = swap_section(jnp.where(first, pairs[1], pairs[0]))
     grad_decay = jnp.concatenate([jnp.where(first, keep, got), jnp.where(first, got, keep)], axis=0).T
 
-    flat = []
-    for layer in range(2):
-        gain_grads, d_taps, d_params, d_gain, _ = small_grads[layer]
-        conv_full = jnp.zeros(conv_weight.shape[1:], F32)
-        pair_full = jnp.zeros((heads, 2), F32)
-        for side, p in enumerate(places):
-            conv_full = lax.dynamic_update_slice_in_dim(conv_full, d_taps[side][:, None, :], p, 1)
-            pair_full = lax.dynamic_update_slice_in_dim(pair_full, d_params[side : side + 1, :2], p, 0)
-        flat.append(
-            jnp.concatenate(
-                [
-                    conv_full.reshape(-1), pair_full[:, 0], pair_full[:, 1], d_gain.reshape(-1),
-                    gain_grads.reshape(-1),
-                ]
-            )
-        )
-    got = swap_section(jnp.where(first, flat[1], flat[0]))
-    own = jnp.where(first, flat[0], flat[1]) + got
-    own = exchange_sum(exchange_sum(own, "tensor"), "dp")
     pieces = [own[a:b] for a, b in zip(edges[:-1], edges[1:])]
     return (
         result_low[None],

time: 744 us -> 727 us (0.977)
  Pallas kernels: 226 us -> 174 us
  waiting for transfers between devices: 279 us -> 297 us
  local copies, waits for them, and re-layouts: 48.8 us -> 64 us
  other arithmetic: 50.8 us -> 64.3 us
    pallas_call x8, Pallas kernels: 47.9 us -> 26.7 us  [ffn_backward(): pl.pallas_call(ffn_backward_kernel, out_shape=[jax.ShapeDtypeStruct((coun...]
    ppermute x0 -> x3, waiting for transfers between devices: none -> 19.4 us  [scatter_direct(): lax.ppermute(sent, 'dp', [(i, (i + k) % peers) for i in range(peers)])]
    pallas_call x8, Pallas kernels: 40.2 us -> 22 us  [ffn_forward(): pl.pallas_call(ffn_forward_kernel, out_shape=[jax.ShapeDtypeStruct((count...]
    pallas_call x2, Pallas kernels: 83.8 us -> 69.7 us  [mixer_backward(): pl.pallas_call(mixer_backward_kernel, grid_spec=pltpu.PrefetchScalarGridS...]
    ppermute x48, waiting for transfers between devices: 205 us -> 217 us  [send_by(): lax.ppermute(array, 'tensor', [(i, i ^ offset) for i in range(peers)])]
    all_gather x4, waiting for transfers between devices: 54.1 us -> 45.4 us  [gather(): full = lax.all_gather(shard, 'dp', axis=0, tiled=True)]
    ppermute x6 -> x4, waiting for transfers between devices: 16.6 us -> 9.37 us  [exchange_sum(): lax.ppermute(array, axis, [(i, i ^ offset) for i in range(peers)])]
    unnamed x310 -> x276, local copies, waits for them, and re-layouts: 25.3 us -> 26.9 us
  transfers between devices with their start and end apart: 81 -> 80, of which waited for: 33 -> 37; matrix products, arithmetic and copies ran while one was open for 14% -> 17% of each run, Pallas kernels for 30% -> 24%
where the time goes in v3:
time: 727 us; the launch traced here: 717 us
  waiting for transfers between devices  297 us (41%)
  Pallas kernels  174 us (24%)
  starting transfers between devices  68.5 us (9%)
  other arithmetic  64.3 us (9%)
  local copies, waits for them, and re-layouts  64 us (9%)
  matrix products  32.4 us (4%)
  between operations  16.6 us (2%)
    ppermute x48, waiting for transfers between devices, send_by(): lax.ppermute(array, 'tensor', [(i, i ^ offset) for i in range(peers)])  217 us
    pallas_call x2, Pallas kernels, mixer_backward(): pl.pallas_call(mixer_backward_kernel, grid_spec=pltpu.PrefetchScalarGridS...  69.7 us
    pallas_call x2, Pallas kernels, mixer_forward(): pl.pallas_call(mixer_forward_kernel, grid_spec=pltpu.PrefetchScalarGridSp...  55.9 us
    ppermute x48, starting transfers between devices, send_by(): lax.ppermute(array, 'tensor', [(i, i ^ offset) for i in range(peers)])  55.3 us
    all_gather x4, waiting for transfers between devices, gather(): full = lax.all_gather(shard, 'dp', axis=0, tiled=True)  45.4 us
    dot_general x18, matrix products, tn(): lax.dot_general(left, right, (((0,), (0,)), ((), ())), preferred_element_...  32.4 us
    unnamed x276, local copies, waits for them, and re-layouts  26.9 us
    pallas_call x8, Pallas kernels, ffn_backward(): pl.pallas_call(ffn_backward_kernel, out_shape=[jax.ShapeDtypeStruct((coun...  26.7 us
  transfers between devices with their start and end apart: 80, of which 37 were waited for; matrix products, arithmetic and copies ran while one was open for 17% of the time, Pallas kernels for 24%

profile of v3, /device:TPU:8, one launch (start us, length us, event | category | flops | bytes accessed | tf_op | source)
XLA Modules:
  0.0 717.1 jit_solution(9266902329652874211)
XLA Ops:
  30.4 34.5 %all-gather.5.cloned.1.call-done.mix_mine = bf16[1024,1152]{1,0:T(8,128)(2,1)} async-done(((bf16[256,1152]{1,0:T(8,128)(2,1)}), bf16[1024,1152]{1,0:T(8,128)(2,1)}) %all-gather.5.cloned.1.call-update) | async-done | bytes 2359312 | tf_op jit(solution)/shard_map/all_gather | solution.py:871
  78.7 27.8 %mixer_forward.2 = (f32[1024,896]{1,0:T(8,128)}, f32[1024,896]{1,0:T(8,128)}, bf16[1024,256]{1,0:T(8,128)(2,1)}, bf16[1024,256]{1,0:T(8,128)(2,1)}, f32[1024,256...) custom-call(s32[17]{0:T(128)} %pad_add_fusion.meta, ...), custom_call_target="tpu_custom_call" | custom-call | tf_op jit(solution)/shard_map/mixer_forward/pallas_call | solution.py:500
  113.8 11.1 %collective-permute-done.10 = bf16[256,1024]{1,0:T(8,128)(2,1)S(1)} collective-permute-done((bf16[256,1024]{1,0:T(8,128)(2,1)}, bf16[256,1024]{1,0:T(8,128)(2,1)S(1)}, u32[]{:S(2)}, u32[]{:S(2)}) %collective-permute-start.10) | collective-permute-done | bytes 524320 | tf_op jit(solution)/shard_map/ppermute | solution.py:622
  124.8 10.7 %collective-permute-done.8 = bf16[256,1024]{1,0:T(8,128)(2,1)S(1)} collective-permute-done((bf16[256,1024]{1,0:T(8,128)(2,1)}, bf16[256,1024]{1,0:T(8,128)(2,1)S(1)}, u32[]{:S(2)}, u32[]{:S(2)}) %collective-permute-start.8) | collective-permute-done | bytes 524320 | tf_op jit(solution)/shard_map/ppermute | solution.py:622
  158.3 7.1 collective-permute-done.13.rows
  177.1 12.3 %collective-permute-done.17 = bf16[256,1024]{1,0:T(8,128)(2,1)S(1)} collective-permute-done((bf16[256,1024]{1,0:T(8,128)(2,1)S(1)}, bf16[256,1024]{1,0:T(8,128)(2,1)S(1)}, u32[]{:S(2)}, u32[]{:S(2)}) %collective-permute-start.17) | collective-permute-done | bytes 524320 | tf_op jit(solution)/shard_map/ppermute | solution.py:622
  189.4 7.7 %collective-permute-done.16 = bf16[256,1024]{1,0:T(8,128)(2,1)S(1)} collective-permute-done((bf16[256,1024]{1,0:T(8,128)(2,1)S(1)}, bf16[256,1024]{1,0:T(8,128)(2,1)S(1)}, u32[]{:S(2)}, u32[]{:S(2)}) %collective-permute-start.16) | collective-permute-done | bytes 524320 | tf_op jit(solution)/shard_map/ppermute | solution.py:622
  208.4 10.9 %collective-permute-done.18 = bf16[256,1024]{1,0:T(8,128)(2,1)} collective-permute-done((bf16[256,1024]{1,0:T(8,128)(2,1)}, bf16[256,1024]{1,0:T(8,128)(2,1)}, u32[]{:S(2)}, u32[]{:S(2)}) %collective-permute-start.18) | collective-permute-done | bytes 524320 | tf_op jit(solution)/shard_map/ppermute | solution.py:622
  219.3 10.8 %collective-permute-done.20 = bf16[256,1024]{1,0:T(8,128)(2,1)} collective-permute-done((bf16[256,1024]{1,0:T(8,128)(2,1)}, bf16[256,1024]{1,0:T(8,128)(2,1)}, u32[]{:S(2)}, u32[]{:S(2)}) %collective-permute-start.20) | collective-permute-done | bytes 524320 | tf_op jit(solution)/shard_map/ppermute | solution.py:622
  237.6 10.9 %all-gather.11.cloned.1.call-done.mine = bf16[1024,1152]{1,0:T(8,128)(2,1)} async-done(((bf16[256,1152]{1,0:T(8,128)(2,1)}), bf16[1024,1152]{1,0:T(8,128)(2,1)}) %all-gather.11.cloned.1.call-update) | async-done | bytes 2359312 | tf_op jit(solution)/shard_map/all_gather | solution.py:871
  250.6 28.2 %mixer_forward.3 = (f32[1024,896]{1,0:T(8,128)}, f32[1024,896]{1,0:T(8,128)}, bf16[1024,256]{1,0:T(8,128)(2,1)}, bf16[1024,256]{1,0:T(8,128)(2,1)}, f32[1024,256...) custom-call(s32[17]{0:T(128)} %pad_add_fusion.meta, ...), custom_call_target="tpu_custom_call" | custom-call | tf_op jit(solution)/shard_map/mixer_forward/pallas_call | solution.py:500
  284.0 11.2 %collective-permute-done.25 = bf16[256,1024]{1,0:T(8,128)(2,1)S(1)} collective-permute-done((bf16[256,1024]{1,0:T(8,128)(2,1)S(1)}, bf16[256,1024]{1,0:T(8,128)(2,1)S(1)}, u32[]{:S(2)}, u32[]{:S(2)}) %collective-permute-start.25) | collective-permute-done | bytes 524320 | tf_op jit(solution)/shard_map/ppermute | solution.py:622
  295.2 12.0 %collective-permute-done.26 = bf16[256,1024]{1,0:T(8,128)(2,1)S(1)} collective-permute-done((bf16[256,1024]{1,0:T(8,128)(2,1)S(1)}, bf16[256,1024]{1,0:T(8,128)(2,1)S(1)}, u32[]{:S(2)}, u32[]{:S(2)}) %collective-permute-start.26) | collective-permute-done | bytes 524320 | tf_op jit(solution)/shard_map/ppermute | solution.py:622
  319.1 4.8 collective-permute-done.28.rows
  328.0 6.7 collective-permute-done.29.rows
  373.4 11.4 %collective-permute-done.36 = bf16[256,1024]{1,0:T(8,128)(2,1)S(1)} collective-permute-done((bf16[256,1024]{1,0:T(8,128)(2,1)S(1)}, bf16[256,1024]{1,0:T(8,128)(2,1)S(1)}, u32[]{:S(2)}, u32[]{:S(2)}) %collective-permute-start.36) | collective-permute-done | bytes 524320 | tf_op jit(solution)/shard_map/ppermute | solution.py:622
  384.8 8.9 %collective-permute-done.37 = bf16[256,1024]{1,0:T(8,128)(2,1)S(1)} collective-permute-done((bf16[256,1024]{1,0:T(8,128)(2,1)S(1)}, bf16[256,1024]{1,0:T(8,128)(2,1)S(1)}, u32[]{:S(2)}, u32[]{:S(2)}) %collective-permute-start.37) | collective-permute-done | bytes 524320 | tf_op jit(solution)/shard_map/ppermute | solution.py:622
  404.9 34.9 %mixer_backward.2 = (bf16[1024,896]{1,0:T(8,128)(2,1)}, bf16[1024,896]{1,0:T(8,128)(2,1)}, f32[2,4,512]{2,1,0:T(4,128)}, f32[1,256]{1,0:T(1,128)}, f32[2,128]{1,...) custom-call(s32[17]{0:T(128)} %pad_add_fusion.meta, f32[2,2]{1,0:T(2,128)} %pad_maximum_fusion.21.params, ...), custom_call_target="tpu_custom_call" | custom-call | tf_op jit(solution)/shard_map/mixer_backward/pallas_call | solution.py:562
  445.4 11.4 %collective-permute-done.43 = bf16[256,1024]{1,0:T(8,128)(2,1)S(1)} collective-permute-done((bf16[256,1024]{1,0:T(8,128)(2,1)S(1)}, bf16[256,1024]{1,0:T(8,128)(2,1)S(1)}, u32[]{:S(2)}, u32[]{:S(2)}) %collective-permute-start.43) | collective-permute-done | bytes 524320 | tf_op jit(solution)/shard_map/ppermute | solution.py:622
  456.7 10.9 %collective-permute-done.44 = bf16[256,1024]{1,0:T(8,128)(2,1)S(1)} collective-permute-done((bf16[256,1024]{1,0:T(8,128)(2,1)S(1)}, bf16[256,1024]{1,0:T(8,128)(2,1)S(1)}, u32[]{:S(2)}, u32[]{:S(2)}) %collective-permute-start.44) | collective-permute-done | bytes 524320 | tf_op jit(solution)/shard_map/ppermute | solution.py:622
  477.3 7.1 collective-permute-done.46.grad
  488.1 5.4 collective-permute-done.48.grad
  512.7 8.4 %collective-permute-done.47 = bf16[256,1024]{1,0:T(8,128)(2,1)S(1)} collective-permute-done((bf16[256,1024]{1,0:T(8,128)(2,1)}, bf16[256,1024]{1,0:T(8,128)(2,1)S(1)}, u32[]{:S(2)}, u32[]{:S(2)}) %collective-permute-start.47) | collective-permute-done | bytes 524320 | tf_op jit(solution)/shard_map/ppermute | solution.py:622
  521.1 12.1 %collective-permute-done.49 = bf16[256,1024]{1,0:T(8,128)(2,1)} collective-permute-done((bf16[256,1024]{1,0:T(8,128)(2,1)}, bf16[256,1024]{1,0:T(8,128)(2,1)}, u32[]{:S(2)}, u32[]{:S(2)}) %collective-permute-start.49) | collective-permute-done | bytes 524320 | tf_op jit(solution)/shard_map/ppermute | solution.py:622
  542.1 11.4 %collective-permute-done.53 = bf16[256,1024]{1,0:T(8,128)(2,1)S(1)} collective-permute-done((bf16[256,1024]{1,0:T(8,128)(2,1)S(1)}, bf16[256,1024]{1,0:T(8,128)(2,1)S(1)}, u32[]{:S(2)}, u32[]{:S(2)}) %collective-permute-start.53) | collective-permute-done | bytes 524320 | tf_op jit(solution)/shard_map/ppermute | solution.py:622
  553.5 10.1 %collective-permute-done.54 = bf16[256,1024]{1,0:T(8,128)(2,1)S(1)} collective-permute-done((bf16[256,1024]{1,0:T(8,128)(2,1)S(1)}, bf16[256,1024]{1,0:T(8,128)(2,1)S(1)}, u32[]{:S(2)}, u32[]{:S(2)}) %collective-permute-start.54) | collective-permute-done | bytes 524320 | tf_op jit(solution)/shard_map/ppermute | solution.py:622
  577.0 34.8 %mixer_backward.3 = (bf16[1024,896]{1,0:T(8,128)(2,1)}, bf16[1024,896]{1,0:T(8,128)(2,1)}, f32[2,4,512]{2,1,0:T(4,128)}, f32[1,256]{1,0:T(1,128)}, f32[2,128]{1,...) custom-call(s32[17]{0:T(128)} %pad_add_fusion.meta, f32[2,2]{1,0:T(2,128)} %pad_maximum_fusion.23.params, ...), custom_call_target="tpu_custom_call" | custom-call | tf_op jit(solution)/shard_map/mixer_backward/pallas_call | solution.py:562
  611.8 4.5 convolution_convert_fusion
  624.3 4.5 add_convert_fusion
  671.6 12.3 %collective-permute-done.67 = bf16[256,768]{1,0:T(8,128)(2,1)} collective-permute-done((bf16[256,768]{1,0:T(8,128)(2,1)}, bf16[256,768]{1,0:T(8,128)(2,1)}, u32[]{:S(2)}, u32[]{:S(2)}) %collective-permute-start.67) | collective-permute-done | bytes 393248 | tf_op jit(solution)/shard_map/ppermute | solution.py:733
  684.4 5.2 collective-permute-done.68
  698.5 6.0 collective-permute-done.65
  (618 shorter events, 294.8 us)
Async XLA Ops:
  7.2 57.7 %all-gather.5.cloned.1.call-start = ((), (), s32[]{:S(2)}) async-start(), calls=%async_computation.3 | async-start | bytes 2949120 | tf_op jit(solution)/shard_map/all_gather | solution.py:871
  14.6 123.7 %all-gather.7.cloned.1.call-start = ((), (), s32[]{:S(2)}) async-start(), calls=%async_computation.4 | async-start | bytes 2949120 | tf_op jit(solution)/shard_map/all_gather | solution.py:871
  15.1 49.9 %collective-permute-start = (f32[1,16656]{1,0:T(1,128)S(1)}, f32[1,16656]{1,0:T(1,128)}, u32[]{:S(2)}, u32[]{:S(2)}) collective-permute-start(f32[1,16656]{1,0:T(1,128)S(1)} %broadcast_in_dim.60), channel_id=1, source_target_pairs={{0,16},{16,0},{1,17},{17,1},{2,18},{18,2},{3,19},{19,3},{4,20},{20... | collective-permute-start | bytes 199880 | tf_op jit(solution)/shard_map/ppermute | solution.py:617
  25.7 48.4 %collective-permute-start.2 = (bf16[256,1024]{1,0:T(8,128)(2,1)}, bf16[256,1024]{1,0:T(8,128)(2,1)}, u32[]{:S(2)}, u32[]{:S(2)}) collective-permute-start(bf16[256,1024]{1,0:T(8,128)(2,1)} %fusion.46), channel_id=1, source_target_pairs={{0,1},{1,0},{2,3},{3,2},{4,5},{5,4},{6,7},{7,6},{8,9},{9,8},{10,11... | collective-permute-start | bytes 1572872 | tf_op jit(solution)/shard_map/ppermute | solution.py:622
  27.2 46.9 %collective-permute-start.3 = (bf16[256,1024]{1,0:T(8,128)(2,1)}, bf16[256,1024]{1,0:T(8,128)(2,1)}, u32[]{:S(2)}, u32[]{:S(2)}) collective-permute-start(bf16[256,1024]{1,0:T(8,128)(2,1)} %fusion.46), channel_id=1, source_target_pairs={{0,2},{1,3},{2,0},{3,1},{4,6},{5,7},{6,4},{7,5},{8,10},{9,11},{10,... | collective-permute-start | bytes 1572872 | tf_op jit(solution)/shard_map/ppermute | solution.py:622
  28.7 45.4 %collective-permute-start.4 = (bf16[256,1024]{1,0:T(8,128)(2,1)}, bf16[256,1024]{1,0:T(8,128)(2,1)}, u32[]{:S(2)}, u32[]{:S(2)}) collective-permute-start(bf16[256,1024]{1,0:T(8,128)(2,1)} %fusion.46), channel_id=1, source_target_pairs={{0,3},{1,2},{2,1},{3,0},{4,7},{5,6},{6,5},{7,4},{8,11},{9,10},{10,... | collective-permute-start | bytes 1572872 | tf_op jit(solution)/shard_map/ppermute | solution.py:622
  64.9 135.9 %all-gather.9.cloned.1.call-start = ((), (), s32[]{:S(2)}) async-start(), calls=%async_computation.5 | async-start | bytes 2949120 | tf_op jit(solution)/shard_map/all_gather | solution.py:871
  138.4 110.2 %all-gather.11.cloned.1.call-start = ((), (), s32[]{:S(2)}) async-start(), calls=%async_computation.6 | async-start | bytes 2949120 | tf_op jit(solution)/shard_map/all_gather | solution.py:871
  141.6 27.1 %collective-permute-start.15 = (bf16[256,1024]{1,0:T(8,128)(2,1)S(1)}, bf16[256,1024]{1,0:T(8,128)(2,1)S(1)}, u32[]{:S(2)}, u32[]{:S(2)}) collective-permute-start(bf16[256,1024]{1,0:T(8,128)(2,1)S(1)} %multiply_convert_fusion.3.rows), channel_id=1, source_target_pairs={{0,3},{1,2},{2,1},{3,0},{4,7},{5,6},{6,5},{7,4},{8,11},{9,10},{10,... | collective-permute-start | bytes 1572872 | tf_op jit(solution)/shard_map/ppermute | solution.py:622
  200.9 334.4 %reduce-scatter.4.cloned.1.call-start = ((), (), s32[]{:S(2)}) async-start(), calls=%async_computation.7 | async-start | bytes 3604480 | tf_op jit(solution)/shard_map/reduce_scatter | solution.py:719
  200.9 49.7 %collective-permute-start.21 = (bf16[1024,1152]{1,0:T(8,128)(2,1)}, bf16[1024,1152]{1,0:T(8,128)(2,1)}, u32[]{:S(2)}, u32[]{:S(2)}) collective-permute-start(bf16[1024,1152]{1,0:T(8,128)(2,1)} %all-gather.9.cloned.1.call-done.mix_mine), channel_id=1, source_target_pairs={{0,16},{16,0},{1,17},{17,1},{2,18},{18,2},{3,19},{19,3},{4,20},{20... | collective-permute-start | bytes 7077896 | tf_op jit(solution)/shard_map/ppermute | solution.py:617
  233.2 45.6 %collective-permute-start.22 = (bf16[256,1024]{1,0:T(8,128)(2,1)S(1)}, bf16[256,1024]{1,0:T(8,128)(2,1)}, u32[]{:S(2)}, u32[]{:S(2)}) collective-permute-start(bf16[256,1024]{1,0:T(8,128)(2,1)S(1)} %get-tuple-element.193.grad), channel_id=1, source_target_pairs={{0,1},{1,0},{2,3},{3,2},{4,5},{5,4},{6,7},{7,6},{8,9},{9,8},{10,11... | collective-permute-start | bytes 1572872 | tf_op jit(solution)/shard_map/ppermute | solution.py:622
  235.0 43.9 %collective-permute-start.23 = (bf16[256,1024]{1,0:T(8,128)(2,1)S(1)}, bf16[256,1024]{1,0:T(8,128)(2,1)}, u32[]{:S(2)}, u32[]{:S(2)}) collective-permute-start(bf16[256,1024]{1,0:T(8,128)(2,1)S(1)} %get-tuple-element.193.grad), channel_id=1, source_target_pairs={{0,2},{1,3},{2,0},{3,1},{4,6},{5,7},{6,4},{7,5},{8,10},{9,11},{10,... | collective-permute-start | bytes 1572872 | tf_op jit(solution)/shard_map/ppermute | solution.py:622
  235.5 43.3 %collective-permute-start.24 = (bf16[256,1024]{1,0:T(8,128)(2,1)S(1)}, bf16[256,1024]{1,0:T(8,128)(2,1)}, u32[]{:S(2)}, u32[]{:S(2)}) collective-permute-start(bf16[256,1024]{1,0:T(8,128)(2,1)S(1)} %get-tuple-element.193.grad), channel_id=1, source_target_pairs={{0,3},{1,2},{2,1},{3,0},{4,7},{5,6},{6,5},{7,4},{8,11},{9,10},{10,... | collective-permute-start | bytes 1572872 | tf_op jit(solution)/shard_map/ppermute | solution.py:622
  248.5 67.3 %collective-permute-start.31 = (bf16[1024,1152]{1,0:T(8,128)(2,1)}, bf16[1024,1152]{1,0:T(8,128)(2,1)}, u32[]{:S(2)}, u32[]{:S(2)}) collective-permute-start(bf16[1024,1152]{1,0:T(8,128)(2,1)} %all-gather.11.cloned.1.call-done.mine), channel_id=1, source_target_pairs={{0,16},{16,0},{1,17},{17,1},{2,18},{18,2},{3,19},{19,3},{4,20},{20... | collective-permute-start | bytes 7077896 | tf_op jit(solution)/shard_map/ppermute | solution.py:617
  281.9 25.3 %collective-permute-start.26 = (bf16[256,1024]{1,0:T(8,128)(2,1)S(1)}, bf16[256,1024]{1,0:T(8,128)(2,1)S(1)}, u32[]{:S(2)}, u32[]{:S(2)}) collective-permute-start(bf16[256,1024]{1,0:T(8,128)(2,1)S(1)} %get-tuple-element.351), channel_id=1, source_target_pairs={{0,2},{1,3},{2,0},{3,1},{4,6},{5,7},{6,4},{7,5},{8,10},{9,11},{10,... | collective-permute-start | bytes 1572872 | tf_op jit(solution)/shard_map/ppermute | solution.py:622
  311.1 27.7 %collective-permute-start.30 = (bf16[256,1024]{1,0:T(8,128)(2,1)S(1)}, bf16[256,1024]{1,0:T(8,128)(2,1)S(1)}, u32[]{:S(2)}, u32[]{:S(2)}) collective-permute-start(bf16[256,1024]{1,0:T(8,128)(2,1)S(1)} %multiply_convert_fusion.2.rows), channel_id=1, source_target_pairs={{0,3},{1,2},{2,1},{3,0},{4,7},{5,6},{6,5},{7,4},{8,11},{9,10},{10,... | collective-permute-start | bytes 1572872 | tf_op jit(solution)/shard_map/ppermute | solution.py:622
  365.5 33.0 %collective-permute-start.32 = (bf16[1024,1152]{0,1:T(8,128)(2,1)S(1)}, bf16[1024,1152]{0,1:T(8,128)(2,1)S(1)}, u32[]{:S(2)}, u32[]{:S(2)}) collective-permute-start(bf16[1024,1152]{0,1:T(8,128)(2,1)S(1)} %pad_maximum_fusion.2), channel_id=1, source_target_pairs={{0,16},{16,0},{1,17},{17,1},{2,18},{18,2},{3,19},{19,3},{4,20},{20... | collective-permute-start | bytes 7077896 | tf_op jit(solution)/shard_map/ppermute | solution.py:617
  401.3 173.7 %reduce-scatter.6.cloned.1.call-start = ((), (), s32[]{:S(2)}) async-start(), calls=%async_computation.8 | async-start | bytes 1966080 | tf_op jit(solution)/shard_map/reduce_scatter | solution.py:719
  401.4 38.5 %collective-permute-start.40 = (bf16[256,1024]{1,0:T(8,128)(2,1)}, bf16[256,1024]{1,0:T(8,128)(2,1)S(1)}, u32[]{:S(2)}, u32[]{:S(2)}) collective-permute-start(bf16[256,1024]{1,0:T(8,128)(2,1)} %get-tuple-element.243), channel_id=1, source_target_pairs={{0,1},{1,0},{2,3},{3,2},{4,5},{5,4},{6,7},{7,6},{8,9},{9,8},{10,11... | collective-permute-start | bytes 1572872 | tf_op jit(solution)/shard_map/ppermute | solution.py:622
  402.8 37.1 %collective-permute-start.41 = (bf16[256,1024]{1,0:T(8,128)(2,1)}, bf16[256,1024]{1,0:T(8,128)(2,1)S(1)}, u32[]{:S(2)}, u32[]{:S(2)}) collective-permute-start(bf16[256,1024]{1,0:T(8,128)(2,1)} %get-tuple-element.244), channel_id=1, source_target_pairs={{0,2},{1,3},{2,0},{3,1},{4,6},{5,7},{6,4},{7,5},{8,10},{9,11},{10,... | collective-permute-start | bytes 1572872 | tf_op jit(solution)/shard_map/ppermute | solution.py:622
  403.5 36.5 %collective-permute-start.42 = (bf16[256,1024]{1,0:T(8,128)(2,1)}, bf16[256,1024]{1,0:T(8,128)(2,1)S(1)}, u32[]{:S(2)}, u32[]{:S(2)}) collective-permute-start(bf16[256,1024]{1,0:T(8,128)(2,1)} %get-tuple-element.245), channel_id=1, source_target_pairs={{0,3},{1,2},{2,1},{3,0},{4,7},{5,6},{6,5},{7,4},{8,11},{9,10},{10,... | collective-permute-start | bytes 1572872 | tf_op jit(solution)/shard_map/ppermute | solution.py:622
  471.6 25.6 %collective-permute-start.50 = (bf16[256,1024]{1,0:T(8,128)(2,1)S(1)}, bf16[256,1024]{1,0:T(8,128)(2,1)S(1)}, u32[]{:S(2)}, u32[]{:S(2)}) collective-permute-start(bf16[256,1024]{1,0:T(8,128)(2,1)S(1)} %get-tuple-element.331.grad), channel_id=1, source_target_pairs={{0,3},{1,2},{2,1},{3,0},{4,7},{5,6},{6,5},{7,4},{8,11},{9,10},{10,... | collective-permute-start | bytes 1572872 | tf_op jit(solution)/shard_map/ppermute | solution.py:622
  475.0 34.7 %collective-permute-start.57 = (bf16[1024,768]{1,0:T(8,128)(2,1)S(1)}, bf16[1024,768]{1,0:T(8,128)(2,1)S(1)}, u32[]{:S(2)}, u32[]{:S(2)}) collective-permute-start(bf16[1024,768]{1,0:T(8,128)(2,1)S(1)} %convolution_convert_fusion.1), channel_id=1, source_target_pairs={{0,16},{16,0},{1,17},{17,1},{2,18},{18,2},{3,19},{19,3},{4,20},{20... | collective-permute-start | bytes 4718600 | tf_op jit(solution)/shard_map/ppermute | solution.py:617
  506.2 64.2 %collective-permute-start.52 = (bf16[1024,1152]{0,1:T(8,128)(2,1)}, bf16[1024,1152]{0,1:T(8,128)(2,1)}, u32[]{:S(2)}, u32[]{:S(2)}) collective-permute-start(bf16[1024,1152]{0,1:T(8,128)(2,1)} %pad_maximum_fusion.3), channel_id=1, source_target_pairs={{0,16},{16,0},{1,17},{17,1},{2,18},{18,2},{3,19},{19,3},{4,20},{20... | collective-permute-start | bytes 7077896 | tf_op jit(solution)/shard_map/ppermute | solution.py:617
  507.6 25.6 %collective-permute-start.49 = (bf16[256,1024]{1,0:T(8,128)(2,1)}, bf16[256,1024]{1,0:T(8,128)(2,1)}, u32[]{:S(2)}, u32[]{:S(2)}) collective-permute-start(bf16[256,1024]{1,0:T(8,128)(2,1)} %get-tuple-element.256), channel_id=1, source_target_pairs={{0,2},{1,3},{2,0},{3,1},{4,6},{5,7},{6,4},{7,5},{8,10},{9,11},{10,... | collective-permute-start | bytes 1572872 | tf_op jit(solution)/shard_map/ppermute | solution.py:622
  535.3 94.8 %reduce-scatter.8.cloned.1.call-start = ((), (), s32[]{:S(2)}) async-start(), calls=%async_computation.9 | async-start | bytes 3604480 | tf_op jit(solution)/shard_map/reduce_scatter | solution.py:719
  649.3 44.4 %collective-permute-start.72 = (bf16[256,1408]{0,1:T(8,128)(2,1)}, bf16[256,1408]{0,1:T(8,128)(2,1)}, u32[]{:S(2)}, u32[]{:S(2)}) collective-permute-start(bf16[256,1408]{0,1:T(8,128)(2,1)} %broadcast_select_fusion), channel_id=1, source_target_pairs={{0,16},{16,0},{1,17},{17,1},{2,18},{18,2},{3,19},{19,3},{4,20},{20... | collective-permute-start | bytes 2162696 | tf_op jit(solution)/shard_map/ppermute | solution.py:617
  655.2 28.7 %collective-permute-start.67 = (bf16[256,768]{1,0:T(8,128)(2,1)}, bf16[256,768]{1,0:T(8,128)(2,1)}, u32[]{:S(2)}, u32[]{:S(2)}) collective-permute-start(bf16[256,768]{1,0:T(8,128)(2,1)} %get-tuple-element.359), channel_id=1, source_target_pairs={{0,4},{4,8},{8,12},{12,0},{1,5},{5,9},{9,13},{13,1},{2,6},{6,10},{... | collective-permute-start | bytes 1179656 | tf_op jit(solution)/shard_map/ppermute | solution.py:733
  657.2 32.4 %collective-permute-start.68 = (bf16[256,768]{1,0:T(8,128)(2,1)}, bf16[256,768]{1,0:T(8,128)(2,1)}, u32[]{:S(2)}, u32[]{:S(2)}) collective-permute-start(bf16[256,768]{1,0:T(8,128)(2,1)} %get-tuple-element.361), channel_id=1, source_target_pairs={{0,8},{4,12},{8,0},{12,4},{1,9},{5,13},{9,1},{13,5},{2,10},{6,14},... | collective-permute-start | bytes 1179656 | tf_op jit(solution)/shard_map/ppermute | solution.py:733
  660.0 32.0 %collective-permute-start.69 = (bf16[256,768]{1,0:T(8,128)(2,1)}, bf16[256,768]{1,0:T(8,128)(2,1)}, u32[]{:S(2)}, u32[]{:S(2)}) collective-permute-start(bf16[256,768]{1,0:T(8,128)(2,1)} %get-tuple-element.360), channel_id=1, source_target_pairs={{0,12},{4,0},{8,4},{12,8},{1,13},{5,1},{9,5},{13,9},{2,14},{6,2},{... | collective-permute-start | bytes 1179656 | tf_op jit(solution)/shard_map/ppermute | solution.py:733
  668.8 29.6 %collective-permute-start.64 = (bf16[256,1024]{1,0:T(8,128)(2,1)}, bf16[256,1024]{1,0:T(8,128)(2,1)S(1)}, u32[]{:S(2)}, u32[]{:S(2)}) collective-permute-start(bf16[256,1024]{1,0:T(8,128)(2,1)} %get-tuple-element.343), channel_id=1, source_target_pairs={{0,1},{1,0},{2,3},{3,2},{4,5},{5,4},{6,7},{7,6},{8,9},{9,8},{10,11... | collective-permute-start | bytes 1572872 | tf_op jit(solution)/shard_map/ppermute | solution.py:622
  (174 other events, 1805.1 us)
Sparse Core Ops, SparseCore 0:
  14.8 50.0 all-gather.4
  66.5 49.2 all-gather.6
  138.5 49.2 all-gather.8
  201.0 47.4 all-gather.10
  401.5 55.1 reduce-scatter.3
  535.4 33.6 reduce-scatter.5
  575.1 54.9 reduce-scatter.7

commit v4 on v3

--- a/solution.py
+++ b/solution.py
@@ -33,9 +33,11 @@
 
 
 def exact(left, right, dims=((1,), (0,))):
-    return lax.dot_general(
-        left, right, (dims, ((), ())), precision=lax.Precision.HIGHEST, preferred_element_type=F32
-    )
+    high = right.astype(LOW)
+    rest = right - high.astype(F32)
+    middle = rest.astype(LOW)
+    low = rest - middle.astype(F32)
+    return _dot(left, high, dims) + (_dot(left, middle, dims) + _dot(left, low, dims))
 
 
 def mm_split(left, right):
@@ -775,7 +777,10 @@
     branch_all = jnp.concatenate(spread_rows((live * grad_after).astype(LOW)), axis=0)
     out_total = share(tn(branch_all, mixed_a), tn(branch_all, mixed_b))
     early = jnp.concatenate([ffn_total, out_total], axis=1)
-    early, branch_all, waiting = lax.optimization_barrier((early, branch_all, waiting))
+    if final is None:
+        branch_all, waiting = lax.optimization_barrier((branch_all, waiting))
+    else:
+        early, branch_all, waiting = lax.optimization_barrier((early, branch_all, waiting))
     early_owned = scatter(early)
     d_mine, d_other, d_taps, d_gain, d_params, inward, gain_one_grad = mixer_backward(
         meta, params, (mine, other, o_a, o_b, states, inverses), normed_all, branch_all,

time: 727 us -> 720 us (level)
  no operation moved by 1% of the time
where the time goes in v4:
time: 720 us; the launch traced here: 710 us
  waiting for transfers between devices  292 us (41%)
  Pallas kernels  173 us (24%)
  starting transfers between devices  68.3 us (9%)
  other arithmetic  64.3 us (9%)
  local copies, waits for them, and re-layouts  64.1 us (9%)
  matrix products  32.3 us (4%)
  between operations  16.6 us (2%)
    ppermute x48, waiting for transfers between devices, send_by(): lax.ppermute(array, 'tensor', [(i, i ^ offset) for i in range(peers)])  211 us
    pallas_call x2, Pallas kernels, mixer_backward(): pl.pallas_call(mixer_backward_kernel, grid_spec=pltpu.PrefetchScalarGridS...  69.2 us
    ppermute x48, starting transfers between devices, send_by(): lax.ppermute(array, 'tensor', [(i, i ^ offset) for i in range(peers)])  55.1 us
    pallas_call x2, Pallas kernels, mixer_forward(): pl.pallas_call(mixer_forward_kernel, grid_spec=pltpu.PrefetchScalarGridSp...  54.9 us
    all_gather x4, waiting for transfers between devices, gather(): full = lax.all_gather(shard, 'dp', axis=0, tiled=True)  45.4 us
    dot_general x18, matrix products, tn(): lax.dot_general(left, right, (((0,), (0,)), ((), ())), preferred_element_...  32.3 us
    unnamed x276, local copies, waits for them, and re-layouts  26.9 us
    pallas_call x8, Pallas kernels, ffn_backward(): pl.pallas_call(ffn_backward_kernel, out_shape=[jax.ShapeDtypeStruct((coun...  26.6 us
  transfers between devices with their start and end apart: 80, of which 37 were waited for; matrix products, arithmetic and copies ran while one was open for 17% of the time, Pallas kernels for 24%

profile of v4, /device:TPU:8, one launch (start us, length us, event | category | flops | bytes accessed | tf_op | source)
XLA Modules:
  0.0 710.1 jit_solution(14540503306801651543)
XLA Ops:
  30.4 34.5 %all-gather.5.cloned.1.call-done.mix_mine = bf16[1024,1152]{1,0:T(8,128)(2,1)} async-done(((bf16[256,1152]{1,0:T(8,128)(2,1)}), bf16[1024,1152]{1,0:T(8,128)(2,1)}) %all-gather.5.cloned.1.call-update) | async-done | bytes 2359312 | tf_op jit(solution)/shard_map/all_gather | solution.py:876
  78.7 27.2 %mixer_forward.2 = (f32[1024,896]{1,0:T(8,128)}, f32[1024,896]{1,0:T(8,128)}, bf16[1024,256]{1,0:T(8,128)(2,1)}, bf16[1024,256]{1,0:T(8,128)(2,1)}, f32[1024,256...) custom-call(s32[17]{0:T(128)} %pad_add_fusion.meta, ...), custom_call_target="tpu_custom_call" | custom-call | tf_op jit(solution)/shard_map/mixer_forward/pallas_call | solution.py:502
  113.2 11.1 %collective-permute-done.10 = bf16[256,1024]{1,0:T(8,128)(2,1)S(1)} collective-permute-done((bf16[256,1024]{1,0:T(8,128)(2,1)}, bf16[256,1024]{1,0:T(8,128)(2,1)S(1)}, u32[]{:S(2)}, u32[]{:S(2)}) %collective-permute-start.10) | collective-permute-done | bytes 524320 | tf_op jit(solution)/shard_map/ppermute | solution.py:624
  124.3 10.7 %collective-permute-done.8 = bf16[256,1024]{1,0:T(8,128)(2,1)S(1)} collective-permute-done((bf16[256,1024]{1,0:T(8,128)(2,1)}, bf16[256,1024]{1,0:T(8,128)(2,1)S(1)}, u32[]{:S(2)}, u32[]{:S(2)}) %collective-permute-start.8) | collective-permute-done | bytes 524320 | tf_op jit(solution)/shard_map/ppermute | solution.py:624
  157.8 7.1 collective-permute-done.13.rows
  176.5 12.3 %collective-permute-done.17 = bf16[256,1024]{1,0:T(8,128)(2,1)S(1)} collective-permute-done((bf16[256,1024]{1,0:T(8,128)(2,1)S(1)}, bf16[256,1024]{1,0:T(8,128)(2,1)S(1)}, u32[]{:S(2)}, u32[]{:S(2)}) %collective-permute-start.17) | collective-permute-done | bytes 524320 | tf_op jit(solution)/shard_map/ppermute | solution.py:624
  188.8 7.7 %collective-permute-done.16 = bf16[256,1024]{1,0:T(8,128)(2,1)S(1)} collective-permute-done((bf16[256,1024]{1,0:T(8,128)(2,1)S(1)}, bf16[256,1024]{1,0:T(8,128)(2,1)S(1)}, u32[]{:S(2)}, u32[]{:S(2)}) %collective-permute-start.16) | collective-permute-done | bytes 524320 | tf_op jit(solution)/shard_map/ppermute | solution.py:624
  207.9 10.9 %collective-permute-done.18 = bf16[256,1024]{1,0:T(8,128)(2,1)} collective-permute-done((bf16[256,1024]{1,0:T(8,128)(2,1)}, bf16[256,1024]{1,0:T(8,128)(2,1)}, u32[]{:S(2)}, u32[]{:S(2)}) %collective-permute-start.18) | collective-permute-done | bytes 524320 | tf_op jit(solution)/shard_map/ppermute | solution.py:624
  218.8 10.8 %collective-permute-done.20 = bf16[256,1024]{1,0:T(8,128)(2,1)} collective-permute-done((bf16[256,1024]{1,0:T(8,128)(2,1)}, bf16[256,1024]{1,0:T(8,128)(2,1)}, u32[]{:S(2)}, u32[]{:S(2)}) %collective-permute-start.20) | collective-permute-done | bytes 524320 | tf_op jit(solution)/shard_map/ppermute | solution.py:624
  237.1 10.9 %all-gather.11.cloned.1.call-done.mine = bf16[1024,1152]{1,0:T(8,128)(2,1)} async-done(((bf16[256,1152]{1,0:T(8,128)(2,1)}), bf16[1024,1152]{1,0:T(8,128)(2,1)}) %all-gather.11.cloned.1.call-update) | async-done | bytes 2359312 | tf_op jit(solution)/shard_map/all_gather | solution.py:876
  250.1 27.6 %mixer_forward.3 = (f32[1024,896]{1,0:T(8,128)}, f32[1024,896]{1,0:T(8,128)}, bf16[1024,256]{1,0:T(8,128)(2,1)}, bf16[1024,256]{1,0:T(8,128)(2,1)}, f32[1024,256...) custom-call(s32[17]{0:T(128)} %pad_add_fusion.meta, ...), custom_call_target="tpu_custom_call" | custom-call | tf_op jit(solution)/shard_map/mixer_forward/pallas_call | solution.py:502
  282.9 11.2 %collective-permute-done.25 = bf16[256,1024]{1,0:T(8,128)(2,1)S(1)} collective-permute-done((bf16[256,1024]{1,0:T(8,128)(2,1)S(1)}, bf16[256,1024]{1,0:T(8,128)(2,1)S(1)}, u32[]{:S(2)}, u32[]{:S(2)}) %collective-permute-start.25) | collective-permute-done | bytes 524320 | tf_op jit(solution)/shard_map/ppermute | solution.py:624
  294.1 12.0 %collective-permute-done.26 = bf16[256,1024]{1,0:T(8,128)(2,1)S(1)} collective-permute-done((bf16[256,1024]{1,0:T(8,128)(2,1)S(1)}, bf16[256,1024]{1,0:T(8,128)(2,1)S(1)}, u32[]{:S(2)}, u32[]{:S(2)}) %collective-permute-start.26) | collective-permute-done | bytes 524320 | tf_op jit(solution)/shard_map/ppermute | solution.py:624
  318.1 4.8 collective-permute-done.29.rows
  357.9 4.6 collective-permute-done.32
  368.1 11.4 %collective-permute-done.35 = bf16[256,1024]{1,0:T(8,128)(2,1)S(1)} collective-permute-done((bf16[256,1024]{1,0:T(8,128)(2,1)S(1)}, bf16[256,1024]{1,0:T(8,128)(2,1)S(1)}, u32[]{:S(2)}, u32[]{:S(2)}) %collective-permute-start.35) | collective-permute-done | bytes 524320 | tf_op jit(solution)/shard_map/ppermute | solution.py:624
  379.4 7.2 %collective-permute-done.37 = bf16[256,1024]{1,0:T(8,128)(2,1)S(1)} collective-permute-done((bf16[256,1024]{1,0:T(8,128)(2,1)S(1)}, bf16[256,1024]{1,0:T(8,128)(2,1)S(1)}, u32[]{:S(2)}, u32[]{:S(2)}) %collective-permute-start.37) | collective-permute-done | bytes 524320 | tf_op jit(solution)/shard_map/ppermute | solution.py:624
  397.9 34.7 %mixer_backward.2 = (bf16[1024,896]{1,0:T(8,128)(2,1)}, bf16[1024,896]{1,0:T(8,128)(2,1)}, f32[2,4,512]{2,1,0:T(4,128)}, f32[1,256]{1,0:T(1,128)}, f32[2,128]{1,...) custom-call(s32[17]{0:T(128)} %pad_add_fusion.meta, f32[2,2]{1,0:T(2,128)} %pad_maximum_fusion.21.params, ...), custom_call_target="tpu_custom_call" | custom-call | tf_op jit(solution)/shard_map/mixer_backward/pallas_call | solution.py:564
  438.1 11.3 %collective-permute-done.41 = bf16[256,1024]{1,0:T(8,128)(2,1)S(1)} collective-permute-done((bf16[256,1024]{1,0:T(8,128)(2,1)S(1)}, bf16[256,1024]{1,0:T(8,128)(2,1)S(1)}, u32[]{:S(2)}, u32[]{:S(2)}) %collective-permute-start.41) | collective-permute-done | bytes 524320 | tf_op jit(solution)/shard_map/ppermute | solution.py:624
  449.4 10.2 %collective-permute-done.42 = bf16[256,1024]{1,0:T(8,128)(2,1)S(1)} collective-permute-done((bf16[256,1024]{1,0:T(8,128)(2,1)S(1)}, bf16[256,1024]{1,0:T(8,128)(2,1)S(1)}, u32[]{:S(2)}, u32[]{:S(2)}) %collective-permute-start.42) | collective-permute-done | bytes 524320 | tf_op jit(solution)/shard_map/ppermute | solution.py:624
  469.3 7.2 %collective-permute-done.44.grad = bf16[256,1024]{1,0:T(8,128)(2,1)S(1)} collective-permute-done((bf16[256,1024]{1,0:T(8,128)(2,1)S(1)}, bf16[256,1024]{1,0:T(8,128)(2,1)S(1)}, u32[]{:S(2)}, u32[]{:S(2)}) %collective-permute-start.44) | collective-permute-done | bytes 524320 | tf_op jit(solution)/shard_map/ppermute | solution.py:624
  480.1 6.3 collective-permute-done.46.grad
  505.7 8.4 %collective-permute-done.45 = bf16[256,1024]{1,0:T(8,128)(2,1)S(1)} collective-permute-done((bf16[256,1024]{1,0:T(8,128)(2,1)}, bf16[256,1024]{1,0:T(8,128)(2,1)S(1)}, u32[]{:S(2)}, u32[]{:S(2)}) %collective-permute-start.45) | collective-permute-done | bytes 524320 | tf_op jit(solution)/shard_map/ppermute | solution.py:624
  514.1 11.1 %collective-permute-done.47 = bf16[256,1024]{1,0:T(8,128)(2,1)} collective-permute-done((bf16[256,1024]{1,0:T(8,128)(2,1)}, bf16[256,1024]{1,0:T(8,128)(2,1)}, u32[]{:S(2)}, u32[]{:S(2)}) %collective-permute-start.47) | collective-permute-done | bytes 524320 | tf_op jit(solution)/shard_map/ppermute | solution.py:624
  534.1 11.4 %collective-permute-done.51 = bf16[256,1024]{1,0:T(8,128)(2,1)S(1)} collective-permute-done((bf16[256,1024]{1,0:T(8,128)(2,1)S(1)}, bf16[256,1024]{1,0:T(8,128)(2,1)S(1)}, u32[]{:S(2)}, u32[]{:S(2)}) %collective-permute-start.51) | collective-permute-done | bytes 524320 | tf_op jit(solution)/shard_map/ppermute | solution.py:624
  545.5 10.9 %collective-permute-done.52 = bf16[256,1024]{1,0:T(8,128)(2,1)S(1)} collective-permute-done((bf16[256,1024]{1,0:T(8,128)(2,1)S(1)}, bf16[256,1024]{1,0:T(8,128)(2,1)S(1)}, u32[]{:S(2)}, u32[]{:S(2)}) %collective-permute-start.52) | collective-permute-done | bytes 524320 | tf_op jit(solution)/shard_map/ppermute | solution.py:624
  569.7 34.5 %mixer_backward.3 = (bf16[1024,896]{1,0:T(8,128)(2,1)}, bf16[1024,896]{1,0:T(8,128)(2,1)}, f32[2,4,512]{2,1,0:T(4,128)}, f32[1,256]{1,0:T(1,128)}, f32[2,128]{1,...) custom-call(s32[17]{0:T(128)} %pad_add_fusion.meta, f32[2,2]{1,0:T(2,128)} %pad_maximum_fusion.23.params, ...), custom_call_target="tpu_custom_call" | custom-call | tf_op jit(solution)/shard_map/mixer_backward/pallas_call | solution.py:564
  604.3 4.4 convolution_convert_fusion
  616.8 4.5 add_convert_fusion
  664.6 12.3 %collective-permute-done.67 = bf16[256,768]{1,0:T(8,128)(2,1)} collective-permute-done((bf16[256,768]{1,0:T(8,128)(2,1)}, bf16[256,768]{1,0:T(8,128)(2,1)}, u32[]{:S(2)}, u32[]{:S(2)}) %collective-permute-start.67) | collective-permute-done | bytes 393248 | tf_op jit(solution)/shard_map/ppermute | solution.py:735
  677.4 5.2 collective-permute-done.68
  691.5 6.0 collective-permute-done.65
  (618 shorter events, 293.2 us)
Async XLA Ops:
  7.2 57.7 %all-gather.5.cloned.1.call-start = ((), (), s32[]{:S(2)}) async-start(), calls=%async_computation.3 | async-start | bytes 2949120 | tf_op jit(solution)/shard_map/all_gather | solution.py:876
  14.6 123.1 %all-gather.7.cloned.1.call-start = ((), (), s32[]{:S(2)}) async-start(), calls=%async_computation.4 | async-start | bytes 2949120 | tf_op jit(solution)/shard_map/all_gather | solution.py:876
  15.1 49.9 %collective-permute-start = (f32[1,16656]{1,0:T(1,128)S(1)}, f32[1,16656]{1,0:T(1,128)}, u32[]{:S(2)}, u32[]{:S(2)}) collective-permute-start(f32[1,16656]{1,0:T(1,128)S(1)} %broadcast_in_dim.60), channel_id=1, source_target_pairs={{0,16},{16,0},{1,17},{17,1},{2,18},{18,2},{3,19},{19,3},{4,20},{20... | collective-permute-start | bytes 199880 | tf_op jit(solution)/shard_map/ppermute | solution.py:619
  25.7 48.4 %collective-permute-start.2 = (bf16[256,1024]{1,0:T(8,128)(2,1)}, bf16[256,1024]{1,0:T(8,128)(2,1)}, u32[]{:S(2)}, u32[]{:S(2)}) collective-permute-start(bf16[256,1024]{1,0:T(8,128)(2,1)} %fusion.46), channel_id=1, source_target_pairs={{0,1},{1,0},{2,3},{3,2},{4,5},{5,4},{6,7},{7,6},{8,9},{9,8},{10,11... | collective-permute-start | bytes 1572872 | tf_op jit(solution)/shard_map/ppermute | solution.py:624
  27.2 46.9 %collective-permute-start.3 = (bf16[256,1024]{1,0:T(8,128)(2,1)}, bf16[256,1024]{1,0:T(8,128)(2,1)}, u32[]{:S(2)}, u32[]{:S(2)}) collective-permute-start(bf16[256,1024]{1,0:T(8,128)(2,1)} %fusion.46), channel_id=1, source_target_pairs={{0,2},{1,3},{2,0},{3,1},{4,6},{5,7},{6,4},{7,5},{8,10},{9,11},{10,... | collective-permute-start | bytes 1572872 | tf_op jit(solution)/shard_map/ppermute | solution.py:624
  28.7 45.4 %collective-permute-start.4 = (bf16[256,1024]{1,0:T(8,128)(2,1)}, bf16[256,1024]{1,0:T(8,128)(2,1)}, u32[]{:S(2)}, u32[]{:S(2)}) collective-permute-start(bf16[256,1024]{1,0:T(8,128)(2,1)} %fusion.46), channel_id=1, source_target_pairs={{0,3},{1,2},{2,1},{3,0},{4,7},{5,6},{6,5},{7,4},{8,11},{9,10},{10,... | collective-permute-start | bytes 1572872 | tf_op jit(solution)/shard_map/ppermute | solution.py:624
  64.9 135.4 %all-gather.9.cloned.1.call-start = ((), (), s32[]{:S(2)}) async-start(), calls=%async_computation.5 | async-start | bytes 2949120 | tf_op jit(solution)/shard_map/all_gather | solution.py:876
  137.8 110.2 %all-gather.11.cloned.1.call-start = ((), (), s32[]{:S(2)}) async-start(), calls=%async_computation.6 | async-start | bytes 2949120 | tf_op jit(solution)/shard_map/all_gather | solution.py:876
  141.1 27.1 %collective-permute-start.15 = (bf16[256,1024]{1,0:T(8,128)(2,1)S(1)}, bf16[256,1024]{1,0:T(8,128)(2,1)S(1)}, u32[]{:S(2)}, u32[]{:S(2)}) collective-permute-start(bf16[256,1024]{1,0:T(8,128)(2,1)S(1)} %multiply_convert_fusion.3.rows), channel_id=1, source_target_pairs={{0,3},{1,2},{2,1},{3,0},{4,7},{5,6},{6,5},{7,4},{8,11},{9,10},{10,... | collective-permute-start | bytes 1572872 | tf_op jit(solution)/shard_map/ppermute | solution.py:624
  200.4 326.9 %reduce-scatter.4.cloned.1.call-start = ((), (), s32[]{:S(2)}) async-start(), calls=%async_computation.7 | async-start | bytes 3604480 | tf_op jit(solution)/shard_map/reduce_scatter | solution.py:721
  200.4 49.7 %collective-permute-start.21 = (bf16[1024,1152]{1,0:T(8,128)(2,1)}, bf16[1024,1152]{1,0:T(8,128)(2,1)}, u32[]{:S(2)}, u32[]{:S(2)}) collective-permute-start(bf16[1024,1152]{1,0:T(8,128)(2,1)} %all-gather.9.cloned.1.call-done.mix_mine), channel_id=1, source_target_pairs={{0,16},{16,0},{1,17},{17,1},{2,18},{18,2},{3,19},{19,3},{4,20},{20... | collective-permute-start | bytes 7077896 | tf_op jit(solution)/shard_map/ppermute | solution.py:619
  232.7 45.1 %collective-permute-start.22 = (bf16[256,1024]{1,0:T(8,128)(2,1)S(1)}, bf16[256,1024]{1,0:T(8,128)(2,1)}, u32[]{:S(2)}, u32[]{:S(2)}) collective-permute-start(bf16[256,1024]{1,0:T(8,128)(2,1)S(1)} %get-tuple-element.192.grad), channel_id=1, source_target_pairs={{0,1},{1,0},{2,3},{3,2},{4,5},{5,4},{6,7},{7,6},{8,9},{9,8},{10,11... | collective-permute-start | bytes 1572872 | tf_op jit(solution)/shard_map/ppermute | solution.py:624
  234.4 43.4 %collective-permute-start.23 = (bf16[256,1024]{1,0:T(8,128)(2,1)S(1)}, bf16[256,1024]{1,0:T(8,128)(2,1)}, u32[]{:S(2)}, u32[]{:S(2)}) collective-permute-start(bf16[256,1024]{1,0:T(8,128)(2,1)S(1)} %get-tuple-element.192.grad), channel_id=1, source_target_pairs={{0,2},{1,3},{2,0},{3,1},{4,6},{5,7},{6,4},{7,5},{8,10},{9,11},{10,... | collective-permute-start | bytes 1572872 | tf_op jit(solution)/shard_map/ppermute | solution.py:624
  235.0 42.8 %collective-permute-start.24 = (bf16[256,1024]{1,0:T(8,128)(2,1)S(1)}, bf16[256,1024]{1,0:T(8,128)(2,1)}, u32[]{:S(2)}, u32[]{:S(2)}) collective-permute-start(bf16[256,1024]{1,0:T(8,128)(2,1)S(1)} %get-tuple-element.192.grad), channel_id=1, source_target_pairs={{0,3},{1,2},{2,1},{3,0},{4,7},{5,6},{6,5},{7,4},{8,11},{9,10},{10,... | collective-permute-start | bytes 1572872 | tf_op jit(solution)/shard_map/ppermute | solution.py:624
  248.0 66.7 %collective-permute-start.28 = (bf16[1024,1152]{1,0:T(8,128)(2,1)}, bf16[1024,1152]{1,0:T(8,128)(2,1)}, u32[]{:S(2)}, u32[]{:S(2)}) collective-permute-start(bf16[1024,1152]{1,0:T(8,128)(2,1)} %all-gather.11.cloned.1.call-done.mine), channel_id=1, source_target_pairs={{0,16},{16,0},{1,17},{17,1},{2,18},{18,2},{3,19},{19,3},{4,20},{20... | collective-permute-start | bytes 7077896 | tf_op jit(solution)/shard_map/ppermute | solution.py:619
  310.0 31.0 %collective-permute-start.33 = (bf16[256,1024]{1,0:T(8,128)(2,1)S(1)}, bf16[256,1024]{1,0:T(8,128)(2,1)S(1)}, u32[]{:S(2)}, u32[]{:S(2)}) collective-permute-start(bf16[256,1024]{1,0:T(8,128)(2,1)S(1)} %multiply_convert_fusion.2.rows), channel_id=1, source_target_pairs={{0,3},{1,2},{2,1},{3,0},{4,7},{5,6},{6,5},{7,4},{8,11},{9,10},{10,... | collective-permute-start | bytes 1572872 | tf_op jit(solution)/shard_map/ppermute | solution.py:624
  330.8 27.0 %collective-permute-start.30 = (bf16[256,1024]{1,0:T(8,128)(2,1)S(1)}, bf16[256,1024]{1,0:T(8,128)(2,1)S(1)}, u32[]{:S(2)}, u32[]{:S(2)}) collective-permute-start(bf16[256,1024]{1,0:T(8,128)(2,1)S(1)} %get-tuple-element.202), channel_id=1, source_target_pairs={{0,1},{1,0},{2,3},{3,2},{4,5},{5,4},{6,7},{7,6},{8,9},{9,8},{10,11... | collective-permute-start | bytes 1572872 | tf_op jit(solution)/shard_map/ppermute | solution.py:624
  357.8 33.7 %collective-permute-start.55 = (bf16[1024,1152]{0,1:T(8,128)(2,1)S(1)}, bf16[1024,1152]{0,1:T(8,128)(2,1)S(1)}, u32[]{:S(2)}, u32[]{:S(2)}) collective-permute-start(bf16[1024,1152]{0,1:T(8,128)(2,1)S(1)} %pad_maximum_fusion.3), channel_id=1, source_target_pairs={{0,16},{16,0},{1,17},{17,1},{2,18},{18,2},{3,19},{19,3},{4,20},{20... | collective-permute-start | bytes 7077896 | tf_op jit(solution)/shard_map/ppermute | solution.py:619
  394.3 173.4 %reduce-scatter.6.cloned.1.call-start = ((), (), s32[]{:S(2)}) async-start(), calls=%async_computation.8 | async-start | bytes 1966080 | tf_op jit(solution)/shard_map/reduce_scatter | solution.py:721
  394.3 38.3 %collective-permute-start.38 = (bf16[256,1024]{1,0:T(8,128)(2,1)}, bf16[256,1024]{1,0:T(8,128)(2,1)S(1)}, u32[]{:S(2)}, u32[]{:S(2)}) collective-permute-start(bf16[256,1024]{1,0:T(8,128)(2,1)} %get-tuple-element.224), channel_id=1, source_target_pairs={{0,1},{1,0},{2,3},{3,2},{4,5},{5,4},{6,7},{7,6},{8,9},{9,8},{10,11... | collective-permute-start | bytes 1572872 | tf_op jit(solution)/shard_map/ppermute | solution.py:624
  395.1 37.6 %collective-permute-start.39 = (bf16[256,1024]{1,0:T(8,128)(2,1)}, bf16[256,1024]{1,0:T(8,128)(2,1)S(1)}, u32[]{:S(2)}, u32[]{:S(2)}) collective-permute-start(bf16[256,1024]{1,0:T(8,128)(2,1)} %get-tuple-element.225), channel_id=1, source_target_pairs={{0,2},{1,3},{2,0},{3,1},{4,6},{5,7},{6,4},{7,5},{8,10},{9,11},{10,... | collective-permute-start | bytes 1572872 | tf_op jit(solution)/shard_map/ppermute | solution.py:624
  396.7 36.0 %collective-permute-start.40 = (bf16[256,1024]{1,0:T(8,128)(2,1)}, bf16[256,1024]{1,0:T(8,128)(2,1)S(1)}, u32[]{:S(2)}, u32[]{:S(2)}) collective-permute-start(bf16[256,1024]{1,0:T(8,128)(2,1)} %get-tuple-element.226), channel_id=1, source_target_pairs={{0,3},{1,2},{2,1},{3,0},{4,7},{5,6},{6,5},{7,4},{8,11},{9,10},{10,... | collective-permute-start | bytes 1572872 | tf_op jit(solution)/shard_map/ppermute | solution.py:624
  463.6 26.6 %collective-permute-start.48 = (bf16[256,1024]{1,0:T(8,128)(2,1)S(1)}, bf16[256,1024]{1,0:T(8,128)(2,1)S(1)}, u32[]{:S(2)}, u32[]{:S(2)}) collective-permute-start(bf16[256,1024]{1,0:T(8,128)(2,1)S(1)} %get-tuple-element.329.grad), channel_id=1, source_target_pairs={{0,3},{1,2},{2,1},{3,0},{4,7},{5,6},{6,5},{7,4},{8,11},{9,10},{10,... | collective-permute-start | bytes 1572872 | tf_op jit(solution)/shard_map/ppermute | solution.py:624
  467.0 35.7 %collective-permute-start.57 = (bf16[1024,768]{1,0:T(8,128)(2,1)S(1)}, bf16[1024,768]{1,0:T(8,128)(2,1)S(1)}, u32[]{:S(2)}, u32[]{:S(2)}) collective-permute-start(bf16[1024,768]{1,0:T(8,128)(2,1)S(1)} %convolution_convert_fusion.1), channel_id=1, source_target_pairs={{0,16},{16,0},{1,17},{17,1},{2,18},{18,2},{3,19},{19,3},{4,20},{20... | collective-permute-start | bytes 4718600 | tf_op jit(solution)/shard_map/ppermute | solution.py:619
  499.1 64.0 %collective-permute-start.50 = (bf16[1024,1152]{0,1:T(8,128)(2,1)}, bf16[1024,1152]{0,1:T(8,128)(2,1)}, u32[]{:S(2)}, u32[]{:S(2)}) collective-permute-start(bf16[1024,1152]{0,1:T(8,128)(2,1)} %pad_maximum_fusion.2), channel_id=1, source_target_pairs={{0,16},{16,0},{1,17},{17,1},{2,18},{18,2},{3,19},{19,3},{4,20},{20... | collective-permute-start | bytes 7077896 | tf_op jit(solution)/shard_map/ppermute | solution.py:619
  499.5 25.6 %collective-permute-start.47 = (bf16[256,1024]{1,0:T(8,128)(2,1)}, bf16[256,1024]{1,0:T(8,128)(2,1)}, u32[]{:S(2)}, u32[]{:S(2)}) collective-permute-start(bf16[256,1024]{1,0:T(8,128)(2,1)} %get-tuple-element.237), channel_id=1, source_target_pairs={{0,2},{1,3},{2,0},{3,1},{4,6},{5,7},{6,4},{7,5},{8,10},{9,11},{10,... | collective-permute-start | bytes 1572872 | tf_op jit(solution)/shard_map/ppermute | solution.py:624
  527.3 95.8 %reduce-scatter.8.cloned.1.call-start = ((), (), s32[]{:S(2)}) async-start(), calls=%async_computation.9 | async-start | bytes 3604480 | tf_op jit(solution)/shard_map/reduce_scatter | solution.py:721
  642.3 44.5 %collective-permute-start.72 = (bf16[256,1408]{0,1:T(8,128)(2,1)}, bf16[256,1408]{0,1:T(8,128)(2,1)}, u32[]{:S(2)}, u32[]{:S(2)}) collective-permute-start(bf16[256,1408]{0,1:T(8,128)(2,1)} %broadcast_select_fusion), channel_id=1, source_target_pairs={{0,16},{16,0},{1,17},{17,1},{2,18},{18,2},{3,19},{19,3},{4,20},{20... | collective-permute-start | bytes 2162696 | tf_op jit(solution)/shard_map/ppermute | solution.py:619
  648.2 28.7 %collective-permute-start.67 = (bf16[256,768]{1,0:T(8,128)(2,1)}, bf16[256,768]{1,0:T(8,128)(2,1)}, u32[]{:S(2)}, u32[]{:S(2)}) collective-permute-start(bf16[256,768]{1,0:T(8,128)(2,1)} %get-tuple-element.357), channel_id=1, source_target_pairs={{0,4},{4,8},{8,12},{12,0},{1,5},{5,9},{9,13},{13,1},{2,6},{6,10},{... | collective-permute-start | bytes 1179656 | tf_op jit(solution)/shard_map/ppermute | solution.py:735
  650.2 32.4 %collective-permute-start.68 = (bf16[256,768]{1,0:T(8,128)(2,1)}, bf16[256,768]{1,0:T(8,128)(2,1)}, u32[]{:S(2)}, u32[]{:S(2)}) collective-permute-start(bf16[256,768]{1,0:T(8,128)(2,1)} %get-tuple-element.359), channel_id=1, source_target_pairs={{0,8},{4,12},{8,0},{12,4},{1,9},{5,13},{9,1},{13,5},{2,10},{6,14},... | collective-permute-start | bytes 1179656 | tf_op jit(solution)/shard_map/ppermute | solution.py:735
  653.0 32.0 %collective-permute-start.69 = (bf16[256,768]{1,0:T(8,128)(2,1)}, bf16[256,768]{1,0:T(8,128)(2,1)}, u32[]{:S(2)}, u32[]{:S(2)}) collective-permute-start(bf16[256,768]{1,0:T(8,128)(2,1)} %get-tuple-element.358), channel_id=1, source_target_pairs={{0,12},{4,0},{8,4},{12,8},{1,13},{5,1},{9,5},{13,9},{2,14},{6,2},{... | collective-permute-start | bytes 1179656 | tf_op jit(solution)/shard_map/ppermute | solution.py:735
  661.8 29.7 %collective-permute-start.64 = (bf16[256,1024]{1,0:T(8,128)(2,1)}, bf16[256,1024]{1,0:T(8,128)(2,1)S(1)}, u32[]{:S(2)}, u32[]{:S(2)}) collective-permute-start(bf16[256,1024]{1,0:T(8,128)(2,1)} %get-tuple-element.341), channel_id=1, source_target_pairs={{0,1},{1,0},{2,3},{3,2},{4,5},{5,4},{6,7},{7,6},{8,9},{9,8},{10,11... | collective-permute-start | bytes 1572872 | tf_op jit(solution)/shard_map/ppermute | solution.py:624
  (174 other events, 1798.1 us)
Sparse Core Ops, SparseCore 0:
  14.8 50.0 all-gather.4
  66.5 49.2 all-gather.6
  137.9 49.2 all-gather.8
  200.5 47.4 all-gather.10
  394.4 55.4 reduce-scatter.3
  527.4 33.8 reduce-scatter.5
  567.9 55.1 reduce-scatter.7
